TPU v7x, 512 devices: a whole 4x4x16 slice. The times are simulated.
512 devices in a mesh: section: 16 (over z), seq: 32 (over x, y, core).
Axes of the slice: x: 4, y: 4, z: 16, core: 2. Of those that a mesh axis runs over, the one named last changes fastest.
Arguments:
- section_input: bfloat16 [16, 4096, 4096], P('section', 'seq'), may hold values from -30 to 30
- cotangent: bfloat16 [16, 4096, 4096], P('section', 'seq'), may hold values from -6 to 6
- norm_gain: float32 [16, 4096], P('section'), may hold values from 0.1 to 1.9
- short_filter: float32 [16, 3, 3, 4096], P('section'), may hold values from -3.5 to 3.5
- decay_rate: float32 [16, 16, 4096], P('section'), may hold values from 4.8828124e-06 to 0.06
- residue: float32 [16, 16, 4096], P('section'), may hold values from -1.5 to 1.5
- skip_gain: float32 [16, 4096], P('section'), may hold values from 0.5 to 1.5
Outputs:
- passed_on: bfloat16 [16, 4096, 4096], P('section', 'seq')
- passed_back: bfloat16 [16, 4096, 4096], P('section', 'seq')
All inputs are finite; a program needn't handle non-finite values.
Results may differ from a plain program's by a relative error of at most 0.005.
Values may be sent and summed in bfloat16 or wider, within the bound.
No kernel may reach another device: no remote copies, remote signals or barrier semaphores. Data moves between devices by JAX's collectives and lax.ppermute only.
A program may use at most 192 MiB of HBM per device.

v0:
```python
import jax
import jax.numpy as jnp
from jax import lax
from jax.sharding import PartitionSpec as P


def shifted(block, axis, distance):
    devices = range(lax.axis_size(axis))
    route = [(i - distance, i) for i in devices if i - distance in devices]
    return lax.ppermute(block, axis, route)


def chain(earlier, later):
    return (earlier[0] * later[1] + later[0], earlier[1] * later[1])


def block_sums(signal, grad_sig, rates, block):
    length, width = signal.shape
    count = length // block
    place = jnp.arange(block).astype(jnp.float32)[:, None, None]
    tail = jnp.exp(-rates[None] * (block - 1 - place))
    head = jnp.exp(-rates[None] * place)
    ends_ahead = jnp.einsum(
        "src,bsc->brc", tail, signal.reshape(count, block, width), precision=lax.Precision.HIGH
    )
    ends_back = jnp.einsum(
        "trc,btc->brc", head, grad_sig.reshape(count, block, width), precision=lax.Precision.HIGH
    )
    factor = jnp.broadcast_to(jnp.exp(-rates * block)[None], ends_ahead.shape)
    incl_ahead = lax.associative_scan(chain, (ends_ahead, factor))[0]
    incl_back = lax.associative_scan(chain, (ends_back, factor), reverse=True)[0]
    return (incl_ahead, incl_back)


def local_toeplitz(stacked, rates, coefs, block):
    place = jnp.arange(block).astype(jnp.float32)
    offsets = jnp.arange(block)
    lag_table = jnp.maximum(offsets[:, None] - offsets[None, :], 0)
    lower = (offsets[:, None] >= offsets[None, :]).astype(jnp.float32)[:, :, None]
    filter_head = jnp.sum(coefs[None] * jnp.exp(-rates[None] * place[:, None, None]), axis=1)
    table = jnp.take(filter_head, lag_table, axis=0) * lower
    return jnp.einsum("tsc,bsc->btc", table, stacked, precision=lax.Precision.HIGH)


def apply_filter(
    signal, grad_sig, rates, coefs, block, incl_ahead, incl_back, enter_ahead, enter_back
):
    length, width = signal.shape
    count = length // block
    order = jnp.arange(count).astype(jnp.float32)[:, None, None]
    carry_ahead = jnp.concatenate([jnp.zeros_like(incl_ahead[:1]), incl_ahead[:-1]], axis=0)
    carry_ahead = carry_ahead + jnp.exp(-rates[None] * block * order) * enter_ahead[None]
    carry_back = jnp.concatenate([incl_back[1:], jnp.zeros_like(incl_back[:1])], axis=0)
    carry_back = carry_back + jnp.exp(-rates[None] * block * (count - 1 - order)) * enter_back[None]
    place = jnp.arange(block).astype(jnp.float32)[:, None, None]
    leading = coefs[None] * jnp.exp(-rates[None] * (place + 1.0))
    trailing = coefs[None] * jnp.exp(-rates[None] * (block - place))
    outer_ahead = jnp.einsum("trc,brc->btc", leading, carry_ahead, precision=lax.Precision.HIGHEST)
    outer_back = jnp.einsum("src,brc->bsc", trailing, carry_back, precision=lax.Precision.HIGHEST)
    signal_blocks = signal.reshape(count, block, width)
    grad_blocks = grad_sig.reshape(count, block, width)
    stacked = jnp.concatenate([signal_blocks, grad_blocks[:, ::-1]], axis=0)
    inner = local_toeplitz(stacked, rates, coefs, block)
    conv_ahead = (inner[:count] + outer_ahead).reshape(length, width)
    conv_back = (inner[count:, ::-1] + outer_back).reshape(length, width)
    return (conv_ahead, conv_back)


def local(section_input, cotangent, norm_gain, short_filter, decay_rate, residue, skip_gain):
    x_rows = section_input[0].astype(jnp.float32)
    grad_out = cotangent[0].astype(jnp.float32)
    gain = norm_gain[0]
    taps = short_filter[0]
    rates = decay_rate[0]
    coefs = residue[0] * jnp.sqrt(1.0 - jnp.exp(-2.0 * rates))
    skip = skip_gain[0]
    rows = x_rows.shape[0]
    depth = taps.shape[1]
    inverse = lax.rsqrt(jnp.mean(x_rows * x_rows, axis=-1, keepdims=True) + 1e-06)
    normed = x_rows * inverse * gain
    rim_prev = shifted(normed[rows - (depth - 1) :], "seq", 1)
    extended = jnp.concatenate([rim_prev, normed], axis=0)
    branches = []
    for branch in range(3):
        total = jnp.zeros_like(normed)
        for lag in range(depth):
            total = total + taps[branch, lag] * extended[depth - 1 - lag : depth - 1 - lag + rows]
        branches.append(total)
    query_rows, key_rows, value_rows = branches
    mixed_in = (key_rows * value_rows).astype(jnp.bfloat16)
    gate_grad = (grad_out * query_rows).astype(jnp.bfloat16)
    mixed_cols, grad_cols = (
        lax.all_to_all(mixed_in, "seq", split_axis=1, concat_axis=0, tiled=True),
        lax.all_to_all(gate_grad, "seq", split_axis=1, concat_axis=0, tiled=True),
    )
    share = mixed_cols.shape[1]
    first = lax.axis_index("seq") * share
    rate_part = lax.dynamic_slice_in_dim(rates, first, share, 1)
    coef_part = lax.dynamic_slice_in_dim(coefs, first, share, 1)
    skip_part = lax.dynamic_slice_in_dim(skip, first, share, 0)
    mixed_f = mixed_cols.astype(jnp.float32)
    grad_f = grad_cols.astype(jnp.float32)
    block = min(128, mixed_f.shape[0])
    incl_ahead, incl_back = block_sums(mixed_f, grad_f, rate_part, block)
    empty = jnp.zeros_like(rate_part)
    conv_ahead, conv_back = apply_filter(
        mixed_f, grad_f, rate_part, coef_part, block, incl_ahead, incl_back, empty, empty
    )
    out_cols = (conv_ahead + skip_part * mixed_f).astype(jnp.bfloat16)
    back_cols = (conv_back + skip_part * grad_f).astype(jnp.bfloat16)
    conv_rows, back_rows = (
        lax.all_to_all(out_cols, "seq", split_axis=0, concat_axis=1, tiled=True),
        lax.all_to_all(back_cols, "seq", split_axis=0, concat_axis=1, tiled=True),
    )
    conv_f = conv_rows.astype(jnp.float32)
    back_f = back_rows.astype(jnp.float32)
    layer_out = (x_rows + query_rows * conv_f).astype(jnp.bfloat16)
    branch_grads = jnp.stack([grad_out * conv_f, back_f * value_rows, back_f * key_rows], axis=0)
    rim_next = shifted(branch_grads[:, : depth - 1], "seq", -1)
    padded = jnp.concatenate([branch_grads, rim_next], axis=1)
    normed_grad = jnp.zeros_like(normed)
    for branch in range(3):
        for lag in range(depth):
            normed_grad = normed_grad + taps[branch, lag] * padded[branch, lag : lag + rows]
    scaled = gain * normed_grad
    input_grad = (
        grad_out
        + inverse * scaled
        - x_rows * inverse * inverse * inverse * jnp.mean(scaled * x_rows, axis=-1, keepdims=True)
    )
    passed_on = shifted(layer_out, "section", 1)
    passed_back = shifted(input_grad.astype(jnp.bfloat16), "section", -1)
    return (passed_on[None], passed_back[None])


def solution(mesh):
    in_specs = (
        P("section", "seq", None),
        P("section", "seq", None),
        P("section", None),
        P("section", None, None, None),
        P("section", None, None),
        P("section", None, None),
        P("section", None),
    )
    out_specs = (P("section", "seq", None), P("section", "seq", None))
    return jax.shard_map(local, mesh=mesh, in_specs=in_specs, out_specs=out_specs, check_vma=False)
```

profile of v0, /device:TPU:103, one launch (start us, length us, event | category | flops | bytes accessed | tf_op | source)
XLA Modules:
  0.0 301.5 jit_solution(6698679638486874137)
XLA Ops:
  8.3 3.8 %collective-permute-start = (f32[2,4096]{1,0:T(2,128)S(1)}, f32[2,4096]{1,0:T(2,128)S(1)}, u32[]{:S(2)}, u32[]{:S(2)}) collective-permute-start(f32[2,4096]{1,0:T(2,128)S(1)} %copy.170), channel_id=1, source_target_pairs={{0,1},{1,2},{2,3},{3,4},{4,5},{5,6},{6,7},{7,8},{8,9},{9,10},{10,1... | collective-permute-start | bytes 98312 | tf_op jit(solution)/shard_map/ppermute | solution.py:10
  16.4 2.3 copy.173
  20.7 9.3 %multiply_convert_fusion = (bf16[128,4096]{0,1:T(8,128)(2,1)}, f32[128,4096]{0,1:T(8,128)}, f32[128,4096]{0,1:T(8,128)}) fusion(f32[128,4096]{0,1:T(8,128)S(1)} %fusion.13, f32[2,4096]{0,1:T(8,128)} %copy.171, f32[4096]{0:T(1024)S(1)} %bitcast.173, f32[4096]{0:T(1024)S(1)} %bitcast.175, f32[4096]{0:T(1024)S(1)} %bitcast.177, f32[4096]{0:T(1024)S(1)} %bitcast.179, ...), kind=kLoop, calls=%fused_computation.70 | loop fusion | flops 7864320 | bytes 7471104 | tf_op jit(solution)/shard_map/convert_element_type | solution.py:90
  30.0 7.1 %all-to-all-start = ((bf16[128,32,128]{0,2,1:T(8,128)(2,1)}), bf16[128,32,128]{0,2,1:T(8,128)(2,1)}, u32[]{:S(2)}, u32[]{:S(2)}) async-start(bf16[128,32,128]{0,2,1:T(8,128)(2,1)} %bitcast.160), calls=%async_computation | async-start | bytes 2097152 | tf_op jit(solution)/shard_map/all_to_all | solution.py:93
  37.1 6.9 %fusion.23 = (bf16[128,4096]{0,1:T(8,128)(2,1)}, f32[128,4096]{0,1:T(8,128)}) fusion(bf16[1,128,4096]{1,2,0:T(8,128)(2,1)} %copy.173, f32[128,4096]{0,1:T(8,128)S(1)} %fusion.13, f32[2,4096]{0,1:T(8,128)} %copy.171, f32[4096]{0:T(1024)S(1)} %bitcast.183, f32[4096]{0:T(1024)S(1)} %bitcast.185, f32[4096]{0:T(1024)S(1)} %bitcast.187), kind=kLoop, calls=%fused_computation.31 | loop fusion | flops 5242880 | bytes 6373376 | tf_op jit(solution)/shard_map/convert_element_type | solution.py:91
  44.0 8.1 %all-to-all-done = bf16[128,32,128]{0,2,1:T(8,128)(2,1)} async-done(((bf16[128,32,128]{0,2,1:T(8,128)(2,1)}), bf16[128,32,128]{0,2,1:T(8,128)(2,1)}, u32[]{:S(2)}, u32[]{:S(2)}) %all-to-all-start) | async-done | bytes 1048608 | tf_op jit(solution)/shard_map/all_to_all | solution.py:93
  52.2 5.9 %all-to-all-start.1 = ((bf16[128,32,128]{0,2,1:T(8,128)(2,1)}), bf16[128,32,128]{0,2,1:T(8,128)(2,1)S(1)}, u32[]{:S(2)}, u32[]{:S(2)}) async-start(bf16[128,32,128]{0,2,1:T(8,128)(2,1)} %bitcast.161), calls=%async_computation.1 | async-start | bytes 2097152 | tf_op jit(solution)/shard_map/all_to_all | solution.py:94
  58.0 3.7 %fusion.54 = f32[128,32,16]{1,2,0:T(8,128)} fusion(bf16[128,32,128]{0,2,1:T(8,128)(2,1)} %all-to-all-done, f32[128]{0:T(128)S(1)} %broadcast_subtract_fusion.2, f32[16,128]{0,1:T(8,128)S(1)} %copy.176), kind=kOutput, calls=%fused_computation.80 | convolution fusion | flops 50593792 | bytes 1319424 | tf_op jit(solution)/shard_map/src,bsc->brc/dot_general | solution.py:23
  66.1 6.9 %all-to-all-done.1 = bf16[128,32,128]{0,2,1:T(8,128)(2,1)S(1)} async-done(((bf16[128,32,128]{0,2,1:T(8,128)(2,1)}), bf16[128,32,128]{0,2,1:T(8,128)(2,1)S(1)}, u32[]{:S(2)}, u32[]{:S(2)}) %all-to-all-start.1) | async-done | bytes 1048608 | tf_op jit(solution)/shard_map/all_to_all | solution.py:94
  73.0 2.5 fusion.57
  83.7 60.0 %gather_fusion = f32[16384,128]{1,0:T(8,128)} fusion(f32[128,128]{1,0:T(8,128)S(1)} %copy.177, s32[16384]{0:T(1024)} %bitcast_clamp_fusion), kind=kCustom, calls=%fused_computation | custom fusion | bytes 16842752 | tf_op jit(solution)/shard_map/jit(_take)/gather | solution.py:41
  143.8 9.4 %copy.178 = f32[128,128,128]{1,0,2:T(8,128)} copy(f32[128,128,128]{2,1,0:T(8,128)} %bitcast.158) | data formatting | bytes 16777216 | tf_op jit(solution)/shard_map/jit(_take)/gather | solution.py:41
  155.1 4.1 %rev.4 = f32[32,128,128]{1,0,2:T(8,128)} reverse(f32[32,128,128]{1,0,2:T(8,128)} %convert_bitcast_fusion.1), dimensions={1} | reverse | bytes 4194304 | tf_op jit(solution)/shard_map/rev | solution.py:62
  161.3 11.1 %fusion.14 = f32[64,128,128]{1,0,2:T(8,128)S(1)} fusion(f32[128,128,128]{1,0,2:T(8,128)} %copy.178, f32[128,128]{1,0:T(8,128)S(1)} %copy-done.15, pred[128,128]{1,0:T(8,128)(4,1)S(1)} %copy-done.37, f32[32,128,128]{1,0,2:T(8,128)S(1)} %copy-done.10, f32[32,128,128]{1,0,2:T(8,128)S(1)} %convert_bitcast_fusion.2), kind=kOutput, calls=%fused_computation.26 | convolution fusion | flops 810549248 | bytes 16859136 | tf_op jit(solution)/shard_map/tsc,bsc->btc/dot_general | solution.py:42
  172.4 7.1 %fusion.45 = bf16[32,128,128]{1,0,2:T(8,128)(2,1)S(1)} fusion(f32[64,128,128]{1,0,2:T(8,128)S(1)} %fusion.14, f32[32,16,128]{0,1,2:T(8,128)S(1)} %copy-done.13, f32[128]{0:T(128)S(1)} %copy-done.39, f32[128]{0:T(128)S(1)} %copy-done.43, f32[16,128]{0,1:T(8,128)S(1)} %copy.176, f32[16,128]{0,1:T(8,128)S(1)} %copy.175, bf16[128,32,128]{0,2,1:T(8,128)(2,1)} %all-to-all-done), kind=kOutput, calls=%fused_computation.60 | convolution fusion | flops 103809024 | bytes 4473856 | tf_op jit(solution)/shard_map/trc,brc->btc/dot_general | solution.py:58
  181.0 5.9 %all-to-all-start.2 = ((bf16[32,128,128]{1,2,0:T(8,128)(2,1)}), bf16[32,128,128]{1,2,0:T(8,128)(2,1)S(1)}, u32[]{:S(2)}, u32[]{:S(2)}) async-start(bf16[32,128,128]{1,2,0:T(8,128)(2,1)} %copy.182), calls=%async_computation.2 | async-start | bytes 2097152 | tf_op jit(solution)/shard_map/all_to_all | solution.py:112
  186.9 3.2 %slice.424 = f32[32,128,128]{1,0,2:T(8,128)} slice(f32[64,128,128]{1,0,2:T(8,128)} %copy-done.9), slice={[32:64], [0:128], [0:128]} | slice | bytes 4194304 | tf_op jit(solution)/shard_map/slice | solution.py:65
  191.4 4.1 %rev.10 = f32[32,128,128]{1,0,2:T(8,128)} reverse(f32[32,128,128]{1,0,2:T(8,128)} %slice.424), dimensions={1} | reverse | bytes 4194304 | tf_op jit(solution)/shard_map/rev | solution.py:65
  195.6 7.8 %fusion.47 = bf16[32,128,128]{1,0,2:T(8,128)(2,1)S(1)} fusion(f32[32,128,128]{1,0,2:T(8,128)} %rev.10, f32[32,16,128]{0,1,2:T(8,128)} %copy.185, f32[128]{0:T(128)S(1)} %copy-done.40, f32[128]{0:T(128)S(1)} %broadcast_subtract_fusion, f32[16,128]{0,1:T(8,128)S(1)} %copy.176, f32[16,128]{0,1:T(8,128)S(1)} %copy.175, bf16[128,32,128]{0,2,1:T(8,128)(2,1)S(1)} %all-to-all-done.1), kind=kOutput, calls=%fused_computation.66 | convolution fusion | flops 103809024 | bytes 4473856 | tf_op jit(solution)/shard_map/src,brc->bsc/dot_general | solution.py:59
  204.8 7.4 %all-to-all-start.3 = ((bf16[32,128,128]{1,2,0:T(8,128)(2,1)}), bf16[32,128,128]{1,2,0:T(8,128)(2,1)S(1)}, u32[]{:S(2)}, u32[]{:S(2)}) async-start(bf16[32,128,128]{1,2,0:T(8,128)(2,1)} %copy.186), calls=%async_computation.3 | async-start | bytes 2097152 | tf_op jit(solution)/shard_map/all_to_all | solution.py:113
  215.0 12.2 %all-to-all-done.3 = bf16[32,128,128]{1,2,0:T(8,128)(2,1)S(1)} async-done(((bf16[32,128,128]{1,2,0:T(8,128)(2,1)}), bf16[32,128,128]{1,2,0:T(8,128)(2,1)S(1)}, u32[]{:S(2)}, u32[]{:S(2)}) %all-to-all-start.3) | async-done | bytes 1048608 | tf_op jit(solution)/shard_map/all_to_all | solution.py:113
  228.2 3.0 bitcast_multiply_fusion.1
  232.5 3.0 %pad_maximum_fusion.1 = f32[3,2,4096]{1,2,0:T(8,128)} fusion(f32[1,128,4096]{1,2,0:T(8,128)S(1)} %bitcast.156, f32[1,128,4096]{1,2,0:T(8,128)S(1)} %bitcast.154, f32[1,128,4096]{1,2,0:T(8,128)S(1)} %copy-done.6), kind=kLoop, calls=%fused_computation.5 | loop fusion | flops 49152 | bytes 6389760 | tf_op jit(solution)/shard_map/stack | solution.py:118
  235.5 4.4 %copy.187 = f32[3,2,4096]{2,1,0:T(2,128)S(1)} copy(f32[3,2,4096]{1,2,0:T(8,128)} %pad_maximum_fusion.1) | data formatting | bytes 196608 | tf_op jit(solution)/shard_map/slice | solution.py:119
  239.9 2.8 collective-permute-start.2
  242.7 3.1 %collective-permute-done.2 = f32[3,2,4096]{2,1,0:T(2,128)S(1)} collective-permute-done((f32[3,2,4096]{2,1,0:T(2,128)S(1)}, f32[3,2,4096]{2,1,0:T(2,128)S(1)}, u32[]{:S(2)}, u32[]{:S(2)}) %collective-permute-start.2) | collective-permute-done | bytes 98336 | tf_op jit(solution)/shard_map/ppermute | solution.py:10
  245.9 4.0 %copy.188 = f32[3,2,4096]{1,2,0:T(8,128)} copy(f32[3,2,4096]{2,1,0:T(2,128)S(1)} %collective-permute-done.2) | data formatting | bytes 196608 | tf_op jit(solution)/shard_map/ppermute | solution.py:10
  249.9 5.8 %pad_maximum_fusion = f32[3,130,4096]{1,2,0:T(8,128)S(1)} fusion(f32[3,2,4096]{1,2,0:T(8,128)} %copy.188, f32[1,128,4096]{1,2,0:T(8,128)} %bitcast.157, f32[1,128,4096]{1,2,0:T(8,128)S(1)} %bitcast.155, f32[1,128,4096]{1,2,0:T(8,128)} %convert_multiply_fusion.3), kind=kLoop, calls=%fused_computation.1 | loop fusion | flops 4792320 | bytes 12779520 | tf_op jit(solution)/shard_map/concatenate | solution.py:120
  255.9 10.4 %fusion.36 = (f32[128]{0:T(128)S(1)}, f32[128,4096]{0,1:T(8,128)S(1)}) fusion(bf16[1,128,4096]{1,2,0:T(8,128)(2,1)S(1)} %copy.169, f32[3,130,4096]{1,2,0:T(8,128)S(1)} %pad_maximum_fusion, f32[4096]{0:T(1024)S(1)} %bitcast.174, f32[4096]{0:T(1024)S(1)} %bitcast.176, f32[128,4096]{0,1:T(8,128)S(1)} %copy-done.3, f32[4096]{0:T(1024)S(1)} %bitcast.178, ...), kind=kLoop, calls=%fused_computation.44 | loop fusion | flops 12582784 | bytes 22184448 | tf_op jit(solution)/shard_map/reduce_sum | solution.py:129
  267.2 4.8 %collective-permute-start.1 = (bf16[128,4096]{0,1:T(8,128)(2,1)S(1)}, bf16[128,4096]{0,1:T(8,128)(2,1)S(1)}, u32[]{:S(2)}, u32[]{:S(2)}) collective-permute-start(bf16[128,4096]{0,1:T(8,128)(2,1)S(1)} %get-tuple-element.20), channel_id=1, source_target_pairs={{0,32},{32,64},{64,96},{96,128},{128,160},{160,192},{192,224},{224... | collective-permute-start | bytes 3145736 | tf_op jit(solution)/shard_map/ppermute | solution.py:10
  273.9 20.8 %collective-permute-done.1 = bf16[128,4096]{0,1:T(8,128)(2,1)S(1)} collective-permute-done((bf16[128,4096]{0,1:T(8,128)(2,1)S(1)}, bf16[128,4096]{0,1:T(8,128)(2,1)S(1)}, u32[]{:S(2)}, u32[]{:S(2)}) %collective-permute-start.1) | collective-permute-done | bytes 1048608 | tf_op jit(solution)/shard_map/ppermute | solution.py:10
  296.1 4.2 %collective-permute-done.3 = bf16[128,4096]{0,1:T(8,128)(2,1)S(1)} collective-permute-done((bf16[128,4096]{0,1:T(8,128)(2,1)S(1)}, bf16[128,4096]{0,1:T(8,128)(2,1)S(1)}, u32[]{:S(2)}, u32[]{:S(2)}) %collective-permute-start.3) | collective-permute-done | bytes 1048608 | tf_op jit(solution)/shard_map/ppermute | solution.py:10
  (198 shorter events, 44.5 us)
Async XLA Ops:
  0.6 15.1 %copy-start = (f32[1,4096]{1,0:T(1,128)S(1)}, f32[1,4096]{1,0:T(1,128)}, u32[]{:S(2)}) copy-start(f32[1,4096]{1,0:T(1,128)} %param.13) | copy-start | bytes 49156
  6.0 9.4 %copy-start.34 = (f32[1,3,3,4096]{3,0,2,1:T(1,128)S(1)}, f32[1,3,3,4096]{3,0,2,1:T(1,128)}, u32[]{:S(2)}) copy-start(f32[1,3,3,4096]{3,0,2,1:T(1,128)} %param.10) | copy-start | bytes 442372
  8.3 10.4 %collective-permute-start = (f32[2,4096]{1,0:T(2,128)S(1)}, f32[2,4096]{1,0:T(2,128)S(1)}, u32[]{:S(2)}, u32[]{:S(2)}) collective-permute-start(f32[2,4096]{1,0:T(2,128)S(1)} %copy.170), channel_id=1, source_target_pairs={{0,1},{1,2},{2,3},{3,4},{4,5},{5,6},{6,7},{7,8},{8,9},{9,10},{10,1... | collective-permute-start | bytes 98312 | tf_op jit(solution)/shard_map/ppermute | solution.py:10
  13.5 59.5 %copy-start.44 = (f32[128]{0:T(128)}, f32[128]{0:T(128)S(1)}, u32[]{:S(2)}) copy-start(f32[128]{0:T(128)S(1)} %iota_convert_fusion.1) | copy-start | bytes 1540
  15.7 21.4 %copy-start.28 = (f32[1,1,4096]{2,1,0:T(1,128)}, f32[1,1,4096]{2,1,0:T(1,128)S(1)}, u32[]{:S(2)}) copy-start(f32[1,1,4096]{2,1,0:T(1,128)S(1)} %get-tuple-element.34) | copy-start | bytes 49156
  15.7 21.4 %copy-start.30 = (f32[1,1,4096]{2,1,0:T(1,128)}, f32[1,1,4096]{2,1,0:T(1,128)S(1)}, u32[]{:S(2)}) copy-start(f32[1,1,4096]{2,1,0:T(1,128)S(1)} %get-tuple-element.35) | copy-start | bytes 49156
  15.7 21.4 %copy-start.32 = (f32[1,1,4096]{2,1,0:T(1,128)}, f32[1,1,4096]{2,1,0:T(1,128)S(1)}, u32[]{:S(2)}) copy-start(f32[1,1,4096]{2,1,0:T(1,128)S(1)} %get-tuple-element.36) | copy-start | bytes 49156
  30.0 22.1 %all-to-all-start = ((bf16[128,32,128]{0,2,1:T(8,128)(2,1)}), bf16[128,32,128]{0,2,1:T(8,128)(2,1)}, u32[]{:S(2)}, u32[]{:S(2)}) async-start(bf16[128,32,128]{0,2,1:T(8,128)(2,1)} %bitcast.160), calls=%async_computation | async-start | bytes 2097152 | tf_op jit(solution)/shard_map/all_to_all | solution.py:93
  52.2 20.9 %all-to-all-start.1 = ((bf16[128,32,128]{0,2,1:T(8,128)(2,1)}), bf16[128,32,128]{0,2,1:T(8,128)(2,1)S(1)}, u32[]{:S(2)}, u32[]{:S(2)}) async-start(bf16[128,32,128]{0,2,1:T(8,128)(2,1)} %bitcast.161), calls=%async_computation.1 | async-start | bytes 2097152 | tf_op jit(solution)/shard_map/all_to_all | solution.py:94
  161.2 11.2 %copy-start.13 = (f32[32,16,128]{0,1,2:T(8,128)S(1)}, f32[32,16,128]{0,1,2:T(8,128)}, u32[]{:S(2)}) copy-start(f32[32,16,128]{0,1,2:T(8,128)} %copy.181) | copy-start | bytes 786436
  161.2 11.2 %copy-start.39 = (f32[128]{0:T(128)S(1)}, f32[128]{0:T(128)}, u32[]{:S(2)}) copy-start(f32[128]{0:T(128)} %fusion.87) | copy-start | bytes 1540
  161.3 11.2 %copy-start.43 = (f32[128]{0:T(128)S(1)}, f32[128]{0:T(128)}, u32[]{:S(2)}) copy-start(f32[128]{0:T(128)} %broadcast_add_fusion) | copy-start | bytes 1540
  172.4 7.1 %copy-start.9 = (f32[64,128,128]{1,0,2:T(8,128)}, f32[64,128,128]{1,0,2:T(8,128)S(1)}, u32[]{:S(2)}) copy-start(f32[64,128,128]{1,0,2:T(8,128)S(1)} %fusion.14) | copy-start | bytes 12582916
  181.0 23.8 %all-to-all-start.2 = ((bf16[32,128,128]{1,2,0:T(8,128)(2,1)}), bf16[32,128,128]{1,2,0:T(8,128)(2,1)S(1)}, u32[]{:S(2)}, u32[]{:S(2)}) async-start(bf16[32,128,128]{1,2,0:T(8,128)(2,1)} %copy.182), calls=%async_computation.2 | async-start | bytes 2097152 | tf_op jit(solution)/shard_map/all_to_all | solution.py:112
  204.8 7.6 %copy-start.7 = (bf16[32,128,128]{1,2,0:T(8,128)(2,1)}, bf16[32,128,128]{1,2,0:T(8,128)(2,1)S(1)}, u32[]{:S(2)}) copy-start(bf16[32,128,128]{1,2,0:T(8,128)(2,1)S(1)} %all-to-all-done.2) | copy-start | bytes 3145732
  204.8 22.4 %all-to-all-start.3 = ((bf16[32,128,128]{1,2,0:T(8,128)(2,1)}), bf16[32,128,128]{1,2,0:T(8,128)(2,1)S(1)}, u32[]{:S(2)}, u32[]{:S(2)}) async-start(bf16[32,128,128]{1,2,0:T(8,128)(2,1)} %copy.186), calls=%async_computation.3 | async-start | bytes 2097152 | tf_op jit(solution)/shard_map/all_to_all | solution.py:113
  239.9 5.9 %collective-permute-start.2 = (f32[3,2,4096]{2,1,0:T(2,128)S(1)}, f32[3,2,4096]{2,1,0:T(2,128)S(1)}, u32[]{:S(2)}, u32[]{:S(2)}) collective-permute-start(f32[3,2,4096]{2,1,0:T(2,128)S(1)} %copy.187), channel_id=1, source_target_pairs={{1,0},{2,1},{3,2},{4,3},{5,4},{6,5},{7,6},{8,7},{9,8},{10,9},{11,1... | collective-permute-start | bytes 294920 | tf_op jit(solution)/shard_map/ppermute | solution.py:10
  249.9 5.9 %copy-start.17 = (f32[1,1,4096]{2,1,0:T(1,128)S(1)}, f32[1,1,4096]{2,1,0:T(1,128)}, u32[]{:S(2)}) copy-start(f32[1,1,4096]{2,1,0:T(1,128)} %copy-done.16) | copy-start | bytes 49156
  249.9 5.9 %copy-start.19 = (f32[1,1,4096]{2,1,0:T(1,128)S(1)}, f32[1,1,4096]{2,1,0:T(1,128)}, u32[]{:S(2)}) copy-start(f32[1,1,4096]{2,1,0:T(1,128)} %copy-done.18) | copy-start | bytes 49156
  249.9 5.9 %copy-start.21 = (f32[1,1,4096]{2,1,0:T(1,128)S(1)}, f32[1,1,4096]{2,1,0:T(1,128)}, u32[]{:S(2)}) copy-start(f32[1,1,4096]{2,1,0:T(1,128)} %copy-done.20) | copy-start | bytes 49156
  249.9 5.9 %copy-start.23 = (f32[1,1,4096]{2,1,0:T(1,128)S(1)}, f32[1,1,4096]{2,1,0:T(1,128)}, u32[]{:S(2)}) copy-start(f32[1,1,4096]{2,1,0:T(1,128)} %copy-done.22) | copy-start | bytes 49156
  249.9 5.9 %copy-start.25 = (f32[1,1,4096]{2,1,0:T(1,128)S(1)}, f32[1,1,4096]{2,1,0:T(1,128)}, u32[]{:S(2)}) copy-start(f32[1,1,4096]{2,1,0:T(1,128)} %copy-done.24) | copy-start | bytes 49156
  249.9 5.9 %copy-start.27 = (f32[1,1,4096]{2,1,0:T(1,128)S(1)}, f32[1,1,4096]{2,1,0:T(1,128)}, u32[]{:S(2)}) copy-start(f32[1,1,4096]{2,1,0:T(1,128)} %copy-done.26) | copy-start | bytes 49156
  249.9 5.9 %copy-start.29 = (f32[1,1,4096]{2,1,0:T(1,128)S(1)}, f32[1,1,4096]{2,1,0:T(1,128)}, u32[]{:S(2)}) copy-start(f32[1,1,4096]{2,1,0:T(1,128)} %copy-done.28) | copy-start | bytes 49156
  249.9 5.9 %copy-start.31 = (f32[1,1,4096]{2,1,0:T(1,128)S(1)}, f32[1,1,4096]{2,1,0:T(1,128)}, u32[]{:S(2)}) copy-start(f32[1,1,4096]{2,1,0:T(1,128)} %copy-done.30) | copy-start | bytes 49156
  249.9 5.9 %copy-start.33 = (f32[1,1,4096]{2,1,0:T(1,128)S(1)}, f32[1,1,4096]{2,1,0:T(1,128)}, u32[]{:S(2)}) copy-start(f32[1,1,4096]{2,1,0:T(1,128)} %copy-done.32) | copy-start | bytes 49156
  249.9 5.9 %copy-start.36 = (f32[1,4096]{1,0:T(1,128)S(1)}, f32[1,4096]{1,0:T(1,128)}, u32[]{:S(2)}) copy-start(f32[1,4096]{1,0:T(1,128)} %param.9) | copy-start | bytes 49156
  255.9 10.4 %copy-start.11 = (f32[128,4096]{0,1:T(8,128)S(1)}, f32[128,4096]{0,1:T(8,128)}, u32[]{:S(2)}) copy-start(f32[128,4096]{0,1:T(8,128)} %get-tuple-element.18) | copy-start | bytes 6291460
  255.9 10.4 %copy-start.42 = (f32[128]{0:T(128)S(1)}, f32[128]{0:T(128)}, u32[]{:S(2)}) copy-start(f32[128]{0:T(128)} %copy-done.41) | copy-start | bytes 1540
  267.2 27.5 %collective-permute-start.1 = (bf16[128,4096]{0,1:T(8,128)(2,1)S(1)}, bf16[128,4096]{0,1:T(8,128)(2,1)S(1)}, u32[]{:S(2)}, u32[]{:S(2)}) collective-permute-start(bf16[128,4096]{0,1:T(8,128)(2,1)S(1)} %get-tuple-element.20), channel_id=1, source_target_pairs={{0,32},{32,64},{64,96},{96,128},{128,160},{160,192},{192,224},{224... | collective-permute-start | bytes 3145736 | tf_op jit(solution)/shard_map/ppermute | solution.py:10
  272.0 28.2 %collective-permute-start.3 = (bf16[128,4096]{0,1:T(8,128)(2,1)S(1)}, bf16[128,4096]{0,1:T(8,128)(2,1)S(1)}, u32[]{:S(2)}, u32[]{:S(2)}) collective-permute-start(bf16[128,4096]{0,1:T(8,128)(2,1)S(1)} %get-tuple-element.19), channel_id=1, source_target_pairs={{32,0},{64,32},{96,64},{128,96},{160,128},{192,160},{224,192},{256... | collective-permute-start | bytes 3145736 | tf_op jit(solution)/shard_map/ppermute | solution.py:10
  294.8 6.8 %copy-start.1 = (f32[1,4096]{1,0:T(1,128)S(1)}, f32[1,4096]{1,0:T(1,128)}, u32[]{:S(2)}) copy-start(f32[1,4096]{1,0:T(1,128)} %param.13) | copy-start | bytes 49156
  (22 other events, 76.5 us)
where the time goes:
time: 304 us; the launch traced here: 302 us
  local copies, waits for them, and re-layouts  119 us (39%)
  waiting for transfers between devices  55.4 us (18%)
  other arithmetic  53.9 us (18%)
  starting transfers between devices  39.5 us (13%)
  matrix products  32.4 us (11%)
    gather x2, local copies, waits for them, and re-layouts, local_toeplitz(): table = jnp.take(filter_head, lag_table, axis=0) * lower  69.4 us
    ppermute x4, waiting for transfers between devices, shifted(): return lax.ppermute(block, axis, route)  28.1 us
    ppermute x4, starting transfers between devices, shifted(): return lax.ppermute(block, axis, route)  13.3 us
    all_to_all x1, waiting for transfers between devices, local(): lax.all_to_all(back_cols, 'seq', split_axis=0, concat_axis=1, tiled=True)  12.2 us
    unnamed x99, local copies, waits for them, and re-layouts  11.2 us
    dot_general x1, matrix products, local_toeplitz(): jnp.einsum('tsc,bsc->btc', table, stacked, precision=lax.Precision.HIGH)  11.1 us
    reduce_sum x1, other arithmetic, local(): jnp.mean(scaled * x_rows, axis=-1, keepdims=True)  10.4 us
    convert_element_type x1, other arithmetic, local(): mixed_in = (key_rows * value_rows).astype(jnp.bfloat16)  9.34 us
  transfers between devices with their start and end apart: 8, of which 6 were waited for; matrix products, arithmetic and copies ran while one was open for 14% of the time, Pallas kernels for 0%

commit v1 on v0

v1 whole, which is shorter than its diff:
```python
import functools

import jax
import jax.numpy as jnp
import ml_dtypes
import numpy as np
from jax import lax
from jax.experimental import pallas as pl
from jax.experimental.pallas import tpu as pltpu
from jax.sharding import PartitionSpec as P

MODES = 16
NODES = 14
PADDED = 16
LANES = 128
WIDE = 256
F32 = jnp.float32
BF16 = jnp.bfloat16


def node_places(rows):
    k = np.arange(NODES)
    return 0.5 * (rows - 1) * (1.0 - np.cos((2 * k + 1) * np.pi / (2 * NODES)))


def cardinals(rows):
    nodes = node_places(rows)
    lags = np.arange(rows, dtype=np.float64)
    table = np.ones((rows, NODES))
    for k in range(NODES):
        for m in range(NODES):
            if m != k:
                table[:, k] *= (lags - nodes[m]) / (nodes[k] - nodes[m])
    return table


def halves(table):
    high = table.astype(ml_dtypes.bfloat16)
    low = (table - high.astype(np.float64)).astype(ml_dtypes.bfloat16)
    return high, low


def constants(rows):
    table = cardinals(rows)
    padded = np.zeros((rows, PADDED))
    padded[:, :NODES] = table
    high, low = halves(padded)
    flip_high, flip_low = high[::-1], low[::-1]
    moment_ahead = np.concatenate([flip_high.T, flip_low.T], axis=0)
    moment_back = np.concatenate([high.T, low.T], axis=0)
    spread_ahead = np.concatenate([high, low, high], axis=1)
    spread_back = np.concatenate([flip_high, flip_low, flip_high], axis=1)
    lag = np.arange(rows)[:, None] - np.arange(rows)[None, :]
    toeplitz = np.where(lag[:, :, None] >= 0, table[np.maximum(lag, 0)], 0.0)
    near_ahead = np.transpose(toeplitz, (0, 2, 1)).reshape(rows, NODES * rows)
    near_back = np.transpose(toeplitz, (1, 2, 0)).reshape(rows, NODES * rows)
    places = np.zeros((PADDED, LANES), np.float32)
    places[:NODES] = node_places(rows)[:, None]
    cast = ml_dtypes.bfloat16
    return dict(
        moments=np.concatenate([moment_ahead, moment_back], axis=0),
        spread=np.concatenate([spread_ahead, spread_back], axis=0),
        near=np.stack([near_ahead, near_back]).astype(cast),
        places=places,
    )


def tables_kernel(nodes, rates_ref, residue_ref, places_ref, powers_ref, columns_ref, nodal_ref, coef_ref):
    rates = rates_ref[...]
    coef = residue_ref[...] * jnp.sqrt(1.0 - jnp.exp(-2.0 * rates))
    coef_ref[...] = coef
    for k in range(NODES):
        powers_ref[k] = jnp.exp(rates * (-nodes[k]))
    places = jnp.concatenate([places_ref[...]] * (rates.shape[1] // LANES), axis=1)
    nodal = jnp.zeros_like(rates)
    for r in range(MODES):
        column = jnp.exp(-rates[r : r + 1] * places)
        columns_ref[r] = column
        nodal = nodal + column * coef[r : r + 1]
    nodal_ref[...] = nodal


def taps_of(taps_ref, cols):
    return [[taps_ref[3 * j + i : 3 * j + i + 1, cols] for i in range(3)] for j in range(3)]


def filtered(taps, now, past, older):
    return [t[0] * now + t[1] * past + t[2] * older for t in taps]


def start_kernel(
    x_ref, cot_ref, rim_ref, gain_ref, taps_ref, powers_ref, moments_ref,
    mixed_ref, gate_ref, state_ref, inverse_ref, front_ref, normed_ref,
):
    rows, width = x_ref.shape

    def square(i, total):
        x = x_ref[:, pl.ds(pl.multiple_of(i * LANES, LANES), LANES)].astype(F32)
        return total + x * x

    total = lax.fori_loop(0, width // LANES, square, jnp.zeros((rows, LANES), F32))
    inverse = lax.rsqrt(jnp.sum(total, axis=1, keepdims=True) * (1.0 / width) + 1e-06)
    rim_all = rim_ref[...].astype(F32)
    rim_inverse = lax.rsqrt(jnp.sum(rim_all * rim_all, axis=1, keepdims=True) * (1.0 / width) + 1e-06)
    inverse_ref[0:rows] = jnp.broadcast_to(inverse, (rows, LANES))
    inverse_ref[rows : rows + 2] = jnp.broadcast_to(rim_inverse, (2, LANES))
    front_ref[0:2] = x_ref[0:16].astype(F32)[0:2]
    front_ref[2:4] = cot_ref[0:16].astype(F32)[0:2]

    def chunk(i, carry):
        cols = pl.ds(pl.multiple_of(i * WIDE, WIDE), WIDE)
        gain = gain_ref[:, cols]
        now = x_ref[:, cols].astype(F32) * inverse * gain
        normed_ref[8 : rows + 8] = now
        normed_ref[6:8] = rim_ref[:, cols].astype(F32) * rim_inverse * gain
        past = normed_ref[7 : rows + 7]
        older = normed_ref[6 : rows + 6]
        query, key, value = filtered(taps_of(taps_ref, cols), now, past, older)
        mixed = (key * value).astype(BF16)
        gate = (cot_ref[:, cols].astype(F32) * query).astype(BF16)
        mixed_ref[:, cols] = mixed
        gate_ref[:, cols] = gate
        for side, signal in enumerate((mixed, gate)):
            both = jnp.dot(
                moments_ref[32 * side : 32 * side + 32], signal, preferred_element_type=F32
            )
            moment = both[:PADDED] + both[PADDED:]
            state = powers_ref[0, :, cols] * moment[0:1]
            for k in range(1, NODES):
                state = state + powers_ref[k, :, cols] * moment[k : k + 1]
            for h in range(WIDE // LANES):
                state_ref[i * (WIDE // LANES) + h, MODES * side : MODES * (side + 1)] = state[
                    :, h * LANES : (h + 1) * LANES
                ].astype(BF16)
        return carry

    lax.fori_loop(0, width // WIDE, chunk, 0)


def near_kernel(mixed_ref, gate_ref, nodal_ref, skip_ref, near_ref, ahead_ref, back_ref, parts_ref):
    rows = mixed_ref.shape[0]
    nodal = nodal_ref[...].astype(BF16)
    for side, (signal_ref, out_ref) in enumerate(((mixed_ref, ahead_ref), (gate_ref, back_ref))):
        signal = signal_ref[...]
        for k in range(NODES):
            parts_ref[k * rows : (k + 1) * rows] = signal * nodal[k : k + 1]
        out_ref[...] = (
            jnp.dot(near_ref[side], parts_ref[...], preferred_element_type=F32)
            + skip_ref[...] * signal.astype(F32)
        )


def scan_kernel(rates_ref, state_ref, enter_ref, *, rows):
    count = state_ref.shape[0]
    first = lax.axis_index("seq") * LANES
    rates = rates_ref[:, pl.ds(pl.multiple_of(first, LANES), LANES)]
    decay = jnp.exp(rates * (-float(rows)))
    ahead = jnp.zeros((MODES, LANES), F32)
    back = jnp.zeros((MODES, LANES), F32)
    for d in range(count):
        enter_ref[d, 0:MODES] = ahead.astype(BF16)
        ahead = decay * ahead + state_ref[d, 0:MODES].astype(F32)
        e = count - 1 - d
        enter_ref[e, MODES : 2 * MODES] = back.astype(BF16)
        back = decay * back + state_ref[e, MODES : 2 * MODES].astype(F32)


def finish_kernel(
    x_ref, cot_ref, ahead_ref, back_ref, columns_ref, enter_ref, state_ref, coef_ref, rates_ref,
    gain_ref, taps_ref, skip_ref, rim_ref, front_ref, inverse_ref, spread_ref,
    layer_ref, grad_ref,
    normed_ref, one_ref, two_ref, base_ref, total_ref, scale_ref,
):
    step = pl.program_id(0)
    rows, width = x_ref.shape
    inverse = inverse_ref[0:rows, 0:1]

    @pl.when(step == 0)
    def _():
        total_ref[...] = jnp.zeros_like(total_ref)
        after = front_ref[0:2]
        scale = lax.rsqrt(jnp.sum(after * after, axis=1, keepdims=True) * (1.0 / width) + 1e-06)
        scale_ref[0:2] = jnp.broadcast_to(scale, (2, LANES))

    cols = pl.ds(pl.multiple_of(step * WIDE, WIDE), WIDE)
    gain = gain_ref[...]
    skip = skip_ref[...]
    taps = taps_of(taps_ref, slice(None))
    x = x_ref[:, cols].astype(F32)
    cot = cot_ref[...].astype(F32)
    now = x * inverse * gain
    normed_ref[8 : rows + 8] = now
    normed_ref[6:8] = rim_ref[:, cols].astype(F32) * inverse_ref[rows : rows + 2, 0:1] * gain
    normed_ref[rows + 8 : rows + 10] = front_ref[0:2, cols] * scale_ref[0:2, 0:1] * gain
    past = normed_ref[7 : rows + 7]
    older = normed_ref[6 : rows + 6]
    query, key, value = filtered(taps, now, past, older)
    n_query, n_key, n_value = filtered(
        taps, normed_ref[rows + 8 : rows + 10], normed_ref[rows + 7 : rows + 9], normed_ref[rows + 6 : rows + 8]
    )

    coef = coef_ref[...]
    rates = rates_ref[...]
    decay = jnp.exp(-rates)
    lead = coef * decay
    entered = [jnp.concatenate([enter_ref[h, 16 * s : 16 * s + 16].astype(F32) for h in range(WIDE // LANES)], axis=1) for s in range(2)]
    own = jnp.concatenate([state_ref[h, 0:16].astype(F32) for h in range(WIDE // LANES)], axis=1)

    convs = []
    for side, near_ref in enumerate((ahead_ref, back_ref)):
        weight = lead * entered[side]
        nodal = columns_ref[0] * weight[0:1]
        for r in range(1, MODES):
            nodal = nodal + columns_ref[r] * weight[r : r + 1]
        high = nodal.astype(BF16)
        low = (nodal - high.astype(F32)).astype(BF16)
        far = jnp.dot(
            spread_ref[side * rows : (side + 1) * rows],
            jnp.concatenate([high, high, low], axis=0),
            preferred_element_type=F32,
        )
        convs.append((near_ref[...] + far).astype(BF16).astype(F32))
    conv, conv_back = convs

    layer_ref[...] = (x + query * conv).astype(BF16)

    n_cot = front_ref[2:4, cols]
    n_mixed = (n_key * n_value).astype(BF16).astype(F32)
    n_gate = (n_cot * n_query).astype(BF16).astype(F32)
    leave = jnp.exp(rates * (-float(rows))) * entered[0] + own
    over = lambda a: jnp.sum(a, axis=0, keepdims=True)
    direct = over(coef) + skip
    mixed_0, mixed_1 = n_mixed[0:1], n_mixed[1:2]
    gate_0, gate_1 = n_gate[0:1], n_gate[1:2]
    conv_0 = over(lead * leave) + direct * mixed_0
    conv_1 = over(lead * decay * leave) + over(lead) * mixed_0 + direct * mixed_1
    back_0 = over(coef * entered[1]) + skip * gate_0
    back_1 = over(coef * (1.0 / decay) * (entered[1] - gate_0)) + skip * gate_1
    n_conv = jnp.concatenate([conv_0, conv_1], axis=0).astype(BF16).astype(F32)
    n_back = jnp.concatenate([back_0, back_1], axis=0).astype(BF16).astype(F32)

    grads = (cot * conv, conv_back * value, conv_back * key)
    n_grads = (n_cot * n_conv, n_back * n_value, n_back * n_key)
    lagged = [sum(taps[j][i] * grads[j] for j in range(3)) for i in range(3)]
    one_ref[0:rows] = lagged[1]
    two_ref[0:rows] = lagged[2]
    one_ref[rows : rows + 2] = sum(taps[j][1] * n_grads[j] for j in range(3))
    two_ref[rows : rows + 2] = sum(taps[j][2] * n_grads[j] for j in range(3))
    scaled = gain * (lagged[0] + one_ref[1 : rows + 1] + two_ref[2 : rows + 2])
    base_ref[:, cols] = cot + inverse * scaled
    product = scaled * x
    partial = total_ref[...]
    for h in range(WIDE // LANES):
        partial = partial + product[:, h * LANES : (h + 1) * LANES]
    total_ref[...] = partial

    @pl.when(step == pl.num_programs(0) - 1)
    def _():
        mean = jnp.sum(total_ref[...], axis=1, keepdims=True) * (1.0 / width)
        factor = inverse * inverse * inverse * mean

        def emit(i, carry):
            part = pl.ds(pl.multiple_of(i * WIDE, WIDE), WIDE)
            grad_ref[:, part] = (base_ref[:, part] - x_ref[:, part].astype(F32) * factor).astype(BF16)
            return carry

        lax.fori_loop(0, width // WIDE, emit, 0)


def shifted(block, axis, distance):
    devices = range(lax.axis_size(axis))
    route = [(i - distance, i) for i in devices if i - distance in devices]
    return lax.ppermute(block, axis, route)


def whole(shape):
    return pl.BlockSpec(shape, lambda *i: (0,) * len(shape))


def across(shape, step, axis=None):
    axis = len(shape) - 1 if axis is None else axis
    block = shape[:axis] + (step,) + shape[axis + 1 :]
    return pl.BlockSpec(block, lambda i: (0,) * axis + (i,) + (0,) * (len(shape) - axis - 1))


def params(mib):
    return pltpu.CompilerParams(vmem_limit_bytes=mib * 1024 * 1024)


def local(section_input, cotangent, norm_gain, short_filter, decay_rate, residue, skip_gain):
    x = section_input[0]
    cot = cotangent[0]
    rows, width = x.shape
    gain = norm_gain
    taps = short_filter[0].reshape(9, width)
    rates = decay_rate[0]
    weights = residue[0]
    skip = skip_gain
    count = lax.axis_size("seq")
    fixed = constants(rows)
    shape = jax.ShapeDtypeStruct

    rim = shifted(x[rows - 2 :], "seq", 1)

    step = 512
    powers, columns, nodal, coef = pl.pallas_call(
        functools.partial(tables_kernel, [float(p) for p in node_places(rows)]),
        grid=(width // step,),
        in_specs=[across((MODES, width), step), across((MODES, width), step), whole((PADDED, LANES))],
        out_specs=[
            across((NODES, MODES, width), step),
            across((MODES, PADDED, width), step),
            across((PADDED, width), step),
            across((MODES, width), step),
        ],
        out_shape=[
            shape((NODES, MODES, width), F32),
            shape((MODES, PADDED, width), F32),
            shape((PADDED, width), F32),
            shape((MODES, width), F32),
        ],
        compiler_params=params(24),
        name="tables",
    )(rates, weights, jnp.asarray(fixed["places"]))

    mixed, gate, state, inverse, front = pl.pallas_call(
        start_kernel,
        out_shape=[
            shape((rows, width), BF16),
            shape((rows, width), BF16),
            shape((width // LANES, 2 * MODES, LANES), BF16),
            shape((rows + 8, LANES), F32),
            shape((4, width), F32),
        ],
        scratch_shapes=[pltpu.VMEM((rows + 8, WIDE), F32)],
        compiler_params=params(32),
        name="start",
    )(x, cot, rim, gain, taps, powers, jnp.asarray(fixed["moments"]))

    gathered = lax.all_to_all(state, "seq", split_axis=0, concat_axis=0, tiled=True)
    front = shifted(front, "seq", -1)

    ahead, back = pl.pallas_call(
        near_kernel,
        grid=(width // WIDE,),
        in_specs=[
            across((rows, width), WIDE),
            across((rows, width), WIDE),
            across((PADDED, width), WIDE),
            across((1, width), WIDE),
            whole((2, rows, NODES * rows)),
        ],
        out_specs=[across((rows, width), WIDE), across((rows, width), WIDE)],
        out_shape=[shape((rows, width), F32), shape((rows, width), F32)],
        scratch_shapes=[pltpu.VMEM((NODES * rows, WIDE), BF16)],
        compiler_params=params(24),
        cost_estimate=pl.CostEstimate(
            flops=4 * NODES * rows * rows * width, bytes_accessed=7 << 20, transcendentals=0
        ),
        name="near",
    )(mixed, gate, nodal, skip, jnp.asarray(fixed["near"]))

    entering = pl.pallas_call(
        functools.partial(scan_kernel, rows=rows),
        out_shape=shape((count, 2 * MODES, LANES), BF16),
        compiler_params=params(16),
        name="scan",
    )(rates, gathered)
    enter = lax.all_to_all(entering, "seq", split_axis=0, concat_axis=0, tiled=True)

    pieces = WIDE // LANES
    layer_out, input_grad = pl.pallas_call(
        finish_kernel,
        grid=(width // WIDE,),
        in_specs=[
            whole((rows, width)),
            across((rows, width), WIDE),
            across((rows, width), WIDE),
            across((rows, width), WIDE),
            across((MODES, PADDED, width), WIDE),
            across((width // LANES, 2 * MODES, LANES), pieces, 0),
            across((width // LANES, 2 * MODES, LANES), pieces, 0),
            across((MODES, width), WIDE),
            across((MODES, width), WIDE),
            across((1, width), WIDE),
            across((9, width), WIDE),
            across((1, width), WIDE),
            whole((2, width)),
            whole((4, width)),
            whole((rows + 8, LANES)),
            whole((2 * rows, 3 * PADDED)),
        ],
        out_specs=[across((rows, width), WIDE), whole((rows, width))],
        out_shape=[shape((rows, width), BF16), shape((rows, width), BF16)],
        scratch_shapes=[
            pltpu.VMEM((rows + 16, WIDE), F32),
            pltpu.VMEM((rows + 8, WIDE), F32),
            pltpu.VMEM((rows + 8, WIDE), F32),
            pltpu.VMEM((rows, width), F32),
            pltpu.VMEM((rows, LANES), F32),
            pltpu.VMEM((8, LANES), F32),
        ],
        compiler_params=params(32),
        name="finish",
    )(
        x, cot, ahead, back, columns, enter, state, coef, rates,
        gain, taps, skip, rim, front, inverse, jnp.asarray(fixed["spread"]),
    )

    passed_on = shifted(layer_out, "section", 1)
    passed_back = shifted(input_grad, "section", -1)
    return passed_on[None], passed_back[None]


def solution(mesh):
    in_specs = (
        P("section", "seq", None),
        P("section", "seq", None),
        P("section", None),
        P("section", None, None, None),
        P("section", None, None),
        P("section", None, None),
        P("section", None),
    )
    out_specs = (P("section", "seq", None), P("section", "seq", None))
    return jax.shard_map(local, mesh=mesh, in_specs=in_specs, out_specs=out_specs, check_vma=False)
```

time: 304 us -> 116 us (0.38)
  the two profiles are of different devices: /device:TPU:103 before, /device:TPU:230 now
where the time goes in v1:
time: 116 us; the launch traced here: 114 us
  Pallas kernels  29.7 us (26%)
  waiting for transfers between devices  28.5 us (25%)
  starting transfers between devices  27.9 us (24%)
  local copies, waits for them, and re-layouts  26.1 us (22%)
  other arithmetic  1.31 us (1%)
    ppermute x4, waiting for transfers between devices, shifted(): return lax.ppermute(block, axis, route)  26.1 us
    unnamed x54, local copies, waits for them, and re-layouts  25.1 us
    ppermute x4, starting transfers between devices, shifted(): return lax.ppermute(block, axis, route)  13.5 us
    pallas_call x1, Pallas kernels, local(): pl.pallas_call(finish_kernel, grid=(width // WIDE,), in_specs=[whole((row...  12.3 us
    all_to_all x1, starting transfers between devices, local(): lax.all_to_all(state, 'seq', split_axis=0, concat_axis=0, tiled=True)  8.6 us
    pallas_call x1, Pallas kernels, local(): pl.pallas_call(near_kernel, grid=(width // WIDE,), in_specs=[across((rows...  7.65 us
    pallas_call x1, Pallas kernels, local(): pl.pallas_call(start_kernel, out_shape=[shape((rows, width), BF16), shape...  6.77 us
    all_to_all x1, starting transfers between devices, local(): lax.all_to_all(entering, 'seq', split_axis=0, concat_axis=0, tiled=True)  5.81 us
  transfers between devices with their start and end apart: 6, of which 3 were waited for; matrix products, arithmetic and copies ran while one was open for 1% of the time, Pallas kernels for 9%

profile of v1, /device:TPU:230, one launch (start us, length us, event | category | flops | bytes accessed | tf_op | source)
XLA Modules:
  0.0 114.3 jit_solution(10389766583339556226)
XLA Ops:
  1.5 1.9 %collective-permute-start = (bf16[2,4096]{1,0:T(2,128)(2,1)S(1)}, bf16[2,4096]{1,0:T(2,128)(2,1)S(1)}, u32[]{:S(2)}, u32[]{:S(2)}) collective-permute-start(bf16[2,4096]{1,0:T(2,128)(2,1)S(1)} %slice_bitcast_fusion), channel_id=1, source_target_pairs={{0,1},{1,2},{2,3},{3,4},{4,5},{5,6},{6,7},{7,8},{8,9},{9,10},{10,1... | collective-permute-start | bytes 49160 | tf_op jit(solution)/shard_map/ppermute | solution.py:273
  3.4 1.3 %reduce = f32[3,3,4096]{2,1,0:T(4,128)S(1)} reduce(f32[1,3,3,4096]{3,0,2,1:T(1,128)} %param.14, f32[]{:T(128)} %constant.19), dimensions={0}, to_apply=%param.14.reduce_sub_computation | reduce | bytes 294916 | tf_op args[3]
  4.8 0.9 copy-done.6
  5.8 0.9 copy-done.12
  7.4 2.2 %tables.1 = (f32[14,16,4096]{2,1,0:T(8,128)S(1)}, f32[16,16,4096]{2,1,0:T(8,128)S(1)}, f32[16,4096]{1,0:T(8,128)S(1)}, f32[16,4096]{1,0:T(8,128)S(1)}) custom-call(f32[16,4096]{1,0:T(8,128)S(1)} %bitcast.12, f32[16,4096]{1,0:T(8,128)S(1)} %bitcast.15, f32[16,128]{1,0:T(8,128)S(1)} %copy-done.18), custom_call_target="tpu_custom_call" | custom-call | tf_op jit(solution)/shard_map/tables/pallas_call | solution.py:306
  9.6 2.0 %copy-done.2 = f32[16,16,4096]{2,1,0:T(8,128)} copy-done((f32[16,16,4096]{2,1,0:T(8,128)}, f32[16,16,4096]{2,1,0:T(8,128)S(1)}, u32[]{:S(2)}) %copy-start.2) | copy-done | bytes 4194328
  11.6 1.3 %copy-done = bf16[1,128,4096]{2,1,0:T(8,128)(2,1)S(1)} copy-done((bf16[1,128,4096]{2,1,0:T(8,128)(2,1)S(1)}, bf16[1,128,4096]{2,1,0:T(8,128)(2,1)}, u32[]{:S(2)}) %copy-start) | copy-done | bytes 1048600
  12.9 1.2 %copy-done.4 = bf16[1,128,4096]{2,1,0:T(8,128)(2,1)S(1)} copy-done((bf16[1,128,4096]{2,1,0:T(8,128)(2,1)S(1)}, bf16[1,128,4096]{2,1,0:T(8,128)(2,1)}, u32[]{:S(2)}) %copy-start.4) | copy-done | bytes 1048600
  15.6 6.8 %start.1 = (bf16[128,4096]{1,0:T(8,128)(2,1)S(1)}, bf16[128,4096]{1,0:T(8,128)(2,1)S(1)}, bf16[32,32,128]{2,1,0:T(8,128)(2,1)}, f32[136,128]{1,0:T(8,128)S(1)}, f32[4,4096]{1,0:T(4,128)S(1)}) custom-call(bf16[128,4096]{1,0:T(8,128)(2,1)S(1)} %bitcast.8, bf16[128,4096]{1,0:T(8,128)(2,1)S(1)} %bitcast.10, bf16[2,4096]{1,0:T(2,128)(2,1)S(1)} %collective-permute-done.rim_ref, ...), custom_call_target="tpu_custom_call" | custom-call | tf_op jit(solution)/shard_map/start/pallas_call | solution.py:326
  22.3 1.0 copy-done.19
  23.3 1.0 copy-done.21
  24.3 8.6 %all-to-all-start = ((bf16[32,32,128]{2,1,0:T(8,128)(2,1)}), bf16[32,32,128]{2,1,0:T(8,128)(2,1)S(1)}, u32[]{:S(2)}, u32[]{:S(2)}) async-start(bf16[32,32,128]{2,1,0:T(8,128)(2,1)} %get-tuple-element.22.state_ref), calls=%async_computation | async-start | bytes 524288 | tf_op jit(solution)/shard_map/all_to_all | solution.py:340
  32.9 4.6 %collective-permute-start.1 = (f32[4,4096]{1,0:T(4,128)S(1)}, f32[4,4096]{1,0:T(4,128)S(1)}, u32[]{:S(2)}, u32[]{:S(2)}) collective-permute-start(f32[4,4096]{1,0:T(4,128)S(1)} %get-tuple-element.24), channel_id=1, source_target_pairs={{1,0},{2,1},{3,2},{4,3},{5,4},{6,5},{7,6},{8,7},{9,8},{10,9},{11,1... | collective-permute-start | bytes 196616 | tf_op jit(solution)/shard_map/ppermute | solution.py:273
  37.5 2.4 %all-to-all-done.state_ref = bf16[32,32,128]{2,1,0:T(8,128)(2,1)S(1)} async-done(((bf16[32,32,128]{2,1,0:T(8,128)(2,1)}), bf16[32,32,128]{2,1,0:T(8,128)(2,1)S(1)}, u32[]{:S(2)}, u32[]{:S(2)}) %all-to-all-start) | async-done | bytes 262176 | tf_op jit(solution)/shard_map/all_to_all | solution.py:340
  40.7 5.8 %all-to-all-start.1 = ((bf16[32,32,128]{2,1,0:T(8,128)(2,1)}), bf16[32,32,128]{2,1,0:T(8,128)(2,1)S(1)}, u32[]{:S(2)}, u32[]{:S(2)}) async-start(bf16[32,32,128]{2,1,0:T(8,128)(2,1)} %scan.1), calls=%async_computation.1 | async-start | bytes 524288 | tf_op jit(solution)/shard_map/all_to_all | solution.py:369
  46.5 1.2 %copy-done.20 = bf16[128,4096]{1,0:T(8,128)(2,1)S(1)} copy-done((bf16[128,4096]{1,0:T(8,128)(2,1)S(1)}, bf16[128,4096]{1,0:T(8,128)(2,1)}, u32[]{:S(2)}) %copy-start.20) | copy-done | bytes 1048600
  47.7 1.2 %copy-done.22 = bf16[128,4096]{1,0:T(8,128)(2,1)S(1)} copy-done((bf16[128,4096]{1,0:T(8,128)(2,1)S(1)}, bf16[128,4096]{1,0:T(8,128)(2,1)}, u32[]{:S(2)}) %copy-start.22) | copy-done | bytes 1048600
  49.0 0.9 copy-done.24
  49.9 1.2 %copy-done.25 = bf16[2,128,1792]{2,1,0:T(8,128)(2,1)S(1)} copy-done((bf16[2,128,1792]{2,1,0:T(8,128)(2,1)S(1)}, bf16[2,128,1792]{2,1,0:T(8,128)(2,1)}, u32[]{:S(2)}) %copy-start.25) | copy-done | bytes 917528
  51.1 7.7 %near.1 = (f32[128,4096]{1,0:T(8,128)S(1)}, f32[128,4096]{1,0:T(8,128)S(1)}) custom-call(bf16[128,4096]{1,0:T(8,128)(2,1)S(1)} %copy-done.20, bf16[128,4096]{1,0:T(8,128)(2,1)S(1)} %copy-done.22, f32[16,4096]{1,0:T(8,128)S(1)} %copy-done.24, f32[1,4096]{1,0:T(1,128)S(1)} %copy-done.16, bf16[2,128,1792]{2,1,0:T(8,128)(2,1)S(1)} %copy-done.25), custom_call_target="tpu_custom_call" | custom-call | flops 3758096384 | bytes 7340032 | tf_op jit(solution)/shard_map/near/pallas_call | solution.py:343
  58.8 1.4 %copy-done.8 = f32[128,4096]{1,0:T(8,128)} copy-done((f32[128,4096]{1,0:T(8,128)}, f32[128,4096]{1,0:T(8,128)S(1)}, u32[]{:S(2)}) %copy-start.8) | copy-done | bytes 2097176
  60.1 1.4 %copy-done.10 = f32[128,4096]{1,0:T(8,128)} copy-done((f32[128,4096]{1,0:T(8,128)}, f32[128,4096]{1,0:T(8,128)S(1)}, u32[]{:S(2)}) %copy-start.10) | copy-done | bytes 2097176
  61.6 2.2 %copy-done.3 = f32[16,16,4096]{2,1,0:T(8,128)S(1)} copy-done((f32[16,16,4096]{2,1,0:T(8,128)S(1)}, f32[16,16,4096]{2,1,0:T(8,128)}, u32[]{:S(2)}) %copy-start.3) | copy-done | bytes 4194328
  63.8 1.6 %copy-done.9 = f32[128,4096]{1,0:T(8,128)S(1)} copy-done((f32[128,4096]{1,0:T(8,128)S(1)}, f32[128,4096]{1,0:T(8,128)}, u32[]{:S(2)}) %copy-start.9) | copy-done | bytes 2097176
  65.4 1.6 %copy-done.11 = f32[128,4096]{1,0:T(8,128)S(1)} copy-done((f32[128,4096]{1,0:T(8,128)S(1)}, f32[128,4096]{1,0:T(8,128)}, u32[]{:S(2)}) %copy-start.11) | copy-done | bytes 2097176
  67.0 12.3 %finish.1 = (bf16[128,4096]{1,0:T(8,128)(2,1)S(1)}, bf16[128,4096]{1,0:T(8,128)(2,1)S(1)}) custom-call(bf16[128,4096]{1,0:T(8,128)(2,1)S(1)} %bitcast.9, bf16[128,4096]{1,0:T(8,128)(2,1)S(1)} %bitcast.11, f32[128,4096]{1,0:T(8,128)S(1)} %copy-done.9, f32[128,4096]{1,0:T(8,128)S(1)} %copy-done.11, f32[16,16,4096]{2,1,0:T(8,128)S(1)} %copy-done.3, ...), custom_call_target="tpu_custom_call" | custom-call | tf_op jit(solution)/shard_map/finish/pallas_call | solution.py:372
  79.2 5.0 %collective-permute-start.2 = (bf16[128,4096]{1,0:T(8,128)(2,1)S(1)}, bf16[128,4096]{1,0:T(8,128)(2,1)S(1)}, u32[]{:S(2)}, u32[]{:S(2)}) collective-permute-start(bf16[128,4096]{1,0:T(8,128)(2,1)S(1)} %get-tuple-element.26), channel_id=1, source_target_pairs={{0,32},{32,64},{64,96},{96,128},{128,160},{160,192},{192,224},{224... | collective-permute-start | bytes 3145736 | tf_op jit(solution)/shard_map/ppermute | solution.py:273
  84.3 1.9 %collective-permute-start.3 = (bf16[128,4096]{1,0:T(8,128)(2,1)S(1)}, bf16[128,4096]{1,0:T(8,128)(2,1)S(1)}, u32[]{:S(2)}, u32[]{:S(2)}) collective-permute-start(bf16[128,4096]{1,0:T(8,128)(2,1)S(1)} %get-tuple-element.27), channel_id=1, source_target_pairs={{32,0},{64,32},{96,64},{128,96},{160,128},{192,160},{224,192},{256... | collective-permute-start | bytes 3145736 | tf_op jit(solution)/shard_map/ppermute | solution.py:273
  86.2 20.8 %collective-permute-done.2 = bf16[128,4096]{1,0:T(8,128)(2,1)S(1)} collective-permute-done((bf16[128,4096]{1,0:T(8,128)(2,1)S(1)}, bf16[128,4096]{1,0:T(8,128)(2,1)S(1)}, u32[]{:S(2)}, u32[]{:S(2)}) %collective-permute-start.2) | collective-permute-done | bytes 1048608 | tf_op jit(solution)/shard_map/ppermute | solution.py:273
  107.0 5.3 %collective-permute-done.3 = bf16[128,4096]{1,0:T(8,128)(2,1)S(1)} collective-permute-done((bf16[128,4096]{1,0:T(8,128)(2,1)S(1)}, bf16[128,4096]{1,0:T(8,128)(2,1)S(1)}, u32[]{:S(2)}, u32[]{:S(2)}) %collective-permute-start.3) | collective-permute-done | bytes 1048608 | tf_op jit(solution)/shard_map/ppermute | solution.py:273
  112.3 1.0 copy.16
  113.3 1.0 copy.17
  (42 shorter events, 3.9 us)
Async XLA Ops:
  1.5 10.1 %collective-permute-start = (bf16[2,4096]{1,0:T(2,128)(2,1)S(1)}, bf16[2,4096]{1,0:T(2,128)(2,1)S(1)}, u32[]{:S(2)}, u32[]{:S(2)}) collective-permute-start(bf16[2,4096]{1,0:T(2,128)(2,1)S(1)} %slice_bitcast_fusion), channel_id=1, source_target_pairs={{0,1},{1,2},{2,3},{3,4},{4,5},{5,6},{6,7},{7,8},{8,9},{9,10},{10,1... | collective-permute-start | bytes 49160 | tf_op jit(solution)/shard_map/ppermute | solution.py:273
  4.7 35.1 %copy-start.7 = (f32[1,16,4096]{2,1,0:T(8,128)S(1)}, f32[1,16,4096]{2,1,0:T(8,128)}, u32[]{:S(2)}) copy-start(f32[1,16,4096]{2,1,0:T(8,128)} %param.15) | copy-start | bytes 786436
  4.8 1.0 copy-start.6
  5.8 0.9 copy-start.12
  6.7 0.7 copy-start.18
  9.6 2.0 %copy-start.2 = (f32[16,16,4096]{2,1,0:T(8,128)}, f32[16,16,4096]{2,1,0:T(8,128)S(1)}, u32[]{:S(2)}) copy-start(f32[16,16,4096]{2,1,0:T(8,128)S(1)} %get-tuple-element.21.columns_ref) | copy-start | bytes 12582916
  11.6 29.1 %copy-start.23 = (f32[16,4096]{1,0:T(8,128)}, f32[16,4096]{1,0:T(8,128)S(1)}, u32[]{:S(2)}) copy-start(f32[16,4096]{1,0:T(8,128)S(1)} %get-tuple-element.18.nodal_ref) | copy-start | bytes 786436
  11.6 1.3 %copy-start = (bf16[1,128,4096]{2,1,0:T(8,128)(2,1)S(1)}, bf16[1,128,4096]{2,1,0:T(8,128)(2,1)}, u32[]{:S(2)}) copy-start(bf16[1,128,4096]{2,1,0:T(8,128)(2,1)} %param.11) | copy-start | bytes 3145732
  12.9 1.2 %copy-start.4 = (bf16[1,128,4096]{2,1,0:T(8,128)(2,1)S(1)}, bf16[1,128,4096]{2,1,0:T(8,128)(2,1)}, u32[]{:S(2)}) copy-start(bf16[1,128,4096]{2,1,0:T(8,128)(2,1)} %param.12) | copy-start | bytes 3145732
  14.1 0.7 copy-start.14
  14.8 0.7 copy-start.17
  15.6 30.9 %copy-start.16 = (f32[1,4096]{1,0:T(1,128)S(1)}, f32[1,4096]{1,0:T(1,128)}, u32[]{:S(2)}) copy-start(f32[1,4096]{1,0:T(1,128)} %skip_ref.3) | copy-start | bytes 49156
  22.3 1.0 copy-start.19
  23.3 1.0 copy-start.21
  24.3 15.6 %all-to-all-start = ((bf16[32,32,128]{2,1,0:T(8,128)(2,1)}), bf16[32,32,128]{2,1,0:T(8,128)(2,1)S(1)}, u32[]{:S(2)}, u32[]{:S(2)}) async-start(bf16[32,32,128]{2,1,0:T(8,128)(2,1)} %get-tuple-element.22.state_ref), calls=%async_computation | async-start | bytes 524288 | tf_op jit(solution)/shard_map/all_to_all | solution.py:340
  32.9 28.7 %collective-permute-start.1 = (f32[4,4096]{1,0:T(4,128)S(1)}, f32[4,4096]{1,0:T(4,128)S(1)}, u32[]{:S(2)}, u32[]{:S(2)}) collective-permute-start(f32[4,4096]{1,0:T(4,128)S(1)} %get-tuple-element.24), channel_id=1, source_target_pairs={{1,0},{2,1},{3,2},{4,3},{5,4},{6,5},{7,6},{8,7},{9,8},{10,9},{11,1... | collective-permute-start | bytes 196616 | tf_op jit(solution)/shard_map/ppermute | solution.py:273
  40.7 20.9 %all-to-all-start.1 = ((bf16[32,32,128]{2,1,0:T(8,128)(2,1)}), bf16[32,32,128]{2,1,0:T(8,128)(2,1)S(1)}, u32[]{:S(2)}, u32[]{:S(2)}) async-start(bf16[32,32,128]{2,1,0:T(8,128)(2,1)} %scan.1), calls=%async_computation.1 | async-start | bytes 524288 | tf_op jit(solution)/shard_map/all_to_all | solution.py:369
  46.5 1.2 %copy-start.20 = (bf16[128,4096]{1,0:T(8,128)(2,1)S(1)}, bf16[128,4096]{1,0:T(8,128)(2,1)}, u32[]{:S(2)}) copy-start(bf16[128,4096]{1,0:T(8,128)(2,1)} %copy-done.19) | copy-start | bytes 3145732
  47.7 1.2 %copy-start.22 = (bf16[128,4096]{1,0:T(8,128)(2,1)S(1)}, bf16[128,4096]{1,0:T(8,128)(2,1)}, u32[]{:S(2)}) copy-start(bf16[128,4096]{1,0:T(8,128)(2,1)} %copy-done.21) | copy-start | bytes 3145732
  49.0 0.9 copy-start.24
  49.9 1.2 %copy-start.25 = (bf16[2,128,1792]{2,1,0:T(8,128)(2,1)S(1)}, bf16[2,128,1792]{2,1,0:T(8,128)(2,1)}, u32[]{:S(2)}) copy-start(bf16[2,128,1792]{2,1,0:T(8,128)(2,1)} %constant.10.clone.near_ref) | copy-start | bytes 2752516
  51.1 10.4 %copy-start.1 = (bf16[1,128,4096]{2,1,0:T(8,128)(2,1)S(1)}, bf16[1,128,4096]{2,1,0:T(8,128)(2,1)}, u32[]{:S(2)}) copy-start(bf16[1,128,4096]{2,1,0:T(8,128)(2,1)} %param.11) | copy-start | bytes 3145732
  51.1 10.4 %copy-start.5 = (bf16[1,128,4096]{2,1,0:T(8,128)(2,1)S(1)}, bf16[1,128,4096]{2,1,0:T(8,128)(2,1)}, u32[]{:S(2)}) copy-start(bf16[1,128,4096]{2,1,0:T(8,128)(2,1)} %param.12) | copy-start | bytes 3145732
  51.1 10.5 %copy-start.13 = (bf16[256,48]{1,0:T(8,128)(2,1)S(1)}, bf16[256,48]{1,0:T(8,128)(2,1)}, u32[]{:S(2)}) copy-start(bf16[256,48]{1,0:T(8,128)(2,1)} %constant.11.clone.spread_ref) | copy-start | bytes 73732
  51.1 10.5 %copy-start.15 = (f32[1,4096]{1,0:T(1,128)S(1)}, f32[1,4096]{1,0:T(1,128)}, u32[]{:S(2)}) copy-start(f32[1,4096]{1,0:T(1,128)} %gain_ref.3) | copy-start | bytes 49156
  58.8 1.4 %copy-start.8 = (f32[128,4096]{1,0:T(8,128)}, f32[128,4096]{1,0:T(8,128)S(1)}, u32[]{:S(2)}) copy-start(f32[128,4096]{1,0:T(8,128)S(1)} %get-tuple-element.19.ahead_ref) | copy-start | bytes 6291460
  60.1 1.4 %copy-start.10 = (f32[128,4096]{1,0:T(8,128)}, f32[128,4096]{1,0:T(8,128)S(1)}, u32[]{:S(2)}) copy-start(f32[128,4096]{1,0:T(8,128)S(1)} %get-tuple-element.20.back_ref) | copy-start | bytes 6291460
  61.6 2.2 %copy-start.3 = (f32[16,16,4096]{2,1,0:T(8,128)S(1)}, f32[16,16,4096]{2,1,0:T(8,128)}, u32[]{:S(2)}) copy-start(f32[16,16,4096]{2,1,0:T(8,128)} %copy-done.2) | copy-start | bytes 12582916
  63.8 1.6 %copy-start.9 = (f32[128,4096]{1,0:T(8,128)S(1)}, f32[128,4096]{1,0:T(8,128)}, u32[]{:S(2)}) copy-start(f32[128,4096]{1,0:T(8,128)} %copy-done.8) | copy-start | bytes 6291460
  65.4 1.6 %copy-start.11 = (f32[128,4096]{1,0:T(8,128)S(1)}, f32[128,4096]{1,0:T(8,128)}, u32[]{:S(2)}) copy-start(f32[128,4096]{1,0:T(8,128)} %copy-done.10) | copy-start | bytes 6291460
  79.2 27.8 %collective-permute-start.2 = (bf16[128,4096]{1,0:T(8,128)(2,1)S(1)}, bf16[128,4096]{1,0:T(8,128)(2,1)S(1)}, u32[]{:S(2)}, u32[]{:S(2)}) collective-permute-start(bf16[128,4096]{1,0:T(8,128)(2,1)S(1)} %get-tuple-element.26), channel_id=1, source_target_pairs={{0,32},{32,64},{64,96},{96,128},{128,160},{160,192},{192,224},{224... | collective-permute-start | bytes 3145736 | tf_op jit(solution)/shard_map/ppermute | solution.py:273
  84.3 28.0 %collective-permute-start.3 = (bf16[128,4096]{1,0:T(8,128)(2,1)S(1)}, bf16[128,4096]{1,0:T(8,128)(2,1)S(1)}, u32[]{:S(2)}, u32[]{:S(2)}) collective-permute-start(bf16[128,4096]{1,0:T(8,128)(2,1)S(1)} %get-tuple-element.27), channel_id=1, source_target_pairs={{32,0},{64,32},{96,64},{128,96},{160,128},{192,160},{224,192},{256... | collective-permute-start | bytes 3145736 | tf_op jit(solution)/shard_map/ppermute | solution.py:273

commit v2 on v0

v2 whole, which is shorter than its diff:
```python
import functools

import jax
import jax.numpy as jnp
import ml_dtypes
import numpy as np
from jax import lax
from jax.experimental import pallas as pl
from jax.experimental.pallas import tpu as pltpu
from jax.sharding import PartitionSpec as P

MODES = 16
NODES = 14
PADDED = 16
LANES = 128
START_GROUP = 512
PIECES = 4
NEAR_STEP = 1024
NEAR_GROUP = 512
FINISH_GROUP = 256
F32 = jnp.float32
BF16 = jnp.bfloat16
shape = jax.ShapeDtypeStruct


def node_places(rows):
    k = np.arange(NODES)
    return 0.5 * (rows - 1) * (1.0 - np.cos((2 * k + 1) * np.pi / (2 * NODES)))


def cardinals(rows):
    nodes = node_places(rows)
    lags = np.arange(rows, dtype=np.float64)
    table = np.ones((rows, NODES))
    for k in range(NODES):
        for m in range(NODES):
            if m != k:
                table[:, k] *= (lags - nodes[m]) / (nodes[k] - nodes[m])
    return table


def halves(table):
    high = table.astype(ml_dtypes.bfloat16)
    low = (table - high.astype(np.float64)).astype(ml_dtypes.bfloat16)
    return high, low


def constants(rows):
    table = cardinals(rows)
    padded = np.zeros((rows, PADDED))
    padded[:, :NODES] = table
    high, low = halves(padded)
    flip_high, flip_low = high[::-1], low[::-1]
    moment_ahead = np.concatenate([flip_high.T, flip_low.T], axis=0)
    moment_back = np.concatenate([high.T, low.T], axis=0)
    spread_ahead = np.concatenate([high, low, high], axis=1)
    spread_back = np.concatenate([flip_high, flip_low, flip_high], axis=1)
    lag = np.arange(rows)[:, None] - np.arange(rows)[None, :]
    toeplitz = np.where(lag[:, :, None] >= 0, table[np.maximum(lag, 0)], 0.0)
    near_ahead = np.transpose(toeplitz, (0, 2, 1)).reshape(rows, NODES * rows)
    near_back = np.transpose(toeplitz, (1, 2, 0)).reshape(rows, NODES * rows)
    places = np.zeros((PADDED, LANES), np.float32)
    places[:NODES] = node_places(rows)[:, None]
    cast = ml_dtypes.bfloat16
    return dict(
        moments=np.concatenate([moment_ahead, moment_back], axis=0),
        spread=np.concatenate([spread_ahead, spread_back], axis=0),
        near=np.stack([near_ahead, near_back]).astype(cast),
        places=places,
    )


def coefs_of(rates, residue):
    return residue * jnp.sqrt(1.0 - jnp.exp(-2.0 * rates))


def nodal_sum(rates, weight, places):
    places = wide(places, rates.shape[1])
    total = jnp.exp(-rates[0:1] * places) * weight[0:1]
    for r in range(1, MODES):
        total = total + jnp.exp(-rates[r : r + 1] * places) * weight[r : r + 1]
    return total


def taps_of(taps_ref, cols):
    return [[taps_ref[j, i, :, cols] for i in range(3)] for j in range(3)]


def group_of(index, size=LANES):
    return pl.ds(pl.multiple_of(index * size, size), size)


def wide(block, width):
    return jnp.concatenate([block] * (width // LANES), axis=1)


def row_scale(block_sum, width):
    return lax.rsqrt(jnp.sum(block_sum, axis=1, keepdims=True) * (1.0 / width) + 1e-06)


def lane_sums(block):
    total = block[:, :LANES]
    for i in range(1, block.shape[1] // LANES):
        total = total + block[:, i * LANES : (i + 1) * LANES]
    return total


def filtered(taps, now, past, older):
    return [t[0] * now + t[1] * past + t[2] * older for t in taps]


def start_kernel(
    nodes, x_hbm, cot_hbm, gain_hbm, taps_hbm, rates_hbm, moments_ref,
    mixed_hbm, gate_hbm, state_ref, inverse_ref,
    x_ref, cot_ref, gain_ref, taps_ref, rates_ref, mixed_ref, gate_ref, normed_ref, moment_ref,
    x_sems, cot_sems, table_sems, mixed_sems, gate_sems,
):
    rows, width = x_ref.shape
    size = START_GROUP
    pieces = x_sems.shape[0]
    part = width // pieces

    def piece(p):
        return slice(None), pl.ds(p * part, part)

    x_copies = [pltpu.make_async_copy(x_hbm.at[piece(p)], x_ref.at[piece(p)], x_sems.at[p]) for p in range(pieces)]
    cot_copies = [
        pltpu.make_async_copy(cot_hbm.at[piece(p)], cot_ref.at[piece(p)], cot_sems.at[p]) for p in range(pieces)
    ]
    table_copies = [
        pltpu.make_async_copy(source, target, table_sems.at[n])
        for n, (source, target) in enumerate(((gain_hbm, gain_ref), (taps_hbm, taps_ref), (rates_hbm, rates_ref)))
    ]
    for copy in x_copies + table_copies + cot_copies:
        copy.start()

    normed_ref[0:8] = jnp.zeros((8, size), F32)
    total = jnp.zeros((rows, LANES), F32)
    for p in range(pieces):
        x_copies[p].wait()

        def square(i, total):
            x = x_ref[:, group_of(p * (part // size) + i, size)].astype(F32)
            return total + lane_sums(x * x)

        total = lax.fori_loop(0, part // size, square, total)
    inverse_ref[...] = jnp.broadcast_to(row_scale(total, width), (rows, LANES))
    for copy in table_copies:
        copy.wait()

    def group(i, carry):
        cols = group_of(i, size)
        now = x_ref[:, cols].astype(F32) * wide(inverse_ref[...], size) * gain_ref[:, cols]
        normed_ref[8 : rows + 8] = now
        past = normed_ref[7 : rows + 7]
        older = normed_ref[6 : rows + 6]
        query, key, value = filtered(taps_of(taps_ref, cols), now, past, older)
        kept = lax.broadcasted_iota(jnp.int32, (16, size), 0) >= 2
        for side, (signal, out_ref) in enumerate(
            ((key * value, mixed_ref), (cot_ref[:, cols].astype(F32) * query, gate_ref))
        ):
            head = jnp.where(kept, signal[0:16], 0.0)
            signal = jnp.concatenate([head, signal[16:]], axis=0).astype(BF16)
            out_ref[:, cols] = signal
            both = jnp.dot(moments_ref[32 * side : 32 * side + 32], signal, preferred_element_type=F32)
            moment_ref[PADDED * side : PADDED * (side + 1), cols] = both[:PADDED] + both[PADDED:]
        return carry

    def project(i, carry):
        cols = group_of(i)
        rates = rates_ref[:, cols]
        states = [0.0, 0.0]
        for k in range(NODES):
            power = jnp.exp(rates * (-nodes[k]))
            states = [
                states[side] + power * moment_ref[PADDED * side + k : PADDED * side + k + 1, cols]
                for side in range(2)
            ]
        for side in range(2):
            state_ref[MODES * side : MODES * (side + 1), cols] = states[side]
        return carry

    out_copies = []
    for p in range(pieces):
        cot_copies[p].wait()
        lax.fori_loop(p * (part // size), (p + 1) * (part // size), group, 0)
        out_copies += [
            pltpu.make_async_copy(mixed_ref.at[piece(p)], mixed_hbm.at[piece(p)], mixed_sems.at[p]),
            pltpu.make_async_copy(gate_ref.at[piece(p)], gate_hbm.at[piece(p)], gate_sems.at[p]),
        ]
        for copy in out_copies[-2:]:
            copy.start()
    lax.fori_loop(0, width // LANES, project, 0, unroll=2)
    for copy in out_copies:
        copy.wait()


def edge_kernel(
    x_ref, cot_ref, rim_ref, gain_ref, taps_ref, rates_ref, part_ref, inverse_ref,
    head_ref, state_ref, rim_scale_ref, front_ref, normed_ref, *, rows,
):
    width = x_ref.shape[1]
    rim = rim_ref[...].astype(F32)
    scale = row_scale(lane_sums(rim * rim), width)
    rim_scale_ref[0:2] = jnp.broadcast_to(scale, (2, LANES))
    front_ref[0:2] = x_ref[...].astype(F32)[0:2]
    front_ref[2:4] = cot_ref[...].astype(F32)[0:2]
    part = 4 * LANES

    def chunk(i, carry):
        cols = pl.ds(pl.multiple_of(i * part, part), part)
        gain = gain_ref[:, cols]
        now = x_ref[:, cols].astype(F32) * wide(inverse_ref[...], part) * gain
        normed_ref[8:24] = now
        normed_ref[6:8] = rim_ref[:, cols].astype(F32) * scale * gain
        taps = taps_of(taps_ref, cols)
        query, key, value = filtered(taps, now, normed_ref[7:23], normed_ref[6:22])
        mixed = (key * value).astype(BF16)
        gate = (cot_ref[:, cols].astype(F32) * query).astype(BF16)
        head_ref[0, :, cols] = mixed
        head_ref[1, :, cols] = gate
        rates = rates_ref[:, cols]
        mixed = mixed.astype(F32)
        gate = gate.astype(F32)
        ahead = (
            part_ref[0:MODES, cols]
            + jnp.exp(rates * (1.0 - rows)) * mixed[0:1]
            + jnp.exp(rates * (2.0 - rows)) * mixed[1:2]
        )
        back = part_ref[MODES : 2 * MODES, cols] + gate[0:1] + jnp.exp(-rates) * gate[1:2]
        for side, state in enumerate((ahead, back)):
            for h in range(part // LANES):
                state_ref[i * (part // LANES) + h, MODES * side : MODES * (side + 1)] = state[
                    :, h * LANES : (h + 1) * LANES
                ].astype(BF16)
        return carry

    lax.fori_loop(0, width // part, chunk, 0)


def near_kernel(
    signal_ref, head_ref, rates_ref, residue_ref, places_ref, skip_ref, near_ref, mark_ref, out_ref, done_ref, parts_ref
):
    rows = signal_ref.shape[0]
    done_ref[...] = jnp.zeros_like(done_ref)
    size = min(NEAR_GROUP, signal_ref.shape[1])

    def group(i, carry):
        cols = group_of(i, size)
        rates = rates_ref[:, cols]
        nodal = nodal_sum(rates, coefs_of(rates, residue_ref[:, cols]), places_ref[...]).astype(BF16)
        signal = jnp.concatenate([head_ref[0, :, cols], signal_ref[16:, cols]], axis=0)
        for k in range(NODES):
            parts_ref[k * rows : (k + 1) * rows] = signal * nodal[k : k + 1]
        out_ref[:, cols] = (
            jnp.dot(near_ref[0], parts_ref[...], preferred_element_type=F32)
            + skip_ref[:, cols] * signal.astype(F32)
        )
        return carry

    lax.fori_loop(0, signal_ref.shape[1] // size, group, 0)


def scan_kernel(rates_ref, state_ref, mark_ref, enter_ref, done_ref, *, rows):
    done_ref[...] = jnp.zeros_like(done_ref)
    count = state_ref.shape[0]
    first = lax.axis_index("seq") * LANES
    rates = rates_ref[:, pl.ds(pl.multiple_of(first, LANES), LANES)]
    decay = jnp.exp(rates * (-float(rows)))
    ahead = jnp.zeros((MODES, LANES), F32)
    back = jnp.zeros((MODES, LANES), F32)
    for d in range(count):
        enter_ref[d, 0:MODES] = ahead.astype(BF16)
        ahead = decay * ahead + state_ref[d, 0:MODES].astype(F32)
        e = count - 1 - d
        enter_ref[e, MODES : 2 * MODES] = back.astype(BF16)
        back = decay * back + state_ref[e, MODES : 2 * MODES].astype(F32)


def nodal_kernel_part(i, size, rates_ref, residue_ref, places_ref, enter_ref, nodal_ref):
    cols = group_of(i, size)
    pieces = size // LANES
    rates = rates_ref[:, cols]
    lead = coefs_of(rates, residue_ref[:, cols]) * jnp.exp(-rates)
    places = wide(places_ref[...], size)
    weights = []
    for side in range(2):
        entered = [enter_ref[i * pieces + h, MODES * side : MODES * (side + 1)].astype(F32) for h in range(pieces)]
        weights.append(lead * jnp.concatenate(entered, axis=1))
    nodals = [0.0, 0.0]
    for r in range(MODES):
        column = jnp.exp(-rates[r : r + 1] * places)
        nodals = [nodals[side] + column * weights[side][r : r + 1] for side in range(2)]
    for side in range(2):
        high = nodals[side].astype(BF16)
        low = (nodals[side] - high.astype(F32)).astype(BF16)
        nodal_ref[side, :, cols] = jnp.concatenate([high, high, low], axis=0)


def finish_kernel(
    rows, first, last, x_hbm, cot_hbm, ahead_hbm, back_hbm, rim_ref, rim_scale_ref, inverse_ref,
    gain_ref, taps_ref, spread_ref, *refs,
):
    if last:
        (places_ref, enter_ref, state_ref, residue_ref, rates_ref, skip_ref, front_ref) = refs[:7]
        refs = refs[7:]
        layer_hbm, grad_hbm, nodal_ref, after_ref = refs[:4]
        refs = refs[4:]
    else:
        nodal_ref, after_ref, layer_hbm, grad_hbm = refs[:4]
        refs = refs[4:]
    (
        x_ref, cot_ref, ahead_ref, back_ref, layer_ref, grad_ref, base_ref, normed_ref, one_ref, two_ref, total_ref,
        load_sems, layer_sems, grad_sems,
    ) = refs
    width = x_ref.shape[1]
    count = cot_ref.shape[0]
    size = min(FINISH_GROUP, width)
    pieces = layer_sems.shape[0]
    part = width // pieces
    top = 16 if first > 0 else 0

    def lanes(p):
        return pl.ds(p * part, part)

    loads = []
    for p in range(pieces):
        loads.append([
            pltpu.make_async_copy(source.at[pl.ds(lo, n), lanes(p)], target.at[:, lanes(p)], load_sems.at[k, p])
            for k, (source, target, lo, n) in enumerate((
                (x_hbm, x_ref, first - top, count + top),
                (cot_hbm, cot_ref, first, count),
                (ahead_hbm, ahead_ref, first, count),
                (back_hbm, back_ref, first, count),
            ))
        ])
        for copy in loads[p]:
            copy.start()

    total_ref[...] = jnp.zeros_like(total_ref)
    if last:
        def fill(i, carry):
            nodal_kernel_part(i, size, rates_ref, residue_ref, places_ref, enter_ref, nodal_ref)
            return carry

        lax.fori_loop(0, width // size, fill, 0)
        following = front_ref[0:2]
        after_scale = row_scale(lane_sums(following * following), width)

    inverse = wide(inverse_ref[first : first + count], size)

    def group(i, carry):
        cols = group_of(i, size)
        gain = gain_ref[:, cols]
        taps = taps_of(taps_ref, cols)
        x = x_ref[top:, cols].astype(F32)
        cot = cot_ref[:, cols].astype(F32)
        normed_ref[16 : count + 16] = x * inverse * gain
        if first > 0:
            above = x_ref[0:16, cols].astype(F32)
            normed_ref[0:16] = above * wide(inverse_ref[first - 16 : first], size) * gain
        else:
            normed_ref[14:16] = rim_ref[:, cols].astype(F32) * wide(rim_scale_ref[0:2], size) * gain
        now = normed_ref[16 : count + 16]
        past = normed_ref[15 : count + 15]
        older = normed_ref[14 : count + 14]
        query, key, value = filtered(taps, now, past, older)

        convs = []
        for side, near_ref in enumerate((ahead_ref, back_ref)):
            far = jnp.dot(
                spread_ref[side * rows + first : side * rows + first + count],
                nodal_ref[side, :, cols],
                preferred_element_type=F32,
            )
            convs.append((near_ref[:, cols] + far).astype(BF16).astype(F32))
        conv, conv_back = convs
        layer_ref[:, cols] = (x + query * conv).astype(BF16)

        grads = (cot * conv, conv_back * value, conv_back * key)
        lagged = [sum(taps[j][i] * grads[j] for j in range(3)) for i in range(3)]
        one_ref[0:count] = lagged[1]
        two_ref[0:count] = lagged[2]
        if last:
            normed_ref[count + 16 : count + 18] = front_ref[0:2, cols] * after_scale * gain
            n_query, n_key, n_value = filtered(
                taps,
                normed_ref[count + 16 : count + 18],
                normed_ref[count + 15 : count + 17],
                normed_ref[count + 14 : count + 16],
            )
            n_cot = front_ref[2:4, cols]
            n_mixed = (n_key * n_value).astype(BF16).astype(F32)
            n_gate = (n_cot * n_query).astype(BF16).astype(F32)
            rates = rates_ref[:, cols]
            coef = coefs_of(rates, residue_ref[:, cols])
            decay = jnp.exp(-rates)
            lead = coef * decay
            skip = skip_ref[:, cols]
            blocks = range(size // LANES)
            start = i * (size // LANES)
            entered = [
                jnp.concatenate(
                    [enter_ref[start + h, MODES * s : MODES * (s + 1)].astype(F32) for h in blocks], axis=1
                )
                for s in range(2)
            ]
            own = jnp.concatenate([state_ref[start + h, 0:MODES].astype(F32) for h in blocks], axis=1)
            leave = jnp.exp(rates * (-float(rows))) * entered[0] + own
            over = lambda a: jnp.sum(a, axis=0, keepdims=True)
            direct = over(coef) + skip
            mixed_0, mixed_1 = n_mixed[0:1], n_mixed[1:2]
            gate_0, gate_1 = n_gate[0:1], n_gate[1:2]
            conv_0 = over(lead * leave) + direct * mixed_0
            conv_1 = over(lead * decay * leave) + over(lead) * mixed_0 + direct * mixed_1
            back_0 = over(coef * entered[1]) + skip * gate_0
            back_1 = over(coef * (1.0 / decay) * (entered[1] - gate_0)) + skip * gate_1
            n_conv = jnp.concatenate([conv_0, conv_1], axis=0).astype(BF16).astype(F32)
            n_back = jnp.concatenate([back_0, back_1], axis=0).astype(BF16).astype(F32)
            n_grads = (n_cot * n_conv, n_back * n_value, n_back * n_key)
            one_ref[count : count + 2] = sum(taps[j][1] * n_grads[j] for j in range(3))
            two_ref[count : count + 2] = sum(taps[j][2] * n_grads[j] for j in range(3))
            after_ref[0:8, cols] = lagged[1][0:8]
            after_ref[8:16, cols] = lagged[2][0:8]
        else:
            one_ref[count : count + 8] = after_ref[0:8, cols]
            two_ref[count : count + 8] = after_ref[8:16, cols]
        scaled = gain * (lagged[0] + one_ref[1 : count + 1] + two_ref[2 : count + 2])
        base_ref[:, cols] = cot + inverse * scaled
        total_ref[...] = total_ref[...] + lane_sums(scaled * x)
        return carry

    outs = []
    for p in range(pieces):
        for copy in loads[p]:
            copy.wait()
        lax.fori_loop(p * (part // size), (p + 1) * (part // size), group, 0)
        outs.append(pltpu.make_async_copy(layer_ref.at[:, lanes(p)], layer_hbm.at[:, lanes(p)], layer_sems.at[p]))
        outs[-1].start()

    mean = jnp.sum(total_ref[...], axis=1, keepdims=True) * (1.0 / width)
    scale = inverse_ref[first : first + count]
    factor = wide(scale * scale * scale * jnp.broadcast_to(mean, (count, LANES)), size)

    def emit(i, carry):
        cols = group_of(i, size)
        grad_ref[:, cols] = (base_ref[:, cols] - x_ref[top:, cols].astype(F32) * factor).astype(BF16)
        return carry

    for p in range(pieces):
        lax.fori_loop(p * (part // size), (p + 1) * (part // size), emit, 0)
        outs.append(pltpu.make_async_copy(grad_ref.at[:, lanes(p)], grad_hbm.at[:, lanes(p)], grad_sems.at[p]))
        outs[-1].start()
    for copy in outs:
        copy.wait()


def join_kernel(first, layer_ref, grad_ref, *refs):
    layer_hbm, grad_hbm, sems = refs[-3:]
    count = layer_ref.shape[0]
    half = layer_ref.shape[1] // 2
    copies = []
    for n, (source, target) in enumerate(((layer_ref, layer_hbm), (grad_ref, grad_hbm))):
        for h in range(2):
            lanes = pl.ds(h * half, half)
            copies.append(
                pltpu.make_async_copy(source.at[:, lanes], target.at[pl.ds(first, count), lanes], sems.at[n, h])
            )
    for copy in copies:
        copy.start()
    for copy in copies:
        copy.wait()


def shifted(block, axis, distance):
    devices = range(lax.axis_size(axis))
    route = [(i - distance, i) for i in devices if i - distance in devices]
    return lax.ppermute(block, axis, route)


def whole(shape):
    return pl.BlockSpec(shape, lambda *i: (0,) * len(shape))


def across(shape, step, axis=None):
    axis = len(shape) - 1 if axis is None else axis
    block = shape[:axis] + (step,) + shape[axis + 1 :]
    return pl.BlockSpec(block, lambda i: (0,) * axis + (i,) + (0,) * (len(shape) - axis - 1))


def params(mib):
    return pltpu.CompilerParams(vmem_limit_bytes=mib << 20)


def stay(array):
    return pltpu.with_memory_space_constraint(array, pltpu.HBM)


def takes(micros):
    return pl.CostEstimate(
        flops=int(micros * 1.1e9), bytes_accessed=int(micros * 3.5e6), transcendentals=0
    )


def start_call(x, cot, gain, taps, rates, moments):
    rows, width = x.shape
    pieces = PIECES
    far = pl.BlockSpec(memory_space=pltpu.HBM)
    near = pl.BlockSpec(memory_space=pltpu.VMEM)
    return pl.pallas_call(
        functools.partial(start_kernel, [float(p) for p in node_places(rows)]),
        in_specs=[far, far, far, far, far, near],
        out_specs=[far, far, near, near],
        out_shape=[
            shape(x.shape, BF16), shape(x.shape, BF16), shape((2 * MODES, width), F32), shape((rows, LANES), F32),
        ],
        scratch_shapes=[
            pltpu.VMEM(x.shape, BF16),
            pltpu.VMEM(x.shape, BF16),
            pltpu.VMEM(gain.shape, F32),
            pltpu.VMEM(taps.shape, F32),
            pltpu.VMEM(rates.shape, F32),
            pltpu.VMEM(x.shape, BF16),
            pltpu.VMEM(x.shape, BF16),
            pltpu.VMEM((rows + 8, START_GROUP), F32),
            pltpu.VMEM((2 * PADDED, width), F32),
            pltpu.SemaphoreType.DMA((pieces,)),
            pltpu.SemaphoreType.DMA((pieces,)),
            pltpu.SemaphoreType.DMA((3,)),
            pltpu.SemaphoreType.DMA((pieces,)),
            pltpu.SemaphoreType.DMA((pieces,)),
        ],
        compiler_params=params(16),
        cost_estimate=takes(6),
        name="start",
    )(stay(x), stay(cot), stay(gain), stay(taps), stay(rates), moments)


def edge_call(x, cot, rim, gain, taps, rates, part, inverse):
    rows, width = x.shape
    return pl.pallas_call(
        functools.partial(edge_kernel, rows=rows),
        grid=(1,),
        in_specs=[
            whole((16, width)), whole((16, width)), whole(rim.shape), whole(gain.shape), whole(taps.shape),
            whole(rates.shape), whole(part.shape), whole((16, LANES)),
        ],
        out_specs=[
            whole((2, 16, width)), whole((width // LANES, 2 * MODES, LANES)), whole((8, LANES)), whole((4, width)),
        ],
        out_shape=[
            shape((2, 16, width), BF16),
            shape((width // LANES, 2 * MODES, LANES), BF16),
            shape((8, LANES), F32),
            shape((4, width), F32),
        ],
        scratch_shapes=[pltpu.VMEM((24, 4 * LANES), F32)],
        compiler_params=params(6),
        cost_estimate=takes(2),
        name="edge",
    )(x, cot, rim, gain, taps, rates, part, inverse)


def near_call(side, signal, head, rates, residue, places, skip, near, mark):
    rows, width = signal.shape
    step = min(NEAR_STEP, width)
    return pl.pallas_call(
        near_kernel,
        grid=(width // step,),
        in_specs=[
            across(signal.shape, step),
            pl.BlockSpec((1, 16, step), lambda i: (side, 0, i)),
            across(rates.shape, step), across(rates.shape, step), whole(places.shape),
            across(skip.shape, step),
            pl.BlockSpec((1,) + near.shape[1:], lambda i: (side, 0, 0)),
            whole(mark.shape),
        ],
        out_specs=[across(signal.shape, step), whole((8, LANES))],
        out_shape=[pltpu.HBM(signal.shape, F32), shape((8, LANES), F32)],
        scratch_shapes=[pltpu.VMEM((NODES * rows, min(NEAR_GROUP, width)), BF16)],
        compiler_params=params(16),
        cost_estimate=takes(4),
        name="near",
    )(stay(signal), head, rates, residue, places, skip, stay(near), mark)


def scan_call(rates, gathered, mark, rows):
    return pl.pallas_call(
        functools.partial(scan_kernel, rows=rows),
        out_shape=[shape(gathered.shape, BF16), shape((8, LANES), F32)],
        compiler_params=params(6),
        cost_estimate=takes(1),
        name="scan",
    )(rates, gathered, mark)


def finish_call(rows, first, last, tables, *arrays):
    x = arrays[0]
    width = x.shape[1]
    count = rows // 2
    pieces = PIECES
    size = min(FINISH_GROUP, width)
    top = 16 if first > 0 else 0
    far = pl.BlockSpec(memory_space=pltpu.HBM)
    near = pl.BlockSpec(memory_space=pltpu.VMEM)
    half = shape((count, width), BF16)
    out_specs = [far, far]
    out_shape = [half, half]
    if last:
        out_specs += [near, near]
        out_shape += [shape((2, 3 * PADDED, width), BF16), shape((16, width), F32)]
    return pl.pallas_call(
        functools.partial(finish_kernel, rows, first, last),
        in_specs=[far] * 4 + [near] * (len(arrays) - 4 + len(tables)),
        out_specs=out_specs,
        out_shape=out_shape,
        scratch_shapes=[
            pltpu.VMEM((count + top, width), BF16),
            pltpu.VMEM((count, width), BF16),
            pltpu.VMEM((count, width), F32),
            pltpu.VMEM((count, width), F32),
            pltpu.VMEM((count, width), BF16),
            pltpu.VMEM((count, width), BF16),
            pltpu.VMEM((count, width), F32),
            pltpu.VMEM((count + 24, size), F32),
            pltpu.VMEM((count + 8, size), F32),
            pltpu.VMEM((count + 8, size), F32),
            pltpu.VMEM((count, LANES), F32),
            pltpu.SemaphoreType.DMA((4, pieces)),
            pltpu.SemaphoreType.DMA((pieces,)),
            pltpu.SemaphoreType.DMA((pieces,)),
        ],
        compiler_params=params(24),
        cost_estimate=takes(6),
        name="finish",
    )(*[stay(array) for array in arrays[:4]], *arrays[4:], *tables)


def join_call(rows, first, layer, grad, *wholes):
    far = pl.BlockSpec(memory_space=pltpu.HBM)
    near = pl.BlockSpec(memory_space=pltpu.VMEM)
    out = shape((rows, layer.shape[1]), BF16)
    return pl.pallas_call(
        functools.partial(join_kernel, first),
        in_specs=[near, near] + [far] * len(wholes),
        out_specs=[far, far],
        out_shape=[out, out],
        scratch_shapes=[pltpu.SemaphoreType.DMA((2, 2))],
        input_output_aliases={2 + n: n for n in range(len(wholes))},
        compiler_params=params(4),
        cost_estimate=takes(1),
        name="join",
    )(layer, grad, *wholes)


def local(section_input, cotangent, norm_gain, short_filter, decay_rate, residue, skip_gain):
    x = section_input[0]
    cot = cotangent[0]
    rows = x.shape[0]
    taps = jnp.transpose(short_filter, (1, 2, 0, 3))
    rates = decay_rate[0]
    fixed = {name: jnp.asarray(table) for name, table in constants(rows).items()}

    rim = shifted(x[rows - 2 :], "seq", 1)
    weights = residue[0]
    mixed, gate, part, inverse = start_call(x, cot, norm_gain, taps, rates, fixed["moments"])
    head, state, rim_scale, front = edge_call(x, cot, rim, norm_gain, taps, rates, part, inverse)

    gathered = lax.all_to_all(state, "seq", split_axis=0, concat_axis=0, tiled=True)
    front = shifted(front, "seq", -1)
    near = (rates, weights, fixed["places"], skip_gain, fixed["near"])
    ahead, mark = near_call(0, mixed, head, *near, inverse[0:8])
    entering, mark = scan_call(rates, gathered, mark, rows)
    enter = lax.all_to_all(entering, "seq", split_axis=0, concat_axis=0, tiled=True)

    back, mark = near_call(1, gate, head, *near, mark)

    common = (x, cot, ahead, back, rim, rim_scale, inverse, norm_gain, taps, fixed["spread"])
    tables = (fixed["places"], enter, state, weights, rates, skip_gain, front)
    layer, grad, nodal, after = finish_call(rows, rows // 2, True, tables, *common)
    on_high = shifted(layer, "section", 1)
    back_high = shifted(grad, "section", -1)
    layer, grad = finish_call(rows, 0, False, (nodal, after), *common)
    on_low = shifted(layer, "section", 1)
    back_low = shifted(grad, "section", -1)
    joined = join_call(rows, rows // 2, on_high, back_high)
    passed_on, passed_back = join_call(rows, 0, on_low, back_low, *joined)
    return passed_on[None], passed_back[None]


def solution(mesh):
    in_specs = (
        P("section", "seq", None),
        P("section", "seq", None),
        P("section", None),
        P("section", None, None, None),
        P("section", None, None),
        P("section", None, None),
        P("section", None),
    )
    out_specs = (P("section", "seq", None), P("section", "seq", None))
    return jax.shard_map(local, mesh=mesh, in_specs=in_specs, out_specs=out_specs, check_vma=False)
```

time: 304 us -> 90.5 us (0.30)
  the two profiles are of different devices: /device:TPU:103 before, /device:TPU:96 now
where the time goes in v2:
time: 90.5 us; the launch traced here: 89.8 us
  Pallas kernels  37.3 us (41%)
  starting transfers between devices  32.5 us (36%)
  waiting for transfers between devices  17.4 us (19%)
  local copies, waits for them, and re-layouts  1.64 us (2%)
    ppermute x6, starting transfers between devices, shifted(): return lax.ppermute(block, axis, route)  17 us
    pallas_call x2, Pallas kernels, finish_call(): pl.pallas_call(functools.partial(finish_kernel, rows, first, last), in_sp...  13.6 us
    ppermute x6, waiting for transfers between devices, shifted(): return lax.ppermute(block, axis, route)  13.5 us
    pallas_call x2, Pallas kernels, near_call(): pl.pallas_call(near_kernel, grid=(width // step,), in_specs=[across(signa...  12.7 us
    all_to_all x1, starting transfers between devices, local(): lax.all_to_all(state, 'seq', split_axis=0, concat_axis=0, tiled=True)  8.49 us
    all_to_all x1, starting transfers between devices, local(): lax.all_to_all(entering, 'seq', split_axis=0, concat_axis=0, tiled=True)  7.01 us
    pallas_call x1, Pallas kernels, start_call(): pl.pallas_call(functools.partial(start_kernel, [float(p) for p in node_pl...  6.82 us
    all_to_all x1, waiting for transfers between devices, local(): lax.all_to_all(entering, 'seq', split_axis=0, concat_axis=0, tiled=True)  2.56 us
  transfers between devices with their start and end apart: 8, of which 5 were waited for; matrix products, arithmetic and copies ran while one was open for 0% of the time, Pallas kernels for 30%

profile of v2, /device:TPU:96, one launch (start us, length us, event | category | flops | bytes accessed | tf_op | source)
XLA Modules:
  0.0 89.8 jit_solution(13972613021114893996)
XLA Ops:
  0.6 0.9 slice_bitcast_fusion
  1.5 1.7 %collective-permute-start = (bf16[2,4096]{1,0:T(2,128)(2,1)S(1)}, bf16[2,4096]{1,0:T(2,128)(2,1)S(1)}, u32[]{:S(2)}, u32[]{:S(2)}) collective-permute-start(bf16[2,4096]{1,0:T(2,128)(2,1)S(1)} %slice_bitcast_fusion), channel_id=1, source_target_pairs={{0,1},{1,2},{2,3},{3,4},{4,5},{5,6},{6,7},{7,8},{8,9},{9,10},{10,1... | collective-permute-start | bytes 49160 | tf_op jit(solution)/shard_map/ppermute | solution.py:478
  3.2 0.0 copy-start.8
  3.3 0.7 copy-done.8
  4.0 0.0 copy-start.6
  4.0 6.8 %start.1 = (bf16[128,4096]{1,0:T(8,128)(2,1)S(1)}, bf16[128,4096]{1,0:T(8,128)(2,1)S(1)}, f32[32,4096]{1,0:T(8,128)S(1)}, f32[128,128]{1,0:T(8,128)S(1)}) custom-call(bf16[128,4096]{1,0:T(8,128)(2,1)} %bitcast.9, bf16[128,4096]{1,0:T(8,128)(2,1)} %bitcast.13, f32[1,4096]{1,0:T(1,128)} %gain_ref.5, f32[3,3,1,4096]{3,2,1,0:T(1,128)} %bitcast.26, ...), custom_call_target="tpu_custom_call" | custom-call | flops 6600000000 | bytes 21000000 | tf_op jit(solution)/shard_map/start/pallas_call | solution.py:510
  10.8 0.0 copy-start.10
  10.8 0.0 copy-start.11
  10.9 0.0 copy-start.3
  10.9 0.0 copy-start.5
  10.9 0.0 copy-start.9
  10.9 1.5 %edge.1 = (bf16[2,16,4096]{2,1,0:T(8,128)(2,1)S(1)}, bf16[32,32,128]{2,1,0:T(8,128)(2,1)}, f32[8,128]{1,0:T(8,128)S(1)}, f32[4,4096]{1,0:T(4,128)S(1)}) custom-call(bf16[128,4096]{1,0:T(8,128)(2,1)S(1)} %bitcast.12, bf16[128,4096]{1,0:T(8,128)(2,1)S(1)} %bitcast.16, bf16[2,4096]{1,0:T(2,128)(2,1)S(1)} %collective-permute-done.rim_ref, ...), custom_call_target="tpu_custom_call" | custom-call | flops 2200000000 | bytes 7000000 | tf_op jit(solution)/shard_map/edge/pallas_call | solution.py:541
  12.4 8.5 %all-to-all-start = ((bf16[32,32,128]{2,1,0:T(8,128)(2,1)}), bf16[32,32,128]{2,1,0:T(8,128)(2,1)S(1)}, u32[]{:S(2)}, u32[]{:S(2)}) async-start(bf16[32,32,128]{2,1,0:T(8,128)(2,1)} %get-tuple-element.31.refs_2_), calls=%async_computation | async-start | bytes 524288 | tf_op jit(solution)/shard_map/all_to_all | solution.py:669
  20.9 1.3 %collective-permute-start.1 = (f32[4,4096]{1,0:T(4,128)S(1)}, f32[4,4096]{1,0:T(4,128)S(1)}, u32[]{:S(2)}, u32[]{:S(2)}) collective-permute-start(f32[4,4096]{1,0:T(4,128)S(1)} %get-tuple-element.37), channel_id=1, source_target_pairs={{1,0},{2,1},{3,2},{4,3},{5,4},{6,5},{7,6},{8,7},{9,8},{10,9},{11,1... | collective-permute-start | bytes 196616 | tf_op jit(solution)/shard_map/ppermute | solution.py:478
  22.3 6.3 %near.2 = (f32[128,4096]{1,0:T(8,128)}, f32[8,128]{1,0:T(8,128)S(1)}) custom-call(bf16[128,4096]{1,0:T(8,128)(2,1)} %copy-done.11, bf16[2,16,4096]{2,1,0:T(8,128)(2,1)S(1)} %get-tuple-element.28.head_ref, f32[16,4096]{1,0:T(8,128)S(1)} %bitcast.19, f32[16,4096]{1,0:T(8,128)S(1)} %bitcast.23, f32[16,128]{1,0:T(8,128)S(1)} %copy-done.9, ...), custom_call_target="tpu_custom_call" | custom-call | flops 4400000000 | bytes 14000000 | tf_op jit(solution)/shard_map/near/pallas_call | solution.py:567
  28.6 1.3 %all-to-all-done.state_ref = bf16[32,32,128]{2,1,0:T(8,128)(2,1)S(1)} async-done(((bf16[32,32,128]{2,1,0:T(8,128)(2,1)}), bf16[32,32,128]{2,1,0:T(8,128)(2,1)S(1)}, u32[]{:S(2)}, u32[]{:S(2)}) %all-to-all-start) | async-done | bytes 262176 | tf_op jit(solution)/shard_map/all_to_all | solution.py:669
  29.9 0.8 scan.1
  30.7 7.0 %all-to-all-start.1 = ((bf16[32,32,128]{2,1,0:T(8,128)(2,1)}), bf16[32,32,128]{2,1,0:T(8,128)(2,1)S(1)}, u32[]{:S(2)}, u32[]{:S(2)}) async-start(bf16[32,32,128]{2,1,0:T(8,128)(2,1)} %get-tuple-element.36), calls=%async_computation.1 | async-start | bytes 524288 | tf_op jit(solution)/shard_map/all_to_all | solution.py:674
  37.7 0.0 copy-start.7
  37.7 6.4 %near.3 = (f32[128,4096]{1,0:T(8,128)}, f32[8,128]{1,0:T(8,128)}) custom-call(bf16[128,4096]{1,0:T(8,128)(2,1)} %copy-done.10, bf16[2,16,4096]{2,1,0:T(8,128)(2,1)S(1)} %get-tuple-element.28.head_ref, f32[16,4096]{1,0:T(8,128)S(1)} %bitcast.21, f32[16,4096]{1,0:T(8,128)S(1)} %bitcast.24, f32[16,128]{1,0:T(8,128)S(1)} %copy-done.9, f32[1,4096]{1,0:T(1,128)S(1)} %copy-done.5, ...), custom_call_target="tpu_custom_call" | custom-call | flops 4400000000 | bytes 14000000 | tf_op jit(solution)/shard_map/near/pallas_call | solution.py:567
  44.1 2.6 %all-to-all-done.1.refs_1_ = bf16[32,32,128]{2,1,0:T(8,128)(2,1)S(1)} async-done(((bf16[32,32,128]{2,1,0:T(8,128)(2,1)}), bf16[32,32,128]{2,1,0:T(8,128)(2,1)S(1)}, u32[]{:S(2)}, u32[]{:S(2)}) %all-to-all-start.1) | async-done | bytes 262176 | tf_op jit(solution)/shard_map/all_to_all | solution.py:674
  46.6 7.9 %finish.2 = (bf16[64,4096]{1,0:T(8,128)(2,1)S(1)}, bf16[64,4096]{1,0:T(8,128)(2,1)S(1)}, bf16[2,48,4096]{2,1,0:T(8,128)(2,1)S(1)}, f32[16,4096]{1,0:T(8,128)S(1)}) custom-call(bf16[128,4096]{1,0:T(8,128)(2,1)} %bitcast.10, bf16[128,4096]{1,0:T(8,128)(2,1)} %bitcast.14, f32[128,4096]{1,0:T(8,128)} %get-tuple-element.29.ahead_hbm, ...), custom_call_target="tpu_custom_call" | custom-call | flops 6600000000 | bytes 21000000 | tf_op jit(solution)/shard_map/finish/pallas_call | solution.py:612
  54.6 5.0 %collective-permute-start.4 = (bf16[64,4096]{1,0:T(8,128)(2,1)S(1)}, bf16[64,4096]{1,0:T(8,128)(2,1)S(1)}, u32[]{:S(2)}, u32[]{:S(2)}) collective-permute-start(bf16[64,4096]{1,0:T(8,128)(2,1)S(1)} %get-tuple-element.42), channel_id=1, source_target_pairs={{0,32},{32,64},{64,96},{96,128},{128,160},{160,192},{192,224},{224... | collective-permute-start | bytes 1572872 | tf_op jit(solution)/shard_map/ppermute | solution.py:478
  59.6 1.9 %collective-permute-start.5 = (bf16[64,4096]{1,0:T(8,128)(2,1)S(1)}, bf16[64,4096]{1,0:T(8,128)(2,1)S(1)}, u32[]{:S(2)}, u32[]{:S(2)}) collective-permute-start(bf16[64,4096]{1,0:T(8,128)(2,1)S(1)} %get-tuple-element.43), channel_id=1, source_target_pairs={{32,0},{64,32},{96,64},{128,96},{160,128},{192,160},{224,192},{256... | collective-permute-start | bytes 1572872 | tf_op jit(solution)/shard_map/ppermute | solution.py:478
  61.5 5.7 %finish.3 = (bf16[64,4096]{1,0:T(8,128)(2,1)S(1)}, bf16[64,4096]{1,0:T(8,128)(2,1)S(1)}) custom-call(bf16[128,4096]{1,0:T(8,128)(2,1)} %bitcast.11, bf16[128,4096]{1,0:T(8,128)(2,1)} %bitcast.15, f32[128,4096]{1,0:T(8,128)} %get-tuple-element.29.ahead_hbm, f32[128,4096]{1,0:T(8,128)} %get-tuple-element.34.back_hbm, ...), custom_call_target="tpu_custom_call" | custom-call | flops 6600000000 | bytes 21000000 | tf_op jit(solution)/shard_map/finish/pallas_call | solution.py:612
  67.2 5.1 %collective-permute-start.2 = (bf16[64,4096]{1,0:T(8,128)(2,1)S(1)}, bf16[64,4096]{1,0:T(8,128)(2,1)S(1)}, u32[]{:S(2)}, u32[]{:S(2)}) collective-permute-start(bf16[64,4096]{1,0:T(8,128)(2,1)S(1)} %get-tuple-element.40), channel_id=1, source_target_pairs={{0,32},{32,64},{64,96},{96,128},{128,160},{160,192},{192,224},{224... | collective-permute-start | bytes 1572872 | tf_op jit(solution)/shard_map/ppermute | solution.py:478
  72.4 1.9 %collective-permute-start.3 = (bf16[64,4096]{1,0:T(8,128)(2,1)S(1)}, bf16[64,4096]{1,0:T(8,128)(2,1)S(1)}, u32[]{:S(2)}, u32[]{:S(2)}) collective-permute-start(bf16[64,4096]{1,0:T(8,128)(2,1)S(1)} %get-tuple-element.41), channel_id=1, source_target_pairs={{32,0},{64,32},{96,64},{128,96},{160,128},{192,160},{224,192},{256... | collective-permute-start | bytes 1572872 | tf_op jit(solution)/shard_map/ppermute | solution.py:478
  74.3 2.3 %collective-permute-done.5.grad_ref = bf16[64,4096]{1,0:T(8,128)(2,1)S(1)} collective-permute-done((bf16[64,4096]{1,0:T(8,128)(2,1)S(1)}, bf16[64,4096]{1,0:T(8,128)(2,1)S(1)}, u32[]{:S(2)}, u32[]{:S(2)}) %collective-permute-start.5) | collective-permute-done | bytes 524320 | tf_op jit(solution)/shard_map/ppermute | solution.py:478
  76.6 1.0 %join.2 = (bf16[128,4096]{1,0:T(8,128)(2,1)}, bf16[128,4096]{1,0:T(8,128)(2,1)}) custom-call(bf16[64,4096]{1,0:T(8,128)(2,1)S(1)} %collective-permute-done.4.layer_ref, bf16[64,4096]{1,0:T(8,128)(2,1)S(1)} %collective-permute-done.5.grad_ref), custom_call_target="tpu_custom_call" | custom-call | flops 1100000000 | bytes 3500000 | tf_op jit(solution)/shard_map/join/pallas_call | solution.py:643
  77.6 5.9 %collective-permute-done.2.layer_ref = bf16[64,4096]{1,0:T(8,128)(2,1)S(1)} collective-permute-done((bf16[64,4096]{1,0:T(8,128)(2,1)S(1)}, bf16[64,4096]{1,0:T(8,128)(2,1)S(1)}, u32[]{:S(2)}, u32[]{:S(2)}) %collective-permute-start.2) | collective-permute-done | bytes 524320 | tf_op jit(solution)/shard_map/ppermute | solution.py:478
  83.4 5.3 %collective-permute-done.3.grad_ref = bf16[64,4096]{1,0:T(8,128)(2,1)S(1)} collective-permute-done((bf16[64,4096]{1,0:T(8,128)(2,1)S(1)}, bf16[64,4096]{1,0:T(8,128)(2,1)S(1)}, u32[]{:S(2)}, u32[]{:S(2)}) %collective-permute-start.3) | collective-permute-done | bytes 524320 | tf_op jit(solution)/shard_map/ppermute | solution.py:478
  88.8 1.0 %join.3 = (bf16[128,4096]{1,0:T(8,128)(2,1)}, bf16[128,4096]{1,0:T(8,128)(2,1)}) custom-call(bf16[64,4096]{1,0:T(8,128)(2,1)S(1)} %collective-permute-done.2.layer_ref, bf16[64,4096]{1,0:T(8,128)(2,1)S(1)} %collective-permute-done.3.grad_ref, bf16[128,4096]{1,0:T(8,128)(2,1)} %get-tuple-element.44.refs_0_, ...), custom_call_target="tpu_custom_call", output_to_operand_aliasing={{0}: (2, {}), {1}: (3, {})} | custom-call | flops 1100000000 | bytes 3500000 | tf_op jit(solution)/shard_map/join/pallas_call | solution.py:643
  (19 shorter events, 0.0 us)
Async XLA Ops:
  1.5 9.4 %collective-permute-start = (bf16[2,4096]{1,0:T(2,128)(2,1)S(1)}, bf16[2,4096]{1,0:T(2,128)(2,1)S(1)}, u32[]{:S(2)}, u32[]{:S(2)}) collective-permute-start(bf16[2,4096]{1,0:T(2,128)(2,1)S(1)} %slice_bitcast_fusion), channel_id=1, source_target_pairs={{0,1},{1,2},{2,3},{3,4},{4,5},{5,6},{6,7},{7,8},{8,9},{9,10},{10,1... | collective-permute-start | bytes 49160 | tf_op jit(solution)/shard_map/ppermute | solution.py:478
  3.2 0.7 copy-start.8
  4.0 6.9 %copy-start = (bf16[1,128,4096]{2,1,0:T(8,128)(2,1)S(1)}, bf16[1,128,4096]{2,1,0:T(8,128)(2,1)}, u32[]{:S(2)}) copy-start(bf16[1,128,4096]{2,1,0:T(8,128)(2,1)} %param.11) | copy-start | bytes 3145732
  4.0 6.9 %copy-start.1 = (bf16[1,128,4096]{2,1,0:T(8,128)(2,1)S(1)}, bf16[1,128,4096]{2,1,0:T(8,128)(2,1)}, u32[]{:S(2)}) copy-start(bf16[1,128,4096]{2,1,0:T(8,128)(2,1)} %param.12) | copy-start | bytes 3145732
  4.0 6.9 %copy-start.2 = (f32[1,16,4096]{2,1,0:T(8,128)S(1)}, f32[1,16,4096]{2,1,0:T(8,128)}, u32[]{:S(2)}) copy-start(f32[1,16,4096]{2,1,0:T(8,128)} %param.15) | copy-start | bytes 786436
  4.0 6.9 %copy-start.4 = (f32[1,3,3,4096]{3,0,2,1:T(1,128)S(1)}, f32[1,3,3,4096]{3,0,2,1:T(1,128)}, u32[]{:S(2)}) copy-start(f32[1,3,3,4096]{3,0,2,1:T(1,128)} %param.14) | copy-start | bytes 442372
  4.0 6.9 %copy-start.6 = (f32[1,4096]{1,0:T(1,128)S(1)}, f32[1,4096]{1,0:T(1,128)}, u32[]{:S(2)}) copy-start(f32[1,4096]{1,0:T(1,128)} %gain_ref.5) | copy-start | bytes 49156
  10.8 1.6 %copy-start.10 = (bf16[128,4096]{1,0:T(8,128)(2,1)}, bf16[128,4096]{1,0:T(8,128)(2,1)S(1)}, u32[]{:S(2)}) copy-start(bf16[128,4096]{1,0:T(8,128)(2,1)S(1)} %get-tuple-element.30.signal_ref) | copy-start | bytes 3145732
  10.8 1.6 %copy-start.11 = (bf16[128,4096]{1,0:T(8,128)(2,1)}, bf16[128,4096]{1,0:T(8,128)(2,1)S(1)}, u32[]{:S(2)}) copy-start(bf16[128,4096]{1,0:T(8,128)(2,1)S(1)} %get-tuple-element.25.signal_ref) | copy-start | bytes 3145732
  10.9 11.3 %copy-start.3 = (f32[1,16,4096]{2,1,0:T(8,128)S(1)}, f32[1,16,4096]{2,1,0:T(8,128)}, u32[]{:S(2)}) copy-start(f32[1,16,4096]{2,1,0:T(8,128)} %param.16) | copy-start | bytes 786436
  10.9 11.3 %copy-start.5 = (f32[1,4096]{1,0:T(1,128)S(1)}, f32[1,4096]{1,0:T(1,128)}, u32[]{:S(2)}) copy-start(f32[1,4096]{1,0:T(1,128)} %refs_5_.1) | copy-start | bytes 49156
  10.9 11.3 %copy-start.9 = (f32[16,128]{1,0:T(8,128)S(1)}, f32[16,128]{1,0:T(8,128)}, u32[]{:S(2)}) copy-start(f32[16,128]{1,0:T(8,128)} %constant.11.clone.places_ref.refs_0_) | copy-start | bytes 24580
  12.4 17.4 %all-to-all-start = ((bf16[32,32,128]{2,1,0:T(8,128)(2,1)}), bf16[32,32,128]{2,1,0:T(8,128)(2,1)S(1)}, u32[]{:S(2)}, u32[]{:S(2)}) async-start(bf16[32,32,128]{2,1,0:T(8,128)(2,1)} %get-tuple-element.31.refs_2_), calls=%async_computation | async-start | bytes 524288 | tf_op jit(solution)/shard_map/all_to_all | solution.py:669
  20.9 23.1 %collective-permute-start.1 = (f32[4,4096]{1,0:T(4,128)S(1)}, f32[4,4096]{1,0:T(4,128)S(1)}, u32[]{:S(2)}, u32[]{:S(2)}) collective-permute-start(f32[4,4096]{1,0:T(4,128)S(1)} %get-tuple-element.37), channel_id=1, source_target_pairs={{1,0},{2,1},{3,2},{4,3},{5,4},{6,5},{7,6},{8,7},{9,8},{10,9},{11,1... | collective-permute-start | bytes 196616 | tf_op jit(solution)/shard_map/ppermute | solution.py:478
  30.7 16.0 %all-to-all-start.1 = ((bf16[32,32,128]{2,1,0:T(8,128)(2,1)}), bf16[32,32,128]{2,1,0:T(8,128)(2,1)S(1)}, u32[]{:S(2)}, u32[]{:S(2)}) async-start(bf16[32,32,128]{2,1,0:T(8,128)(2,1)} %get-tuple-element.36), calls=%async_computation.1 | async-start | bytes 524288 | tf_op jit(solution)/shard_map/all_to_all | solution.py:674
  37.7 8.9 %copy-start.7 = (bf16[256,48]{1,0:T(8,128)(2,1)S(1)}, bf16[256,48]{1,0:T(8,128)(2,1)}, u32[]{:S(2)}) copy-start(bf16[256,48]{1,0:T(8,128)(2,1)} %constant.9.clone.spread_ref) | copy-start | bytes 73732
  54.6 19.7 %collective-permute-start.4 = (bf16[64,4096]{1,0:T(8,128)(2,1)S(1)}, bf16[64,4096]{1,0:T(8,128)(2,1)S(1)}, u32[]{:S(2)}, u32[]{:S(2)}) collective-permute-start(bf16[64,4096]{1,0:T(8,128)(2,1)S(1)} %get-tuple-element.42), channel_id=1, source_target_pairs={{0,32},{32,64},{64,96},{96,128},{128,160},{160,192},{192,224},{224... | collective-permute-start | bytes 1572872 | tf_op jit(solution)/shard_map/ppermute | solution.py:478
  59.6 17.0 %collective-permute-start.5 = (bf16[64,4096]{1,0:T(8,128)(2,1)S(1)}, bf16[64,4096]{1,0:T(8,128)(2,1)S(1)}, u32[]{:S(2)}, u32[]{:S(2)}) collective-permute-start(bf16[64,4096]{1,0:T(8,128)(2,1)S(1)} %get-tuple-element.43), channel_id=1, source_target_pairs={{32,0},{64,32},{96,64},{128,96},{160,128},{192,160},{224,192},{256... | collective-permute-start | bytes 1572872 | tf_op jit(solution)/shard_map/ppermute | solution.py:478
  67.2 16.2 %collective-permute-start.2 = (bf16[64,4096]{1,0:T(8,128)(2,1)S(1)}, bf16[64,4096]{1,0:T(8,128)(2,1)S(1)}, u32[]{:S(2)}, u32[]{:S(2)}) collective-permute-start(bf16[64,4096]{1,0:T(8,128)(2,1)S(1)} %get-tuple-element.40), channel_id=1, source_target_pairs={{0,32},{32,64},{64,96},{96,128},{128,160},{160,192},{192,224},{224... | collective-permute-start | bytes 1572872 | tf_op jit(solution)/shard_map/ppermute | solution.py:478
  72.4 16.4 %collective-permute-start.3 = (bf16[64,4096]{1,0:T(8,128)(2,1)S(1)}, bf16[64,4096]{1,0:T(8,128)(2,1)S(1)}, u32[]{:S(2)}, u32[]{:S(2)}) collective-permute-start(bf16[64,4096]{1,0:T(8,128)(2,1)S(1)} %get-tuple-element.41), channel_id=1, source_target_pairs={{32,0},{64,32},{96,64},{128,96},{160,128},{192,160},{224,192},{256... | collective-permute-start | bytes 1572872 | tf_op jit(solution)/shard_map/ppermute | solution.py:478

commit v3 on v2

v3 whole, which is shorter than its diff:
```python
import functools

import jax
import jax.numpy as jnp
import ml_dtypes
import numpy as np
from jax import lax
from jax.experimental import pallas as pl
from jax.experimental.pallas import tpu as pltpu
from jax.sharding import PartitionSpec as P

MODES = 16
NODES = 14
PADDED = 16
PACKET = 40
EXTRA = 32
LANES = 128
START_GROUP = 1024
PIECES = 4
SPLIT = 80
NEAR_STEP = 1024
NEAR_GROUP = 1024
FINISH_GROUP = 128
FINISH_TOGETHER = 8
FILL_GROUP = 512
F32 = jnp.float32
BF16 = jnp.bfloat16
shape = jax.ShapeDtypeStruct


def node_places(rows):
    k = np.arange(NODES)
    return 0.5 * (rows - 1) * (1.0 - np.cos((2 * k + 1) * np.pi / (2 * NODES)))


def cardinals(rows):
    nodes = node_places(rows)
    lags = np.arange(rows, dtype=np.float64)
    table = np.ones((rows, NODES))
    for k in range(NODES):
        for m in range(NODES):
            if m != k:
                table[:, k] *= (lags - nodes[m]) / (nodes[k] - nodes[m])
    return table


def halves(table):
    high = table.astype(ml_dtypes.bfloat16)
    low = (table - high.astype(np.float64)).astype(ml_dtypes.bfloat16)
    return high, low


def constants(rows):
    table = cardinals(rows)
    padded = np.zeros((rows, PADDED))
    padded[:, :NODES] = table
    high, low = halves(padded)
    flip_high, flip_low = high[::-1], low[::-1]
    moment_ahead = np.concatenate([flip_high.T, flip_low.T], axis=0)
    moment_back = np.concatenate([high.T, low.T], axis=0)
    spread_ahead = np.concatenate([high, low, high], axis=1)
    spread_back = np.concatenate([flip_high, flip_low, flip_high], axis=1)
    lag = np.arange(rows)[:, None] - np.arange(rows)[None, :]
    toeplitz = np.where(lag[:, :, None] >= 0, table[np.maximum(lag, 0)], 0.0)
    near_ahead = np.transpose(toeplitz, (0, 2, 1)).reshape(rows, NODES * rows)
    near_back = np.transpose(toeplitz, (1, 2, 0)).reshape(rows, NODES * rows)
    places = np.zeros((PADDED, LANES), np.float32)
    places[:NODES] = node_places(rows)[:, None]
    cast = ml_dtypes.bfloat16
    return dict(
        moments=np.concatenate(
            [
                np.concatenate([moment_ahead, np.zeros_like(moment_ahead)], axis=1),
                np.concatenate([np.zeros_like(moment_back), moment_back], axis=1),
            ],
            axis=0,
        ),
        spread=np.concatenate([spread_ahead, spread_back], axis=0),
        near=np.stack([near_ahead, near_back]).astype(cast),
        places=places,
    )


def coefs_of(rates, residue):
    return residue * jnp.sqrt(1.0 - jnp.exp(-2.0 * rates))


def nodal_sum(rates, weight, places):
    places = wide(places, rates.shape[1])
    total = jnp.exp(-rates[0:1] * places) * weight[0:1]
    for r in range(1, MODES):
        total = total + jnp.exp(-rates[r : r + 1] * places) * weight[r : r + 1]
    return total


def taps_of(taps_ref, gain_ref, cols):
    gain = gain_ref[:, cols]
    return [[taps_ref[j, i, :, cols] * gain for i in range(3)] for j in range(3)]


def group_of(index, size=LANES):
    return pl.ds(pl.multiple_of(index * size, size), size)


def wide(block, width):
    return jnp.concatenate([block] * (width // LANES), axis=1)


def row_scale(block_sum, width):
    return lax.rsqrt(jnp.sum(block_sum, axis=1, keepdims=True) * (1.0 / width) + 1e-06)


def lane_sums(block):
    total = block[:, :LANES]
    for i in range(1, block.shape[1] // LANES):
        total = total + block[:, i * LANES : (i + 1) * LANES]
    return total


def filtered(taps, now, past, older):
    return [t[0] * now + t[1] * past + t[2] * older for t in taps]


def start_kernel(
    nodes, x_hbm, cot_hbm, gain_hbm, taps_hbm, rates_hbm, moments_hbm,
    mixed_hbm, gate_hbm, packet_hbm, state_hbm, inverse_hbm,
    x_ref, cot_ref, gain_ref, taps_ref, rates_ref, moments_ref, mixed_ref, gate_ref, packet_ref, state_ref, inverse_ref,
    normed_ref, moment_ref, x_sems, cot_sems, table_sems, mixed_sems, gate_sems, last_sems,
):
    rows, width = x_ref.shape
    size = normed_ref.shape[1]
    pieces = x_sems.shape[0]
    part = width // pieces

    def piece(p):
        return slice(None), pl.ds(p * part, part)

    x_copies = [pltpu.make_async_copy(x_hbm.at[piece(p)], x_ref.at[piece(p)], x_sems.at[p]) for p in range(pieces)]
    cot_copies = [
        pltpu.make_async_copy(cot_hbm.at[piece(p)], cot_ref.at[piece(p)], cot_sems.at[p]) for p in range(pieces)
    ]
    table_copies = [
        pltpu.make_async_copy(source, target, table_sems.at[n])
        for n, (source, target) in enumerate(
            ((gain_hbm, gain_ref), (taps_hbm, taps_ref), (moments_hbm, moments_ref), (rates_hbm, rates_ref))
        )
    ]
    for copy in x_copies + table_copies + cot_copies:
        copy.start()

    normed_ref[0:8] = jnp.zeros((8, size), F32)
    total = jnp.zeros((rows, LANES), F32)
    for p in range(pieces):
        x_copies[p].wait()

        def square(i, total):
            x = x_ref[:, group_of(p * (part // size) + i, size)].astype(F32)
            return total + lane_sums(x * x)

        total = lax.fori_loop(0, part // size, square, total)
    inverse_ref[...] = jnp.broadcast_to(row_scale(total, width), (rows, LANES))
    for copy in table_copies:
        copy.wait()

    def group(i, carry):
        cols = group_of(i, size)
        now = x_ref[:, cols].astype(F32) * wide(inverse_ref[...], size)
        normed_ref[8 : rows + 8] = now
        past = normed_ref[7 : rows + 7]
        older = normed_ref[6 : rows + 6]
        query, key, value = filtered(taps_of(taps_ref, gain_ref, cols), now, past, older)
        kept = lax.broadcasted_iota(jnp.int32, (16, size), 0) >= 2
        signals = []
        for signal, out_ref in ((key * value, mixed_ref), (cot_ref[:, cols].astype(F32) * query, gate_ref)):
            head = jnp.where(kept, signal[0:16], 0.0)
            signal = jnp.concatenate([head, signal[16:]], axis=0).astype(BF16)
            out_ref[:, cols] = signal
            signals.append(signal)
        both = jnp.dot(moments_ref[...], jnp.concatenate(signals, axis=0), preferred_element_type=F32)
        for side in range(2):
            high = 2 * PADDED * side
            moment_ref[PADDED * side : PADDED * (side + 1), cols] = (
                both[high : high + PADDED] + both[high + PADDED : high + 2 * PADDED]
            )
        return carry

    def project(i, carry):
        cols = group_of(i)
        rates = rates_ref[:, cols]
        states = [0.0, 0.0]
        for k in range(NODES):
            power = jnp.exp(rates * (-nodes[k]))
            states = [
                states[side] + power * moment_ref[PADDED * side + k : PADDED * side + k + 1, cols]
                for side in range(2)
            ]
        for side in range(2):
            state_ref[MODES * side : MODES * (side + 1), cols] = states[side]
        x_head = x_ref[0:16, cols].astype(F32)
        x_tail = x_ref[rows - 16 : rows, cols].astype(F32)
        cot_head = cot_ref[0:16, cols].astype(F32)
        packet_ref[i] = jnp.concatenate(
            states + [x_head[0:2], x_tail[14:16], cot_head[0:2], scales], axis=0
        ).astype(BF16)
        return carry

    lane = lax.broadcasted_iota(jnp.int32, (1, LANES), 1)
    scale = jnp.zeros((1, LANES), F32)
    for n, row in enumerate((0, 1, rows - 2, rows - 1)):
        scale = jnp.where(lane == n, inverse_ref[row : row + 1], scale)
    scale_high = scale.astype(BF16).astype(F32)
    scales = jnp.concatenate([scale_high, scale - scale_high], axis=0)

    out_copies = []
    for p in range(pieces):
        cot_copies[p].wait()
        lax.fori_loop(p * (part // size), (p + 1) * (part // size), group, 0)
        out_copies += [
            pltpu.make_async_copy(mixed_ref.at[piece(p)], mixed_hbm.at[piece(p)], mixed_sems.at[p]),
            pltpu.make_async_copy(gate_ref.at[piece(p)], gate_hbm.at[piece(p)], gate_sems.at[p]),
        ]
        for copy in out_copies[-2:]:
            copy.start()
    lax.fori_loop(0, width // LANES, project, 0, unroll=2)
    out_copies += [
        pltpu.make_async_copy(source, target, last_sems.at[n])
        for n, (source, target) in enumerate(
            ((packet_ref, packet_hbm), (state_ref, state_hbm), (inverse_ref, inverse_hbm))
        )
    ]
    for copy in out_copies[-3:]:
        copy.start()
    for copy in out_copies:
        copy.wait()


def near_kernel(
    signal_ref, rates_ref, residue_ref, places_ref, skip_ref, near_ref, mark_ref, out_ref, done_ref, parts_ref
):
    rows = signal_ref.shape[0]
    done_ref[...] = jnp.zeros_like(done_ref)
    size = min(NEAR_GROUP, signal_ref.shape[1])

    def group(i, carry):
        cols = group_of(i, size)
        rates = rates_ref[:, cols]
        nodal = nodal_sum(rates, coefs_of(rates, residue_ref[:, cols]), places_ref[...]).astype(BF16)
        signal = signal_ref[:, cols]
        for k in range(NODES):
            parts_ref[k * rows : (k + 1) * rows] = signal * nodal[k : k + 1]
        out_ref[:, cols] = (
            jnp.dot(near_ref[0], parts_ref[...], preferred_element_type=F32)
            + skip_ref[:, cols] * signal.astype(F32)
        )
        return carry

    lax.fori_loop(0, signal_ref.shape[1] // size, group, 0)


def scan_kernel(rates_ref, gain_ref, taps_ref, packet_ref, mark_ref, enter_ref, done_ref, wide_ref, row_ref, *, rows):
    done_ref[...] = jnp.zeros_like(done_ref)
    count = packet_ref.shape[0]
    first = lax.axis_index("seq") * LANES
    cols = pl.ds(pl.multiple_of(first, LANES), LANES)
    rates = rates_ref[:, cols]
    taps = taps_of(taps_ref, gain_ref, cols)
    for d in range(count):
        wide_ref[d * PACKET : (d + 1) * PACKET] = packet_ref[d].astype(F32)
    x_0, x_1, x_2, x_3, cot_0, cot_1, high, low = [
        wide_ref[pl.ds(EXTRA + n, count, stride=PACKET), :] for n in range(8)
    ]
    scale = high + low
    n_0, n_1, n_2, n_3 = [
        x * jnp.broadcast_to(scale[:, n : n + 1], (count, LANES))
        for n, x in enumerate((x_0, x_1, x_2, x_3))
    ]
    zero = jnp.zeros((1, LANES), F32)

    def before(block):
        return jnp.concatenate([zero, block[:-1]], axis=0)

    def after(block):
        return jnp.concatenate([block[1:], zero], axis=0)

    n_2, n_3 = before(n_2), before(n_3)
    query_0, key_0, value_0 = filtered(taps, n_0, n_3, n_2)
    query_1, key_1, value_1 = filtered(taps, n_1, n_0, n_3)
    heads = (key_0 * value_0, key_1 * value_1, cot_0 * query_0, cot_1 * query_1)
    edges = (before(x_2), before(x_3), after(x_0), after(x_1), after(cot_0), after(cot_1))
    for n, block in enumerate(heads):
        row_ref[n] = block.astype(BF16).astype(F32)
    for n, block in enumerate(edges):
        row_ref[len(heads) + n] = block

    decay = jnp.exp(rates * (-float(rows)))
    lead_0 = jnp.exp(rates * (1.0 - rows))
    lead_1 = jnp.exp(rates * (2.0 - rows))
    decay_1 = jnp.exp(-rates)
    ahead = jnp.zeros((MODES, LANES), F32)
    back = jnp.zeros((MODES, LANES), F32)
    backs = [None] * count
    for d in reversed(range(count)):
        backs[d] = back
        own = wide_ref[d * PACKET + MODES : d * PACKET + 2 * MODES]
        back = decay * back + (own + row_ref[2, d : d + 1] + decay_1 * row_ref[3, d : d + 1])
    for d in range(count):
        extra = [row_ref[len(heads) + n, d : d + 1] for n in range(6)]
        enter_ref[d] = jnp.concatenate([ahead, backs[d]] + extra + [zero, zero], axis=0).astype(BF16)
        own = wide_ref[d * PACKET : d * PACKET + MODES]
        ahead = decay * ahead + (own + lead_0 * row_ref[0, d : d + 1] + lead_1 * row_ref[1, d : d + 1])


def over(block):
    return jnp.sum(block, axis=0, keepdims=True)


def entered_of(enter_ref, i, size, side):
    pieces = size // LANES
    return jnp.concatenate(
        [enter_ref[i * pieces + h, MODES * side : MODES * (side + 1)].astype(F32) for h in range(pieces)], axis=1
    )


def fill_part(
    i, size, x_ref, cot_ref, inverse_ref, gain_ref, taps_ref, rates_ref, residue_ref, skip_ref, places_ref, enter_ref,
    edge_ref, edge_scale, small_ref, nodal_ref, patch_ref, mixed_ref,
):
    cols = group_of(i, size)
    skip = skip_ref[:, cols]
    small_ref[6:8] = edge_ref[0:2, cols] * edge_scale[0:2]
    small_ref[8:16] = x_ref[:, cols].astype(F32)[0:8] * wide(inverse_ref[0:8], size)
    query, key, value = filtered(taps_of(taps_ref, gain_ref, cols), small_ref[8:16], small_ref[7:15], small_ref[6:14])
    mixed = (key * value).astype(BF16).astype(F32)
    gate = (cot_ref[:, cols].astype(F32)[0:8] * query).astype(BF16).astype(F32)
    mixed_ref[:, cols] = mixed
    mixed_0, mixed_1 = mixed[0:1], mixed[1:2]
    gate_0, gate_1 = gate[0:1], gate[1:2]

    rates = rates_ref[:, cols]
    coef = coefs_of(rates, residue_ref[:, cols])
    decay = jnp.exp(-rates)
    rise = jnp.exp(rates)
    now, later, earlier = over(coef), over(coef * decay), over(coef * rise)
    patches = (
        skip * mixed_0 - earlier * mixed_1,
        skip * mixed_1,
        (now + skip) * gate_0 + later * gate_1,
        (now + skip) * gate_1,
    )
    zeros = jnp.zeros((6, size), F32)
    patch_ref[0:8, cols] = jnp.concatenate([patches[0], patches[1], zeros], axis=0)
    patch_ref[8:16, cols] = jnp.concatenate([patches[2], patches[3], zeros], axis=0)

    weights = [
        coef * (decay * entered_of(enter_ref, i, size, 0) + mixed_0 + rise * mixed_1),
        coef * decay * entered_of(enter_ref, i, size, 1),
    ]
    places = wide(places_ref[...], size)
    nodals = [0.0, 0.0]
    for r in range(MODES):
        column = jnp.exp(-rates[r : r + 1] * places)
        nodals = [nodals[side] + column * weights[side][r : r + 1] for side in range(2)]
    for side in range(2):
        high = nodals[side].astype(BF16)
        low = (nodals[side] - high.astype(F32)).astype(BF16)
        nodal_ref[side, :, cols] = jnp.concatenate([high, high, low], axis=0)


def finish_kernel(
    rows, first, count, x_hbm, cot_hbm, ahead_hbm, back_hbm, inverse_ref, gain_ref, taps_ref, spread_ref, enter_ref,
    residue_ref, rates_ref, skip_ref, *refs,
):
    low = first == 0
    if low:
        (
            places_ref, layer_ref, grad_ref, nodal_ref, edge_ref, mixed_ref,
            head_x_ref, head_cot_ref, head_sems, small_ref, patch_ref, *refs,
        ) = refs
    else:
        state_ref, nodal_ref, edge_ref, mixed_ref, layer_ref, grad_ref, *refs = refs
    (
        x_ref, cot_ref, ahead_ref, back_ref, base_ref, normed_refs, one_refs, two_refs, total_ref, load_sems,
    ) = refs
    width = x_ref.shape[1]
    size = normed_refs.shape[2]
    together = normed_refs.shape[0]
    pieces = load_sems.shape[1]
    part = width // pieces
    top = 0 if low else 16
    reach = count + 8 if low else count

    def lanes(p):
        return pl.ds(p * part, part)

    if low:
        heads = [
            pltpu.make_async_copy(source.at[pl.ds(0, 16)], target, head_sems.at[n])
            for n, (source, target) in enumerate(((x_hbm, head_x_ref), (cot_hbm, head_cot_ref)))
        ]
        for copy in heads:
            copy.start()
    loads = []
    for p in range(pieces):
        loads.append([
            pltpu.make_async_copy(
                source.at[pl.ds(lo, target.shape[0]), lanes(p)], target.at[:, lanes(p)], load_sems.at[k, p]
            )
            for k, (source, target, lo) in enumerate((
                (x_hbm, x_ref, first - top),
                (cot_hbm, cot_ref, first),
                (ahead_hbm, ahead_ref, first),
                (back_hbm, back_ref, first),
            ))
        ])
        for copy in loads[p]:
            copy.start()

    total_ref[...] = jnp.zeros_like(total_ref)
    if low:
        def edges(j, total):
            block = enter_ref[j].astype(F32)[EXTRA:PACKET]
            edge_ref[0:8, group_of(j)] = block
            return total + block * block

        total = lax.fori_loop(0, width // LANES, edges, jnp.zeros((8, LANES), F32), unroll=4)
        edge_ref[8:16, 0:LANES] = jnp.broadcast_to(row_scale(total, width), (8, LANES))
        for copy in heads:
            copy.wait()
        fill_size = small_ref.shape[1]
        fill_scale = wide(edge_ref[8:16, 0:LANES], fill_size)

        def fill(i, carry):
            fill_part(
                i, fill_size, head_x_ref, head_cot_ref, inverse_ref, gain_ref, taps_ref, rates_ref, residue_ref,
                skip_ref, places_ref, enter_ref, edge_ref, fill_scale, small_ref, nodal_ref, patch_ref, mixed_ref,
            )
            return carry

        lax.fori_loop(0, width // fill_size, fill, 0)

    edge_scale = wide(edge_ref[8:16, 0:LANES], size)
    inverse = wide(inverse_ref[first : first + reach], size)

    def group(i, normed_ref, one_ref, two_ref):
        cols = group_of(i, size)
        taps = taps_of(taps_ref, gain_ref, cols)
        x = x_ref[top:, cols].astype(F32)[0:reach]
        cot = cot_ref[:, cols].astype(F32)[0:reach]
        normed_ref[16 : reach + 16] = x * inverse
        if low:
            normed_ref[14:16] = edge_ref[0:2, cols] * edge_scale[0:2]
        else:
            above = x_ref[0:16, cols].astype(F32)
            normed_ref[0:16] = above * wide(inverse_ref[first - 16 : first], size)
        now = normed_ref[16 : reach + 16]
        past = normed_ref[15 : reach + 15]
        older = normed_ref[14 : reach + 14]
        query, key, value = filtered(taps, now, past, older)

        convs = []
        for side, near_ref in enumerate((ahead_ref, back_ref)):
            far = jnp.dot(
                spread_ref[side * rows + first : side * rows + first + reach],
                nodal_ref[side, :, cols],
                preferred_element_type=F32,
            )
            total = near_ref[:, cols] + far
            if low:
                total = jnp.concatenate([total[0:8] + patch_ref[8 * side : 8 * side + 8, cols], total[8:]], axis=0)
            convs.append(total.astype(BF16).astype(F32))
        conv, conv_back = convs
        layer_ref[:, cols] = (x[0:count] + query[0:count] * conv[0:count]).astype(BF16)

        grads = (cot * conv, conv_back * value, conv_back * key)
        lagged = [sum(taps[j][i] * grads[j] for j in range(3)) for i in range(3)]
        one_ref[0:reach] = lagged[1]
        two_ref[0:reach] = lagged[2]
        if not low:
            normed_ref[count + 16 : count + 18] = edge_ref[2:4, cols] * edge_scale[2:4]
            n_query, n_key, n_value = filtered(
                taps,
                normed_ref[count + 16 : count + 18],
                normed_ref[count + 15 : count + 17],
                normed_ref[count + 14 : count + 16],
            )
            n_cot = edge_ref[4:6, cols]
            n_mixed = (n_key * n_value).astype(BF16).astype(F32)
            n_gate = (n_cot * n_query).astype(BF16).astype(F32)
            rates = rates_ref[:, cols]
            coef = coefs_of(rates, residue_ref[:, cols])
            decay = jnp.exp(-rates)
            lead = coef * decay
            skip = skip_ref[:, cols]
            entered = [entered_of(enter_ref, i, size, side) for side in range(2)]
            own = (
                state_ref[0:MODES, cols]
                + jnp.exp(rates * (1.0 - rows)) * mixed_ref[0:1, cols]
                + jnp.exp(rates * (2.0 - rows)) * mixed_ref[1:2, cols]
            )
            leave = jnp.exp(rates * (-float(rows))) * entered[0] + own
            direct = over(coef) + skip
            mixed_0, mixed_1 = n_mixed[0:1], n_mixed[1:2]
            gate_0, gate_1 = n_gate[0:1], n_gate[1:2]
            conv_0 = over(lead * leave) + direct * mixed_0
            conv_1 = over(lead * decay * leave) + over(lead) * mixed_0 + direct * mixed_1
            back_0 = over(coef * entered[1]) + skip * gate_0
            back_1 = over(coef * (1.0 / decay) * (entered[1] - gate_0)) + skip * gate_1
            n_conv = jnp.concatenate([conv_0, conv_1], axis=0).astype(BF16).astype(F32)
            n_back = jnp.concatenate([back_0, back_1], axis=0).astype(BF16).astype(F32)
            n_grads = (n_cot * n_conv, n_back * n_value, n_back * n_key)
            one_ref[count : count + 2] = sum(taps[j][1] * n_grads[j] for j in range(3))
            two_ref[count : count + 2] = sum(taps[j][2] * n_grads[j] for j in range(3))
        scaled = lagged[0][0:count] + one_ref[1 : count + 1] + two_ref[2 : count + 2]
        base_ref[:, cols] = cot[0:count] + inverse[0:count] * scaled
        return lane_sums(scaled * x[0:count])

    def groups(i, carry):
        sums = [group(i * together + n, normed_refs.at[n], one_refs.at[n], two_refs.at[n]) for n in range(together)]
        total_ref[...] = total_ref[...] + sum(sums)
        return carry

    for p in range(pieces):
        for copy in loads[p]:
            copy.wait()
        steps = part // size // together
        lax.fori_loop(p * steps, (p + 1) * steps, groups, 0)

    mean = jnp.sum(total_ref[...], axis=1, keepdims=True) * (1.0 / width)
    scale = inverse_ref[first : first + count]
    factor = scale * scale * scale * jnp.broadcast_to(mean, (count, LANES))

    def emit(i, carry):
        cols = group_of(i)
        x = x_ref[top : top + count, cols].astype(F32)
        grad_ref[:, cols] = (base_ref[:, cols] - x * factor).astype(BF16)
        return carry

    lax.fori_loop(0, width // LANES, emit, 0, unroll=4)


def join_kernel(first, layer_ref, grad_ref, *refs):
    layer_hbm, grad_hbm, sems = refs[-3:]
    count = layer_ref.shape[0]
    half = layer_ref.shape[1] // 2
    copies = []
    for n, (source, target) in enumerate(((layer_ref, layer_hbm), (grad_ref, grad_hbm))):
        for h in range(2):
            lanes = pl.ds(h * half, half)
            copies.append(
                pltpu.make_async_copy(source.at[:, lanes], target.at[pl.ds(first, count), lanes], sems.at[n, h])
            )
    for copy in copies:
        copy.start()
    for copy in copies:
        copy.wait()


def shifted(block, axis, distance):
    devices = range(lax.axis_size(axis))
    route = [(i - distance, i) for i in devices if i - distance in devices]
    return lax.ppermute(block, axis, route)


def whole(shape):
    return pl.BlockSpec(shape, lambda *i: (0,) * len(shape))


def across(shape, step, axis=None):
    axis = len(shape) - 1 if axis is None else axis
    block = shape[:axis] + (step,) + shape[axis + 1 :]
    return pl.BlockSpec(block, lambda i: (0,) * axis + (i,) + (0,) * (len(shape) - axis - 1))


def params(mib):
    return pltpu.CompilerParams(vmem_limit_bytes=mib << 20)


def stay(array):
    return pltpu.with_memory_space_constraint(array, pltpu.HBM)


def takes(micros):
    return pl.CostEstimate(
        flops=int(micros * 1.1e9), bytes_accessed=int(micros * 3.5e6), transcendentals=0
    )


def start_call(x, cot, gain, taps, rates, moments):
    rows, width = x.shape
    pieces = PIECES
    far = pl.BlockSpec(memory_space=pltpu.HBM)
    outs = [
        (x.shape, BF16),
        (x.shape, BF16),
        ((width // LANES, PACKET, LANES), BF16),
        ((2 * MODES, width), F32),
        ((rows, LANES), F32),
    ]
    ins = (x, cot, gain, taps, rates, moments)
    held = (x, cot, gain, taps, rates, moments)
    return pl.pallas_call(
        functools.partial(start_kernel, [float(p) for p in node_places(rows)]),
        in_specs=[far] * len(ins),
        out_specs=[far] * len(outs),
        out_shape=[pltpu.HBM(*out) for out in outs],
        scratch_shapes=[pltpu.VMEM(array.shape, array.dtype) for array in held]
        + [pltpu.VMEM(*out) for out in outs]
        + [
            pltpu.VMEM((rows + 8, min(START_GROUP, width // pieces)), F32),
            pltpu.VMEM((2 * PADDED, width), F32),
            pltpu.SemaphoreType.DMA((pieces,)),
            pltpu.SemaphoreType.DMA((pieces,)),
            pltpu.SemaphoreType.DMA((4,)),
            pltpu.SemaphoreType.DMA((pieces,)),
            pltpu.SemaphoreType.DMA((pieces,)),
            pltpu.SemaphoreType.DMA((3,)),
        ],
        compiler_params=params(24),
        cost_estimate=takes(6),
        name="start",
    )(*[stay(array) for array in ins])


def near_call(side, signal, rates, residue, places, skip, near, mark):
    rows, width = signal.shape
    step = min(NEAR_STEP, width)
    return pl.pallas_call(
        near_kernel,
        grid=(width // step,),
        in_specs=[
            across(signal.shape, step),
            across(rates.shape, step), across(rates.shape, step), whole(places.shape),
            across(skip.shape, step),
            pl.BlockSpec((1,) + near.shape[1:], lambda i: (side, 0, 0)),
            whole((8, LANES)),
        ],
        out_specs=[across(signal.shape, step), whole((8, LANES))],
        out_shape=[pltpu.HBM(signal.shape, F32), shape((8, LANES), F32)],
        scratch_shapes=[pltpu.VMEM((NODES * rows, min(NEAR_GROUP, width)), BF16)],
        compiler_params=params(16),
        cost_estimate=takes(4),
        name="near",
    )(stay(signal), rates, residue, places, skip, stay(near), mark)


def scan_call(rates, gain, taps, gathered, mark, rows):
    return pl.pallas_call(
        functools.partial(scan_kernel, rows=rows),
        out_shape=[shape(gathered.shape, BF16), shape((8, LANES), F32)],
        scratch_shapes=[
            pltpu.VMEM((gathered.shape[0] * PACKET, LANES), F32),
            pltpu.VMEM((10, gathered.shape[0], LANES), F32),
        ],
        compiler_params=params(6),
        cost_estimate=takes(1),
        name="scan",
    )(rates, gain, taps, gathered, mark)


def finish_call(rows, first, count, *arrays):
    x = arrays[0]
    width = x.shape[1]
    low = first == 0
    pieces = PIECES
    size = min(FINISH_GROUP, width)
    together = min(FINISH_TOGETHER, width // pieces // size)
    fill_size = min(FILL_GROUP, width)
    far = pl.BlockSpec(memory_space=pltpu.HBM)
    near = pl.BlockSpec(memory_space=pltpu.VMEM)
    half = shape((count, width), BF16)
    out_shape = [half, half]
    scratch = []
    above, below, reach = (0, 16, count + 8) if low else (16, 0, count)
    if low:
        out_shape += [shape((2, 3 * PADDED, width), BF16), shape((16, width), F32), shape((8, width), F32)]
        scratch = [
            pltpu.VMEM((16, width), BF16),
            pltpu.VMEM((16, width), BF16),
            pltpu.SemaphoreType.DMA((2,)),
            pltpu.VMEM((16, fill_size), F32),
            pltpu.VMEM((16, width), F32),
        ]
    return pl.pallas_call(
        functools.partial(finish_kernel, rows, first, count),
        in_specs=[far] * 4 + [near] * (len(arrays) - 4),
        out_specs=[near] * len(out_shape),
        out_shape=out_shape,
        scratch_shapes=scratch
        + [
            pltpu.VMEM((above + count + below, width), BF16),
            pltpu.VMEM((count + below, width), BF16),
            pltpu.VMEM((reach, width), F32),
            pltpu.VMEM((reach, width), F32),
            pltpu.VMEM((count, width), F32),
            pltpu.VMEM((together, reach + 24, size), F32),
            pltpu.VMEM((together, reach + 8, size), F32),
            pltpu.VMEM((together, reach + 8, size), F32),
            pltpu.VMEM((count, LANES), F32),
            pltpu.SemaphoreType.DMA((4, pieces)),
        ],
        compiler_params=params(24),
        cost_estimate=takes(6),
        name="finish",
    )(*[stay(array) for array in arrays[:4]], *arrays[4:])


def join_call(rows, first, layer, grad, *wholes):
    far = pl.BlockSpec(memory_space=pltpu.HBM)
    near = pl.BlockSpec(memory_space=pltpu.VMEM)
    out = shape((rows, layer.shape[1]), BF16)
    return pl.pallas_call(
        functools.partial(join_kernel, first),
        in_specs=[near, near] + [far] * len(wholes),
        out_specs=[far, far],
        out_shape=[out, out],
        scratch_shapes=[pltpu.SemaphoreType.DMA((2, 2))],
        input_output_aliases={2 + n: n for n in range(len(wholes))},
        compiler_params=params(4),
        cost_estimate=takes(1),
        name="join",
    )(layer, grad, *wholes)


def local(section_input, cotangent, norm_gain, short_filter, decay_rate, residue, skip_gain):
    x = section_input[0]
    cot = cotangent[0]
    rows = x.shape[0]
    taps = jnp.transpose(short_filter, (1, 2, 0, 3))
    rates = decay_rate[0]
    fixed = {name: jnp.asarray(table) for name, table in constants(rows).items()}

    weights = residue[0]
    mixed, gate, packet, state, inverse = start_call(x, cot, norm_gain, taps, rates, fixed["moments"])
    gathered = lax.all_to_all(packet, "seq", split_axis=0, concat_axis=0, tiled=True)
    near = (rates, weights, fixed["places"], skip_gain, fixed["near"])
    ahead, mark = near_call(0, mixed, *near, stay(inverse))
    entering, mark = scan_call(rates, norm_gain, taps, gathered, mark, rows)
    enter = lax.all_to_all(entering, "seq", split_axis=0, concat_axis=0, tiled=True)
    back, mark = near_call(1, gate, *near, mark)

    common = (x, cot, ahead, back, inverse, norm_gain, taps, fixed["spread"], enter, weights, rates, skip_gain)
    layer, grad, *passed = finish_call(rows, 0, SPLIT, *common, fixed["places"])
    on_low = shifted(layer, "section", 1)
    back_low = shifted(grad, "section", -1)
    layer, grad = finish_call(rows, SPLIT, rows - SPLIT, *common, state, *passed)
    on_high = shifted(layer, "section", 1)
    back_high = shifted(grad, "section", -1)
    joined = join_call(rows, 0, on_low, back_low)
    passed_on, passed_back = join_call(rows, SPLIT, on_high, back_high, *joined)
    return passed_on[None], passed_back[None]


def solution(mesh):
    in_specs = (
        P("section", "seq", None),
        P("section", "seq", None),
        P("section", None),
        P("section", None, None, None),
        P("section", None, None),
        P("section", None, None),
        P("section", None),
    )
    out_specs = (P("section", "seq", None), P("section", "seq", None))
    return jax.shard_map(local, mesh=mesh, in_specs=in_specs, out_specs=out_specs, check_vma=False)
```

time: 90.5 us -> 82.2 us (0.908)
  starting transfers between devices: 32.5 us -> 25.4 us
  waiting for transfers between devices: 17.4 us -> 20.8 us
  Pallas kernels: 37.3 us -> 34.4 us
  local copies, waits for them, and re-layouts: 1.64 us -> 0.05 us
    all_to_all x1, starting transfers between devices: 7.01 us -> 3.88 us  [local(): lax.all_to_all(entering, 'seq', split_axis=0, concat_axis=0, tiled=True)]
    ppermute x6 -> x4, starting transfers between devices: 17 us -> 14.2 us  [shifted(): return lax.ppermute(block, axis, route)]
    pallas_call x3 -> x2, Pallas kernels: 15.1 us -> 12.8 us  [finish_call(): pl.pallas_call(functools.partial(finish_kernel, rows, first, count), in_s...]
    all_to_all x1, waiting for transfers between devices: 1.31 us -> 3.56 us  [local(): lax.all_to_all(packet, 'seq', split_axis=0, concat_axis=0, tiled=True)]
    all_to_all x1, starting transfers between devices: 8.49 us -> 7.33 us  [local(): lax.all_to_all(packet, 'seq', split_axis=0, concat_axis=0, tiled=True)]
    pallas_call x2, Pallas kernels: 12.7 us -> 11.6 us  [near_call(): pl.pallas_call(near_kernel, grid=(width // step,), in_specs=[across(signa...]
    all_to_all x1, waiting for transfers between devices: 2.56 us -> 3.61 us  [local(): lax.all_to_all(entering, 'seq', split_axis=0, concat_axis=0, tiled=True)]
    ppermute x6 -> x4, waiting for transfers between devices: 13.5 us -> 13.6 us  [shifted(): return lax.ppermute(block, axis, route)]
  transfers between devices with their start and end apart: 8 -> 6, of which waited for: 5 -> 6; matrix products, arithmetic and copies ran while one was open for 0% -> 0% of each run, Pallas kernels for 30% -> 21%
where the time goes in v3:
time: 82.2 us; the launch traced here: 81.6 us
  Pallas kernels  34.4 us (42%)
  starting transfers between devices  25.4 us (31%)
  waiting for transfers between devices  20.8 us (25%)
  between operations  0.98 us (1%)
    ppermute x4, starting transfers between devices, shifted(): return lax.ppermute(block, axis, route)  14.2 us
    ppermute x4, waiting for transfers between devices, shifted(): return lax.ppermute(block, axis, route)  13.6 us
    pallas_call x2, Pallas kernels, finish_call(): pl.pallas_call(functools.partial(finish_kernel, rows, first, count), in_s...  12.8 us
    pallas_call x2, Pallas kernels, near_call(): pl.pallas_call(near_kernel, grid=(width // step,), in_specs=[across(signa...  11.6 us
    all_to_all x1, starting transfers between devices, local(): lax.all_to_all(packet, 'seq', split_axis=0, concat_axis=0, tiled=True)  7.33 us
    pallas_call x1, Pallas kernels, start_call(): pl.pallas_call(functools.partial(start_kernel, [float(p) for p in node_pl...  7.06 us
    all_to_all x1, starting transfers between devices, local(): lax.all_to_all(entering, 'seq', split_axis=0, concat_axis=0, tiled=True)  3.88 us
    all_to_all x1, waiting for transfers between devices, local(): lax.all_to_all(entering, 'seq', split_axis=0, concat_axis=0, tiled=True)  3.61 us
  transfers between devices with their start and end apart: 6, of which 6 were waited for; matrix products, arithmetic and copies ran while one was open for 0% of the time, Pallas kernels for 21%

profile of v3, /device:TPU:96, one launch (start us, length us, event | category | flops | bytes accessed | tf_op | source)
XLA Modules:
  0.0 81.6 jit_solution(8430492222013691573)
XLA Ops:
  0.6 0.0 copy-start
  0.6 0.0 copy-start.1
  0.7 0.0 copy-start.4
  0.7 0.0 copy-start.6
  0.7 7.1 %start.1 = (bf16[128,4096]{1,0:T(8,128)(2,1)}, bf16[128,4096]{1,0:T(8,128)(2,1)}, bf16[32,40,128]{2,1,0:T(8,128)(2,1)}, f32[32,4096]{1,0:T(8,128)}, f32[128,128]{1,0:T(8,128)}) custom-call(bf16[128,4096]{1,0:T(8,128)(2,1)} %bitcast.21, bf16[128,4096]{1,0:T(8,128)(2,1)} %bitcast.24, f32[1,4096]{1,0:T(1,128)} %gain_ref.5, f32[3,3,1,4096]{3,2,1,0:T(1,128)} %bitcast.17, ...), custom_call_target="tpu_custom_call" | custom-call | flops 6600000000 | bytes 21000000 | tf_op jit(solution)/shard_map/start/pallas_call | solution.py:601
  7.7 7.3 %all-to-all-start = ((bf16[32,40,128]{2,1,0:T(8,128)(2,1)}), bf16[32,40,128]{2,1,0:T(8,128)(2,1)S(1)}, u32[]{:S(2)}, u32[]{:S(2)}) async-start(bf16[32,40,128]{2,1,0:T(8,128)(2,1)} %get-tuple-element.27), calls=%async_computation | async-start | bytes 655360 | tf_op jit(solution)/shard_map/all_to_all | solution.py:734
  15.1 0.0 copy-done
  15.1 0.0 copy-done.1
  15.1 0.0 copy-done.4
  15.1 0.0 copy-done.6
  15.1 0.0 copy-start.2
  15.1 0.0 copy-start.3
  15.1 5.8 %near.2 = (f32[128,4096]{1,0:T(8,128)}, f32[8,128]{1,0:T(8,128)S(1)}) custom-call(bf16[128,4096]{1,0:T(8,128)(2,1)} %get-tuple-element.23.signal_ref, f32[16,4096]{1,0:T(8,128)S(1)} %bitcast.8, f32[16,4096]{1,0:T(8,128)S(1)} %bitcast.13, f32[16,128]{1,0:T(8,128)S(1)} %copy-done.6, f32[1,4096]{1,0:T(1,128)S(1)} %copy-done.4, ...), custom_call_target="tpu_custom_call" | custom-call | flops 4400000000 | bytes 14000000 | tf_op jit(solution)/shard_map/near/pallas_call | solution.py:627
  20.9 3.6 %all-to-all-done.packet_ref = bf16[32,40,128]{2,1,0:T(8,128)(2,1)S(1)} async-done(((bf16[32,40,128]{2,1,0:T(8,128)(2,1)}), bf16[32,40,128]{2,1,0:T(8,128)(2,1)S(1)}, u32[]{:S(2)}, u32[]{:S(2)}) %all-to-all-start) | async-done | bytes 327712 | tf_op jit(solution)/shard_map/all_to_all | solution.py:734
  24.5 1.0 %scan.1 = (bf16[32,40,128]{2,1,0:T(8,128)(2,1)}, f32[8,128]{1,0:T(8,128)S(1)}) custom-call(f32[16,4096]{1,0:T(8,128)S(1)} %bitcast.9, f32[1,4096]{1,0:T(1,128)S(1)} %copy-done.3, f32[3,3,1,4096]{3,2,1,0:T(1,128)S(1)} %bitcast.18, bf16[32,40,128]{2,1,0:T(8,128)(2,1)S(1)} %all-to-all-done.packet_ref, f32[8,128]{1,0:T(8,128)S(1)} %get-tuple-element.28.mark_ref), custom_call_target="tpu_custom_call" | custom-call | flops 1100000000 | bytes 3500000 | tf_op jit(solution)/shard_map/scan/pallas_call | solution.py:647
  25.5 3.9 %all-to-all-start.1 = ((bf16[32,40,128]{2,1,0:T(8,128)(2,1)}), bf16[32,40,128]{2,1,0:T(8,128)(2,1)S(1)}, u32[]{:S(2)}, u32[]{:S(2)}) async-start(bf16[32,40,128]{2,1,0:T(8,128)(2,1)} %get-tuple-element.31), calls=%async_computation.1 | async-start | bytes 655360 | tf_op jit(solution)/shard_map/all_to_all | solution.py:738
  29.4 0.0 copy-start.5
  29.4 5.8 %near.3 = (f32[128,4096]{1,0:T(8,128)}, f32[8,128]{1,0:T(8,128)}) custom-call(bf16[128,4096]{1,0:T(8,128)(2,1)} %get-tuple-element.26.signal_ref, f32[16,4096]{1,0:T(8,128)S(1)} %bitcast.10, f32[16,4096]{1,0:T(8,128)S(1)} %bitcast.14, f32[16,128]{1,0:T(8,128)S(1)} %copy-done.6, f32[1,4096]{1,0:T(1,128)S(1)} %copy-done.4, ...), custom_call_target="tpu_custom_call" | custom-call | flops 4400000000 | bytes 14000000 | tf_op jit(solution)/shard_map/near/pallas_call | solution.py:627
  35.2 3.6 %all-to-all-done.1.enter_ref = bf16[32,40,128]{2,1,0:T(8,128)(2,1)S(1)} async-done(((bf16[32,40,128]{2,1,0:T(8,128)(2,1)}), bf16[32,40,128]{2,1,0:T(8,128)(2,1)S(1)}, u32[]{:S(2)}, u32[]{:S(2)}) %all-to-all-start.1) | async-done | bytes 327712 | tf_op jit(solution)/shard_map/all_to_all | solution.py:738
  38.8 0.0 copy-done.5
  38.8 8.3 %finish.2 = (bf16[80,4096]{1,0:T(8,128)(2,1)S(1)}, bf16[80,4096]{1,0:T(8,128)(2,1)S(1)}, bf16[2,48,4096]{2,1,0:T(8,128)(2,1)S(1)}, f32[16,4096]{1,0:T(8,128)S(1)}, f32[8,4096]{1,0:T(8,128)S(1)}) custom-call(bf16[128,4096]{1,0:T(8,128)(2,1)} %bitcast.22, bf16[128,4096]{1,0:T(8,128)(2,1)} %bitcast.25, f32[128,4096]{1,0:T(8,128)} %get-tuple-element.25.ahead_hbm, ...), custom_call_target="tpu_custom_call" | custom-call | flops 6600000000 | bytes 21000000 | tf_op jit(solution)/shard_map/finish/pallas_call | solution.py:683
  47.1 5.0 %collective-permute-start.2 = (bf16[80,4096]{1,0:T(8,128)(2,1)S(1)}, bf16[80,4096]{1,0:T(8,128)(2,1)S(1)}, u32[]{:S(2)}, u32[]{:S(2)}) collective-permute-start(bf16[80,4096]{1,0:T(8,128)(2,1)S(1)} %get-tuple-element.38), channel_id=1, source_target_pairs={{0,32},{32,64},{64,96},{96,128},{128,160},{160,192},{192,224},{224... | collective-permute-start | bytes 1966088 | tf_op jit(solution)/shard_map/ppermute | solution.py:561
  52.2 2.1 %collective-permute-start.3 = (bf16[80,4096]{1,0:T(8,128)(2,1)S(1)}, bf16[80,4096]{1,0:T(8,128)(2,1)S(1)}, u32[]{:S(2)}, u32[]{:S(2)}) collective-permute-start(bf16[80,4096]{1,0:T(8,128)(2,1)S(1)} %get-tuple-element.39), channel_id=1, source_target_pairs={{32,0},{64,32},{96,64},{128,96},{160,128},{192,160},{224,192},{256... | collective-permute-start | bytes 1966088 | tf_op jit(solution)/shard_map/ppermute | solution.py:561
  54.3 4.5 %finish.3 = (bf16[48,4096]{1,0:T(8,128)(2,1)S(1)}, bf16[48,4096]{1,0:T(8,128)(2,1)S(1)}) custom-call(bf16[128,4096]{1,0:T(8,128)(2,1)} %bitcast.23, bf16[128,4096]{1,0:T(8,128)(2,1)} %bitcast.26, f32[128,4096]{1,0:T(8,128)} %get-tuple-element.25.ahead_hbm, f32[128,4096]{1,0:T(8,128)} %get-tuple-element.30.back_hbm, f32[128,128]{1,0:T(8,128)S(1)} %copy-done.8, ...), custom_call_target="tpu_custom_call" | custom-call | flops 6600000000 | bytes 21000000 | tf_op jit(solution)/shard_map/finish/pallas_call | solution.py:683
  58.8 5.1 %collective-permute-start = (bf16[48,4096]{1,0:T(8,128)(2,1)S(1)}, bf16[48,4096]{1,0:T(8,128)(2,1)S(1)}, u32[]{:S(2)}, u32[]{:S(2)}) collective-permute-start(bf16[48,4096]{1,0:T(8,128)(2,1)S(1)} %get-tuple-element.36), channel_id=1, source_target_pairs={{0,32},{32,64},{64,96},{96,128},{128,160},{160,192},{192,224},{224... | collective-permute-start | bytes 1179656 | tf_op jit(solution)/shard_map/ppermute | solution.py:561
  64.0 1.9 %collective-permute-start.1 = (bf16[48,4096]{1,0:T(8,128)(2,1)S(1)}, bf16[48,4096]{1,0:T(8,128)(2,1)S(1)}, u32[]{:S(2)}, u32[]{:S(2)}) collective-permute-start(bf16[48,4096]{1,0:T(8,128)(2,1)S(1)} %get-tuple-element.37), channel_id=1, source_target_pairs={{32,0},{64,32},{96,64},{128,96},{160,128},{192,160},{224,192},{256... | collective-permute-start | bytes 1179656 | tf_op jit(solution)/shard_map/ppermute | solution.py:561
  65.9 1.3 %collective-permute-done.2.layer_ref = bf16[80,4096]{1,0:T(8,128)(2,1)S(1)} collective-permute-done((bf16[80,4096]{1,0:T(8,128)(2,1)S(1)}, bf16[80,4096]{1,0:T(8,128)(2,1)S(1)}, u32[]{:S(2)}, u32[]{:S(2)}) %collective-permute-start.2) | collective-permute-done | bytes 655392 | tf_op jit(solution)/shard_map/ppermute | solution.py:561
  67.2 5.6 %collective-permute-done.3.grad_ref = bf16[80,4096]{1,0:T(8,128)(2,1)S(1)} collective-permute-done((bf16[80,4096]{1,0:T(8,128)(2,1)S(1)}, bf16[80,4096]{1,0:T(8,128)(2,1)S(1)}, u32[]{:S(2)}, u32[]{:S(2)}) %collective-permute-start.3) | collective-permute-done | bytes 655392 | tf_op jit(solution)/shard_map/ppermute | solution.py:561
  72.8 1.1 %join.2 = (bf16[128,4096]{1,0:T(8,128)(2,1)}, bf16[128,4096]{1,0:T(8,128)(2,1)}) custom-call(bf16[80,4096]{1,0:T(8,128)(2,1)S(1)} %collective-permute-done.2.layer_ref, bf16[80,4096]{1,0:T(8,128)(2,1)S(1)} %collective-permute-done.3.grad_ref), custom_call_target="tpu_custom_call" | custom-call | flops 1100000000 | bytes 3500000 | tf_op jit(solution)/shard_map/join/pallas_call | solution.py:711
  73.9 1.3 %collective-permute-done.layer_ref = bf16[48,4096]{1,0:T(8,128)(2,1)S(1)} collective-permute-done((bf16[48,4096]{1,0:T(8,128)(2,1)S(1)}, bf16[48,4096]{1,0:T(8,128)(2,1)S(1)}, u32[]{:S(2)}, u32[]{:S(2)}) %collective-permute-start) | collective-permute-done | bytes 393248 | tf_op jit(solution)/shard_map/ppermute | solution.py:561
  75.2 5.3 %collective-permute-done.1.grad_ref = bf16[48,4096]{1,0:T(8,128)(2,1)S(1)} collective-permute-done((bf16[48,4096]{1,0:T(8,128)(2,1)S(1)}, bf16[48,4096]{1,0:T(8,128)(2,1)S(1)}, u32[]{:S(2)}, u32[]{:S(2)}) %collective-permute-start.1) | collective-permute-done | bytes 393248 | tf_op jit(solution)/shard_map/ppermute | solution.py:561
  80.6 0.9 %join.3 = (bf16[128,4096]{1,0:T(8,128)(2,1)}, bf16[128,4096]{1,0:T(8,128)(2,1)}) custom-call(bf16[48,4096]{1,0:T(8,128)(2,1)S(1)} %collective-permute-done.layer_ref, bf16[48,4096]{1,0:T(8,128)(2,1)S(1)} %collective-permute-done.1.grad_ref, bf16[128,4096]{1,0:T(8,128)(2,1)} %get-tuple-element.40.refs_0_, ...), custom_call_target="tpu_custom_call", output_to_operand_aliasing={{0}: (2, {}), {1}: (3, {})} | custom-call | flops 1100000000 | bytes 3500000 | tf_op jit(solution)/shard_map/join/pallas_call | solution.py:711
  (6 shorter events, 0.0 us)
Async XLA Ops:
  0.6 14.4 %copy-start = (f32[1,16,4096]{2,1,0:T(8,128)S(1)}, f32[1,16,4096]{2,1,0:T(8,128)}, u32[]{:S(2)}) copy-start(f32[1,16,4096]{2,1,0:T(8,128)} %param.15) | copy-start | bytes 786436
  0.6 14.4 %copy-start.1 = (f32[1,16,4096]{2,1,0:T(8,128)S(1)}, f32[1,16,4096]{2,1,0:T(8,128)}, u32[]{:S(2)}) copy-start(f32[1,16,4096]{2,1,0:T(8,128)} %param.16) | copy-start | bytes 786436
  0.7 14.4 %copy-start.4 = (f32[1,4096]{1,0:T(1,128)S(1)}, f32[1,4096]{1,0:T(1,128)}, u32[]{:S(2)}) copy-start(f32[1,4096]{1,0:T(1,128)} %skip_ref.7) | copy-start | bytes 49156
  0.7 14.4 %copy-start.6 = (f32[16,128]{1,0:T(8,128)S(1)}, f32[16,128]{1,0:T(8,128)}, u32[]{:S(2)}) copy-start(f32[16,128]{1,0:T(8,128)} %constant.11.clone.places_ref.refs_0_) | copy-start | bytes 24580
  7.7 16.8 %all-to-all-start = ((bf16[32,40,128]{2,1,0:T(8,128)(2,1)}), bf16[32,40,128]{2,1,0:T(8,128)(2,1)S(1)}, u32[]{:S(2)}, u32[]{:S(2)}) async-start(bf16[32,40,128]{2,1,0:T(8,128)(2,1)} %get-tuple-element.27), calls=%async_computation | async-start | bytes 655360 | tf_op jit(solution)/shard_map/all_to_all | solution.py:734
  15.1 9.4 %copy-start.2 = (f32[1,3,3,4096]{3,0,2,1:T(1,128)S(1)}, f32[1,3,3,4096]{3,0,2,1:T(1,128)}, u32[]{:S(2)}) copy-start(f32[1,3,3,4096]{3,0,2,1:T(1,128)} %param.14) | copy-start | bytes 442372
  15.1 9.4 %copy-start.3 = (f32[1,4096]{1,0:T(1,128)S(1)}, f32[1,4096]{1,0:T(1,128)}, u32[]{:S(2)}) copy-start(f32[1,4096]{1,0:T(1,128)} %gain_ref.5) | copy-start | bytes 49156
  25.5 13.3 %all-to-all-start.1 = ((bf16[32,40,128]{2,1,0:T(8,128)(2,1)}), bf16[32,40,128]{2,1,0:T(8,128)(2,1)S(1)}, u32[]{:S(2)}, u32[]{:S(2)}) async-start(bf16[32,40,128]{2,1,0:T(8,128)(2,1)} %get-tuple-element.31), calls=%async_computation.1 | async-start | bytes 655360 | tf_op jit(solution)/shard_map/all_to_all | solution.py:738
  29.4 9.4 %copy-start.5 = (bf16[256,48]{1,0:T(8,128)(2,1)S(1)}, bf16[256,48]{1,0:T(8,128)(2,1)}, u32[]{:S(2)}) copy-start(bf16[256,48]{1,0:T(8,128)(2,1)} %constant.9.clone.spread_ref) | copy-start | bytes 73732
  29.4 9.4 %copy-start.8 = (f32[128,128]{1,0:T(8,128)S(1)}, f32[128,128]{1,0:T(8,128)}, u32[]{:S(2)}) copy-start(f32[128,128]{1,0:T(8,128)} %get-tuple-element.24.mark_ref.inverse_ref) | copy-start | bytes 196612
  38.8 15.5 %copy-start.7 = (f32[32,4096]{1,0:T(8,128)S(1)}, f32[32,4096]{1,0:T(8,128)}, u32[]{:S(2)}) copy-start(f32[32,4096]{1,0:T(8,128)} %get-tuple-element.32.refs_0_) | copy-start | bytes 1572868
  47.1 20.1 %collective-permute-start.2 = (bf16[80,4096]{1,0:T(8,128)(2,1)S(1)}, bf16[80,4096]{1,0:T(8,128)(2,1)S(1)}, u32[]{:S(2)}, u32[]{:S(2)}) collective-permute-start(bf16[80,4096]{1,0:T(8,128)(2,1)S(1)} %get-tuple-element.38), channel_id=1, source_target_pairs={{0,32},{32,64},{64,96},{96,128},{128,160},{160,192},{192,224},{224... | collective-permute-start | bytes 1966088 | tf_op jit(solution)/shard_map/ppermute | solution.py:561
  52.2 20.7 %collective-permute-start.3 = (bf16[80,4096]{1,0:T(8,128)(2,1)S(1)}, bf16[80,4096]{1,0:T(8,128)(2,1)S(1)}, u32[]{:S(2)}, u32[]{:S(2)}) collective-permute-start(bf16[80,4096]{1,0:T(8,128)(2,1)S(1)} %get-tuple-element.39), channel_id=1, source_target_pairs={{32,0},{64,32},{96,64},{128,96},{160,128},{192,160},{224,192},{256... | collective-permute-start | bytes 1966088 | tf_op jit(solution)/shard_map/ppermute | solution.py:561
  58.8 16.4 %collective-permute-start = (bf16[48,4096]{1,0:T(8,128)(2,1)S(1)}, bf16[48,4096]{1,0:T(8,128)(2,1)S(1)}, u32[]{:S(2)}, u32[]{:S(2)}) collective-permute-start(bf16[48,4096]{1,0:T(8,128)(2,1)S(1)} %get-tuple-element.36), channel_id=1, source_target_pairs={{0,32},{32,64},{64,96},{96,128},{128,160},{160,192},{192,224},{224... | collective-permute-start | bytes 1179656 | tf_op jit(solution)/shard_map/ppermute | solution.py:561
  64.0 16.6 %collective-permute-start.1 = (bf16[48,4096]{1,0:T(8,128)(2,1)S(1)}, bf16[48,4096]{1,0:T(8,128)(2,1)S(1)}, u32[]{:S(2)}, u32[]{:S(2)}) collective-permute-start(bf16[48,4096]{1,0:T(8,128)(2,1)S(1)} %get-tuple-element.37), channel_id=1, source_target_pairs={{32,0},{64,32},{96,64},{128,96},{160,128},{192,160},{224,192},{256... | collective-permute-start | bytes 1179656 | tf_op jit(solution)/shard_map/ppermute | solution.py:561

commit v4 on v3

--- a/solution.py
+++ b/solution.py
@@ -15,14 +15,15 @@
 PACKET = 40
 EXTRA = 32
 LANES = 128
-START_GROUP = 1024
+START_GROUP = 128
+START_TOGETHER = 8
+PROJECT_UNROLL = 4
 PIECES = 4
 SPLIT = 80
 NEAR_STEP = 1024
 NEAR_GROUP = 1024
 FINISH_GROUP = 128
 FINISH_TOGETHER = 8
-FILL_GROUP = 512
 F32 = jnp.float32
 BF16 = jnp.bfloat16
 shape = jax.ShapeDtypeStruct
@@ -58,8 +59,10 @@
     flip_high, flip_low = high[::-1], low[::-1]
     moment_ahead = np.concatenate([flip_high.T, flip_low.T], axis=0)
     moment_back = np.concatenate([high.T, low.T], axis=0)
-    spread_ahead = np.concatenate([high, low, high], axis=1)
-    spread_back = np.concatenate([flip_high, flip_low, flip_high], axis=1)
+    first_rows = np.zeros((rows, PADDED), high.dtype)
+    first_rows[0, NODES] = first_rows[1, NODES + 1] = 1.0
+    spread_ahead = np.concatenate([high + first_rows, low], axis=1)
+    spread_back = np.concatenate([flip_high + first_rows, flip_low], axis=1)
     lag = np.arange(rows)[:, None] - np.arange(rows)[None, :]
     toeplitz = np.where(lag[:, :, None] >= 0, table[np.maximum(lag, 0)], 0.0)
     near_ahead = np.transpose(toeplitz, (0, 2, 1)).reshape(rows, NODES * rows)
@@ -123,12 +126,12 @@
 
 def start_kernel(
     nodes, x_hbm, cot_hbm, gain_hbm, taps_hbm, rates_hbm, moments_hbm,
-    mixed_hbm, gate_hbm, packet_hbm, state_hbm, inverse_hbm,
-    x_ref, cot_ref, gain_ref, taps_ref, rates_ref, moments_ref, mixed_ref, gate_ref, packet_ref, state_ref, inverse_ref,
-    normed_ref, moment_ref, x_sems, cot_sems, table_sems, mixed_sems, gate_sems, last_sems,
+    mixed_hbm, gate_hbm, packet_hbm, inverse_hbm,
+    x_ref, cot_ref, gain_ref, taps_ref, rates_ref, moments_ref, mixed_ref, gate_ref, packet_ref, inverse_ref,
+    normed_refs, moment_ref, x_sems, cot_sems, table_sems, mixed_sems, gate_sems, last_sems,
 ):
     rows, width = x_ref.shape
-    size = normed_ref.shape[1]
+    size = normed_refs.shape[2]
     pieces = x_sems.shape[0]
     part = width // pieces
 
@@ -148,21 +151,29 @@
     for copy in x_copies + table_copies + cot_copies:
         copy.start()
 
-    normed_ref[0:8] = jnp.zeros((8, size), F32)
+    for n in range(normed_refs.shape[0]):
+        normed_refs[n, 0:8] = jnp.zeros((8, size), F32)
     total = jnp.zeros((rows, LANES), F32)
     for p in range(pieces):
         x_copies[p].wait()
 
         def square(i, total):
-            x = x_ref[:, group_of(p * (part // size) + i, size)].astype(F32)
-            return total + lane_sums(x * x)
-
-        total = lax.fori_loop(0, part // size, square, total)
+            x = x_ref[:, group_of(p * (part // LANES) + i)].astype(F32)
+            return total + x * x
+
+        total = lax.fori_loop(0, part // LANES, square, total, unroll=4)
     inverse_ref[...] = jnp.broadcast_to(row_scale(total, width), (rows, LANES))
     for copy in table_copies:
         copy.wait()
 
-    def group(i, carry):
+    lane = lax.broadcasted_iota(jnp.int32, (1, LANES), 1)
+    scale = jnp.zeros((1, LANES), F32)
+    for n, row in enumerate((0, 1, rows - 2, rows - 1)):
+        scale = jnp.where(lane == n, inverse_ref[row : row + 1], scale)
+    scale_high = scale.astype(BF16).astype(F32)
+    scales = jnp.concatenate([scale_high, scale - scale_high], axis=0)
+
+    def group(i, normed_ref):
         cols = group_of(i, size)
         now = x_ref[:, cols].astype(F32) * wide(inverse_ref[...], size)
         normed_ref[8 : rows + 8] = now
@@ -170,19 +181,26 @@
         older = normed_ref[6 : rows + 6]
         query, key, value = filtered(taps_of(taps_ref, gain_ref, cols), now, past, older)
         kept = lax.broadcasted_iota(jnp.int32, (16, size), 0) >= 2
-        signals = []
         for signal, out_ref in ((key * value, mixed_ref), (cot_ref[:, cols].astype(F32) * query, gate_ref)):
             head = jnp.where(kept, signal[0:16], 0.0)
-            signal = jnp.concatenate([head, signal[16:]], axis=0).astype(BF16)
-            out_ref[:, cols] = signal
-            signals.append(signal)
-        both = jnp.dot(moments_ref[...], jnp.concatenate(signals, axis=0), preferred_element_type=F32)
+            out_ref[:, cols] = jnp.concatenate([head, signal[16:]], axis=0).astype(BF16)
+
+    together = normed_refs.shape[0]
+
+    def groups(i, carry):
+        for n in range(together):
+            group(i * together + n, normed_refs.at[n])
+        return carry
+
+    def gather(p):
+        cols = pl.ds(p * part, part)
+        signals = jnp.concatenate([mixed_ref[:, cols], gate_ref[:, cols]], axis=0)
+        both = jnp.dot(moments_ref[...], signals, preferred_element_type=F32)
         for side in range(2):
             high = 2 * PADDED * side
             moment_ref[PADDED * side : PADDED * (side + 1), cols] = (
                 both[high : high + PADDED] + both[high + PADDED : high + 2 * PADDED]
             )
-        return carry
 
     def project(i, carry):
         cols = group_of(i)
@@ -194,8 +212,6 @@
                 states[side] + power * moment_ref[PADDED * side + k : PADDED * side + k + 1, cols]
                 for side in range(2)
             ]
-        for side in range(2):
-            state_ref[MODES * side : MODES * (side + 1), cols] = states[side]
         x_head = x_ref[0:16, cols].astype(F32)
         x_tail = x_ref[rows - 16 : rows, cols].astype(F32)
         cot_head = cot_ref[0:16, cols].astype(F32)
@@ -204,31 +220,26 @@
         ).astype(BF16)
         return carry
 
-    lane = lax.broadcasted_iota(jnp.int32, (1, LANES), 1)
-    scale = jnp.zeros((1, LANES), F32)
-    for n, row in enumerate((0, 1, rows - 2, rows - 1)):
-        scale = jnp.where(lane == n, inverse_ref[row : row + 1], scale)
-    scale_high = scale.astype(BF16).astype(F32)
-    scales = jnp.concatenate([scale_high, scale - scale_high], axis=0)
-
     out_copies = []
     for p in range(pieces):
         cot_copies[p].wait()
-        lax.fori_loop(p * (part // size), (p + 1) * (part // size), group, 0)
+        steps = part // size // together
+        lax.fori_loop(p * steps, (p + 1) * steps, groups, 0)
         out_copies += [
             pltpu.make_async_copy(mixed_ref.at[piece(p)], mixed_hbm.at[piece(p)], mixed_sems.at[p]),
             pltpu.make_async_copy(gate_ref.at[piece(p)], gate_hbm.at[piece(p)], gate_sems.at[p]),
         ]
         for copy in out_copies[-2:]:
             copy.start()
-    lax.fori_loop(0, width // LANES, project, 0, unroll=2)
+        gather(p)
+        lax.fori_loop(p * (part // LANES), (p + 1) * (part // LANES), project, 0, unroll=PROJECT_UNROLL)
     out_copies += [
         pltpu.make_async_copy(source, target, last_sems.at[n])
         for n, (source, target) in enumerate(
-            ((packet_ref, packet_hbm), (state_ref, state_hbm), (inverse_ref, inverse_hbm))
+            ((packet_ref, packet_hbm), (inverse_ref, inverse_hbm))
         )
     ]
-    for copy in out_copies[-3:]:
+    for copy in out_copies[-2:]:
         copy.start()
     for copy in out_copies:
         copy.wait()
@@ -244,26 +255,40 @@
     def group(i, carry):
         cols = group_of(i, size)
         rates = rates_ref[:, cols]
-        nodal = nodal_sum(rates, coefs_of(rates, residue_ref[:, cols]), places_ref[...]).astype(BF16)
-        signal = signal_ref[:, cols]
+        nodal = nodal_sum(rates, coefs_of(rates, residue_ref[:, cols]), places_ref[...])
+        signal = signal_ref[:, cols].astype(F32)
         for k in range(NODES):
-            parts_ref[k * rows : (k + 1) * rows] = signal * nodal[k : k + 1]
+            parts_ref[k * rows : (k + 1) * rows] = (signal * nodal[k : k + 1]).astype(BF16)
         out_ref[:, cols] = (
             jnp.dot(near_ref[0], parts_ref[...], preferred_element_type=F32)
-            + skip_ref[:, cols] * signal.astype(F32)
+            + skip_ref[:, cols] * signal
         )
         return carry
 
     lax.fori_loop(0, signal_ref.shape[1] // size, group, 0)
 
 
-def scan_kernel(rates_ref, gain_ref, taps_ref, packet_ref, mark_ref, enter_ref, done_ref, wide_ref, row_ref, *, rows):
+def over(block):
+    return jnp.sum(block, axis=0, keepdims=True)
+
+
+def scan_kernel(
+    rates_ref, residue_ref, skip_ref, gain_ref, taps_ref, places_ref, packet_ref, mark_ref, enter_ref, done_ref,
+    wide_ref, row_ref, base_ref, column_ref, *, rows,
+):
     done_ref[...] = jnp.zeros_like(done_ref)
     count = packet_ref.shape[0]
-    first = lax.axis_index("seq") * LANES
-    cols = pl.ds(pl.multiple_of(first, LANES), LANES)
+    cols = pl.ds(pl.multiple_of(lax.axis_index("seq") * LANES, LANES), LANES)
     rates = rates_ref[:, cols]
+    skip = skip_ref[:, cols]
     taps = taps_of(taps_ref, gain_ref, cols)
+    coef = coefs_of(rates, residue_ref[:, cols])
+    fall = jnp.exp(-rates)
+    rise = jnp.exp(rates)
+    now, later, earlier = over(coef), over(coef * fall), over(coef * rise)
+    places = places_ref[...]
+    for r in range(MODES):
+        column_ref[r] = jnp.exp(-rates[r : r + 1] * places)
     for d in range(count):
         wide_ref[d * PACKET : (d + 1) * PACKET] = packet_ref[d].astype(F32)
     x_0, x_1, x_2, x_3, cot_0, cot_1, high, low = [
@@ -271,8 +296,7 @@
     ]
     scale = high + low
     n_0, n_1, n_2, n_3 = [
-        x * jnp.broadcast_to(scale[:, n : n + 1], (count, LANES))
-        for n, x in enumerate((x_0, x_1, x_2, x_3))
+        x * jnp.broadcast_to(scale[:, n : n + 1], (count, LANES)) for n, x in enumerate((x_0, x_1, x_2, x_3))
     ]
     zero = jnp.zeros((1, LANES), F32)
 
@@ -285,99 +309,90 @@
     n_2, n_3 = before(n_2), before(n_3)
     query_0, key_0, value_0 = filtered(taps, n_0, n_3, n_2)
     query_1, key_1, value_1 = filtered(taps, n_1, n_0, n_3)
-    heads = (key_0 * value_0, key_1 * value_1, cot_0 * query_0, cot_1 * query_1)
-    edges = (before(x_2), before(x_3), after(x_0), after(x_1), after(cot_0), after(cot_1))
-    for n, block in enumerate(heads):
-        row_ref[n] = block.astype(BF16).astype(F32)
-    for n, block in enumerate(edges):
-        row_ref[len(heads) + n] = block
-
-    decay = jnp.exp(rates * (-float(rows)))
-    lead_0 = jnp.exp(rates * (1.0 - rows))
-    lead_1 = jnp.exp(rates * (2.0 - rows))
-    decay_1 = jnp.exp(-rates)
-    ahead = jnp.zeros((MODES, LANES), F32)
-    back = jnp.zeros((MODES, LANES), F32)
-    backs = [None] * count
-    for d in reversed(range(count)):
-        backs[d] = back
-        own = wide_ref[d * PACKET + MODES : d * PACKET + 2 * MODES]
-        back = decay * back + (own + row_ref[2, d : d + 1] + decay_1 * row_ref[3, d : d + 1])
-    for d in range(count):
-        extra = [row_ref[len(heads) + n, d : d + 1] for n in range(6)]
-        enter_ref[d] = jnp.concatenate([ahead, backs[d]] + extra + [zero, zero], axis=0).astype(BF16)
-        own = wide_ref[d * PACKET : d * PACKET + MODES]
-        ahead = decay * ahead + (own + lead_0 * row_ref[0, d : d + 1] + lead_1 * row_ref[1, d : d + 1])
-
-
-def over(block):
-    return jnp.sum(block, axis=0, keepdims=True)
-
-
-def entered_of(enter_ref, i, size, side):
-    pieces = size // LANES
-    return jnp.concatenate(
-        [enter_ref[i * pieces + h, MODES * side : MODES * (side + 1)].astype(F32) for h in range(pieces)], axis=1
-    )
-
-
-def fill_part(
-    i, size, x_ref, cot_ref, inverse_ref, gain_ref, taps_ref, rates_ref, residue_ref, skip_ref, places_ref, enter_ref,
-    edge_ref, edge_scale, small_ref, nodal_ref, patch_ref, mixed_ref,
-):
-    cols = group_of(i, size)
-    skip = skip_ref[:, cols]
-    small_ref[6:8] = edge_ref[0:2, cols] * edge_scale[0:2]
-    small_ref[8:16] = x_ref[:, cols].astype(F32)[0:8] * wide(inverse_ref[0:8], size)
-    query, key, value = filtered(taps_of(taps_ref, gain_ref, cols), small_ref[8:16], small_ref[7:15], small_ref[6:14])
-    mixed = (key * value).astype(BF16).astype(F32)
-    gate = (cot_ref[:, cols].astype(F32)[0:8] * query).astype(BF16).astype(F32)
-    mixed_ref[:, cols] = mixed
-    mixed_0, mixed_1 = mixed[0:1], mixed[1:2]
-    gate_0, gate_1 = gate[0:1], gate[1:2]
-
-    rates = rates_ref[:, cols]
-    coef = coefs_of(rates, residue_ref[:, cols])
-    decay = jnp.exp(-rates)
-    rise = jnp.exp(rates)
-    now, later, earlier = over(coef), over(coef * decay), over(coef * rise)
-    patches = (
+    mixed_0, mixed_1, gate_0, gate_1 = [
+        block.astype(BF16).astype(F32)
+        for block in (key_0 * value_0, key_1 * value_1, cot_0 * query_0, cot_1 * query_1)
+    ]
+    rows_kept = (
+        mixed_0,
+        mixed_1,
+        gate_0,
+        gate_1,
         skip * mixed_0 - earlier * mixed_1,
         skip * mixed_1,
         (now + skip) * gate_0 + later * gate_1,
         (now + skip) * gate_1,
     )
-    zeros = jnp.zeros((6, size), F32)
-    patch_ref[0:8, cols] = jnp.concatenate([patches[0], patches[1], zeros], axis=0)
-    patch_ref[8:16, cols] = jnp.concatenate([patches[2], patches[3], zeros], axis=0)
-
-    weights = [
-        coef * (decay * entered_of(enter_ref, i, size, 0) + mixed_0 + rise * mixed_1),
-        coef * decay * entered_of(enter_ref, i, size, 1),
-    ]
-    places = wide(places_ref[...], size)
-    nodals = [0.0, 0.0]
-    for r in range(MODES):
-        column = jnp.exp(-rates[r : r + 1] * places)
-        nodals = [nodals[side] + column * weights[side][r : r + 1] for side in range(2)]
-    for side in range(2):
-        high = nodals[side].astype(BF16)
-        low = (nodals[side] - high.astype(F32)).astype(BF16)
-        nodal_ref[side, :, cols] = jnp.concatenate([high, high, low], axis=0)
+    for n, block in enumerate(rows_kept):
+        row_ref[n] = block
+
+    decay = jnp.exp(rates * (-float(rows)))
+    lead_0 = jnp.exp(rates * (1.0 - rows))
+    lead_1 = jnp.exp(rates * (2.0 - rows))
+
+    def spread(weight):
+        total = column_ref[0] * weight[0:1]
+        for r in range(1, MODES):
+            total = total + column_ref[r] * weight[r : r + 1]
+        return total[0:NODES]
+
+    ahead = jnp.zeros((MODES, LANES), F32)
+    back = jnp.zeros((MODES, LANES), F32)
+    for step in range(count):
+        d = step
+        reached = coef * fall * ahead
+        base_ref[0, d : d + 1] = over(reached)
+        base_ref[1, d : d + 1] = over(reached * fall)
+        nodal = spread(reached + coef * (row_ref[0, d : d + 1] + rise * row_ref[1, d : d + 1]))
+        own = wide_ref[d * PACKET : d * PACKET + MODES]
+        wide_ref[d * PACKET : d * PACKET + PADDED] = jnp.concatenate(
+            [nodal, row_ref[4, d : d + 1], row_ref[5, d : d + 1]], axis=0
+        )
+        ahead = decay * ahead + (own + lead_0 * row_ref[0, d : d + 1] + lead_1 * row_ref[1, d : d + 1])
+
+        d = count - 1 - step
+        nodal = spread(coef * fall * back)
+        back = decay * back + wide_ref[d * PACKET + MODES : d * PACKET + 2 * MODES]
+        wide_ref[d * PACKET + PADDED : d * PACKET + 2 * PADDED] = jnp.concatenate(
+            [nodal, row_ref[6, d : d + 1], row_ref[7, d : d + 1]], axis=0
+        )
+        reached = coef * back
+        base_ref[2, d : d + 1] = over(reached)
+        base_ref[3, d : d + 1] = over(reached * rise)
+        back = back + row_ref[2, d : d + 1] + fall * row_ref[3, d : d + 1]
+
+    conv_0 = base_ref[0] + (now + skip) * mixed_0
+    conv_1 = base_ref[1] + later * mixed_0 + (now + skip) * mixed_1
+    back_0 = base_ref[2] + row_ref[6]
+    back_1 = base_ref[3] + row_ref[7]
+    conv_0, conv_1, back_0, back_1 = [block.astype(BF16).astype(F32) for block in (conv_0, conv_1, back_0, back_1)]
+    grads_0 = (cot_0 * conv_0, back_0 * value_0, back_0 * key_0)
+    grads_1 = (cot_1 * conv_1, back_1 * value_1, back_1 * key_1)
+    edges = (
+        before(x_2),
+        before(x_3),
+        after(sum(taps[j][1] * grads_0[j] for j in range(3))),
+        after(sum(taps[j][2] * grads_0[j] for j in range(3))),
+        after(sum(taps[j][2] * grads_1[j] for j in range(3))),
+    )
+    for n, block in enumerate(edges):
+        row_ref[n] = block
+    unused = jnp.zeros((PACKET - EXTRA - len(edges), LANES), F32)
+    for d in range(count):
+        extra = [row_ref[n, d : d + 1] for n in range(len(edges))]
+        wide_ref[d * PACKET + EXTRA : (d + 1) * PACKET] = jnp.concatenate(extra + [unused], axis=0)
+        enter_ref[d] = wide_ref[d * PACKET : (d + 1) * PACKET].astype(BF16)
 
 
 def finish_kernel(
     rows, first, count, x_hbm, cot_hbm, ahead_hbm, back_hbm, inverse_ref, gain_ref, taps_ref, spread_ref, enter_ref,
-    residue_ref, rates_ref, skip_ref, *refs,
+    *refs,
 ):
     low = first == 0
     if low:
-        (
-            places_ref, layer_ref, grad_ref, nodal_ref, edge_ref, mixed_ref,
-            head_x_ref, head_cot_ref, head_sems, small_ref, patch_ref, *refs,
-        ) = refs
+        layer_ref, grad_ref, edge_ref, *refs = refs
     else:
-        state_ref, nodal_ref, edge_ref, mixed_ref, layer_ref, grad_ref, *refs = refs
+        edge_ref, layer_ref, grad_ref, *refs = refs
     (
         x_ref, cot_ref, ahead_ref, back_ref, base_ref, normed_refs, one_refs, two_refs, total_ref, load_sems,
     ) = refs
@@ -392,13 +407,6 @@
     def lanes(p):
         return pl.ds(p * part, part)
 
-    if low:
-        heads = [
-            pltpu.make_async_copy(source.at[pl.ds(0, 16)], target, head_sems.at[n])
-            for n, (source, target) in enumerate(((x_hbm, head_x_ref), (cot_hbm, head_cot_ref)))
-        ]
-        for copy in heads:
-            copy.start()
     loads = []
     for p in range(pieces):
         loads.append([
@@ -424,22 +432,10 @@
 
         total = lax.fori_loop(0, width // LANES, edges, jnp.zeros((8, LANES), F32), unroll=4)
         edge_ref[8:16, 0:LANES] = jnp.broadcast_to(row_scale(total, width), (8, LANES))
-        for copy in heads:
-            copy.wait()
-        fill_size = small_ref.shape[1]
-        fill_scale = wide(edge_ref[8:16, 0:LANES], fill_size)
-
-        def fill(i, carry):
-            fill_part(
-                i, fill_size, head_x_ref, head_cot_ref, inverse_ref, gain_ref, taps_ref, rates_ref, residue_ref,
-                skip_ref, places_ref, enter_ref, edge_ref, fill_scale, small_ref, nodal_ref, patch_ref, mixed_ref,
-            )
-            return carry
-
-        lax.fori_loop(0, width // fill_size, fill, 0)
 
     edge_scale = wide(edge_ref[8:16, 0:LANES], size)
     inverse = wide(inverse_ref[first : first + reach], size)
+    blocks = size // LANES
 
     def group(i, normed_ref, one_ref, two_ref):
         cols = group_of(i, size)
@@ -459,14 +455,15 @@
 
         convs = []
         for side, near_ref in enumerate((ahead_ref, back_ref)):
+            nodal = jnp.concatenate(
+                [enter_ref[i * blocks + h, PADDED * side : PADDED * (side + 1)] for h in range(blocks)], axis=1
+            )
             far = jnp.dot(
-                spread_ref[side * rows + first : side * rows + first + reach],
-                nodal_ref[side, :, cols],
+                spread_ref[side * rows + first : side * rows + first + cot_ref.shape[0]],
+                jnp.concatenate([nodal, nodal], axis=0),
                 preferred_element_type=F32,
             )
-            total = near_ref[:, cols] + far
-            if low:
-                total = jnp.concatenate([total[0:8] + patch_ref[8 * side : 8 * side + 8, cols], total[8:]], axis=0)
+            total = near_ref[:, cols] + far[0:reach]
             convs.append(total.astype(BF16).astype(F32))
         conv, conv_back = convs
         layer_ref[:, cols] = (x[0:count] + query[0:count] * conv[0:count]).astype(BF16)
@@ -476,40 +473,8 @@
         one_ref[0:reach] = lagged[1]
         two_ref[0:reach] = lagged[2]
         if not low:
-            normed_ref[count + 16 : count + 18] = edge_ref[2:4, cols] * edge_scale[2:4]
-            n_query, n_key, n_value = filtered(
-                taps,
-                normed_ref[count + 16 : count + 18],
-                normed_ref[count + 15 : count + 17],
-                normed_ref[count + 14 : count + 16],
-            )
-            n_cot = edge_ref[4:6, cols]
-            n_mixed = (n_key * n_value).astype(BF16).astype(F32)
-            n_gate = (n_cot * n_query).astype(BF16).astype(F32)
-            rates = rates_ref[:, cols]
-            coef = coefs_of(rates, residue_ref[:, cols])
-            decay = jnp.exp(-rates)
-            lead = coef * decay
-            skip = skip_ref[:, cols]
-            entered = [entered_of(enter_ref, i, size, side) for side in range(2)]
-            own = (
-                state_ref[0:MODES, cols]
-                + jnp.exp(rates * (1.0 - rows)) * mixed_ref[0:1, cols]
-                + jnp.exp(rates * (2.0 - rows)) * mixed_ref[1:2, cols]
-            )
-            leave = jnp.exp(rates * (-float(rows))) * entered[0] + own
-            direct = over(coef) + skip
-            mixed_0, mixed_1 = n_mixed[0:1], n_mixed[1:2]
-            gate_0, gate_1 = n_gate[0:1], n_gate[1:2]
-            conv_0 = over(lead * leave) + direct * mixed_0
-            conv_1 = over(lead * decay * leave) + over(lead) * mixed_0 + direct * mixed_1
-            back_0 = over(coef * entered[1]) + skip * gate_0
-            back_1 = over(coef * (1.0 / decay) * (entered[1] - gate_0)) + skip * gate_1
-            n_conv = jnp.concatenate([conv_0, conv_1], axis=0).astype(BF16).astype(F32)
-            n_back = jnp.concatenate([back_0, back_1], axis=0).astype(BF16).astype(F32)
-            n_grads = (n_cot * n_conv, n_back * n_value, n_back * n_key)
-            one_ref[count : count + 2] = sum(taps[j][1] * n_grads[j] for j in range(3))
-            two_ref[count : count + 2] = sum(taps[j][2] * n_grads[j] for j in range(3))
+            one_ref[count : count + 1] = edge_ref[2:3, cols]
+            two_ref[count : count + 2] = edge_ref[3:5, cols]
         scaled = lagged[0][0:count] + one_ref[1 : count + 1] + two_ref[2 : count + 2]
         base_ref[:, cols] = cot[0:count] + inverse[0:count] * scaled
         return lane_sums(scaled * x[0:count])
@@ -593,7 +558,6 @@
         (x.shape, BF16),
         (x.shape, BF16),
         ((width // LANES, PACKET, LANES), BF16),
-        ((2 * MODES, width), F32),
         ((rows, LANES), F32),
     ]
     ins = (x, cot, gain, taps, rates, moments)
@@ -606,14 +570,14 @@
         scratch_shapes=[pltpu.VMEM(array.shape, array.dtype) for array in held]
         + [pltpu.VMEM(*out) for out in outs]
         + [
-            pltpu.VMEM((rows + 8, min(START_GROUP, width // pieces)), F32),
+            pltpu.VMEM((min(START_TOGETHER, width // pieces // START_GROUP), rows + 8, START_GROUP), F32),
             pltpu.VMEM((2 * PADDED, width), F32),
             pltpu.SemaphoreType.DMA((pieces,)),
             pltpu.SemaphoreType.DMA((pieces,)),
             pltpu.SemaphoreType.DMA((4,)),
             pltpu.SemaphoreType.DMA((pieces,)),
             pltpu.SemaphoreType.DMA((pieces,)),
-            pltpu.SemaphoreType.DMA((3,)),
+            pltpu.SemaphoreType.DMA((2,)),
         ],
         compiler_params=params(24),
         cost_estimate=takes(6),
@@ -643,18 +607,21 @@
     )(stay(signal), rates, residue, places, skip, stay(near), mark)
 
 
-def scan_call(rates, gain, taps, gathered, mark, rows):
+def scan_call(rates, residue, skip, gain, taps, places, gathered, mark, rows):
+    count = gathered.shape[0]
     return pl.pallas_call(
         functools.partial(scan_kernel, rows=rows),
         out_shape=[shape(gathered.shape, BF16), shape((8, LANES), F32)],
         scratch_shapes=[
-            pltpu.VMEM((gathered.shape[0] * PACKET, LANES), F32),
-            pltpu.VMEM((10, gathered.shape[0], LANES), F32),
+            pltpu.VMEM((count * PACKET, LANES), F32),
+            pltpu.VMEM((8, count, LANES), F32),
+            pltpu.VMEM((4, count, LANES), F32),
+            pltpu.VMEM((MODES, PADDED, LANES), F32),
         ],
-        compiler_params=params(6),
-        cost_estimate=takes(1),
+        compiler_params=params(8),
+        cost_estimate=takes(2),
         name="scan",
-    )(rates, gain, taps, gathered, mark)
+    )(rates, residue, skip, gain, taps, places, gathered, mark)
 
 
 def finish_call(rows, first, count, *arrays):
@@ -664,29 +631,19 @@
     pieces = PIECES
     size = min(FINISH_GROUP, width)
     together = min(FINISH_TOGETHER, width // pieces // size)
-    fill_size = min(FILL_GROUP, width)
     far = pl.BlockSpec(memory_space=pltpu.HBM)
     near = pl.BlockSpec(memory_space=pltpu.VMEM)
     half = shape((count, width), BF16)
     out_shape = [half, half]
-    scratch = []
     above, below, reach = (0, 16, count + 8) if low else (16, 0, count)
     if low:
-        out_shape += [shape((2, 3 * PADDED, width), BF16), shape((16, width), F32), shape((8, width), F32)]
-        scratch = [
-            pltpu.VMEM((16, width), BF16),
-            pltpu.VMEM((16, width), BF16),
-            pltpu.SemaphoreType.DMA((2,)),
-            pltpu.VMEM((16, fill_size), F32),
-            pltpu.VMEM((16, width), F32),
-        ]
+        out_shape += [shape((16, width), F32)]
     return pl.pallas_call(
         functools.partial(finish_kernel, rows, first, count),
         in_specs=[far] * 4 + [near] * (len(arrays) - 4),
         out_specs=[near] * len(out_shape),
         out_shape=out_shape,
-        scratch_shapes=scratch
-        + [
+        scratch_shapes=[
             pltpu.VMEM((above + count + below, width), BF16),
             pltpu.VMEM((count + below, width), BF16),
             pltpu.VMEM((reach, width), F32),
@@ -730,19 +687,19 @@
     fixed = {name: jnp.asarray(table) for name, table in constants(rows).items()}
 
     weights = residue[0]
-    mixed, gate, packet, state, inverse = start_call(x, cot, norm_gain, taps, rates, fixed["moments"])
+    mixed, gate, packet, inverse = start_call(x, cot, norm_gain, taps, rates, fixed["moments"])
     gathered = lax.all_to_all(packet, "seq", split_axis=0, concat_axis=0, tiled=True)
     near = (rates, weights, fixed["places"], skip_gain, fixed["near"])
     ahead, mark = near_call(0, mixed, *near, stay(inverse))
-    entering, mark = scan_call(rates, norm_gain, taps, gathered, mark, rows)
+    entering, mark = scan_call(rates, weights, skip_gain, norm_gain, taps, fixed["places"], gathered, mark, rows)
     enter = lax.all_to_all(entering, "seq", split_axis=0, concat_axis=0, tiled=True)
     back, mark = near_call(1, gate, *near, mark)
 
-    common = (x, cot, ahead, back, inverse, norm_gain, taps, fixed["spread"], enter, weights, rates, skip_gain)
-    layer, grad, *passed = finish_call(rows, 0, SPLIT, *common, fixed["places"])
+    common = (x, cot, ahead, back, inverse, norm_gain, taps, fixed["spread"], enter)
+    layer, grad, edge = finish_call(rows, 0, SPLIT, *common)
     on_low = shifted(layer, "section", 1)
     back_low = shifted(grad, "section", -1)
-    layer, grad = finish_call(rows, SPLIT, rows - SPLIT, *common, state, *passed)
+    layer, grad = finish_call(rows, SPLIT, rows - SPLIT, *common, edge)
     on_high = shifted(layer, "section", 1)
     back_high = shifted(grad, "section", -1)
     joined = join_call(rows, 0, on_low, back_low)

time: 82.2 us -> 79.7 us (0.970)
  Pallas kernels: 34.4 us -> 31.7 us
    pallas_call x2, Pallas kernels: 12.8 us -> 8.93 us  [finish_call(): pl.pallas_call(functools.partial(finish_kernel, rows, first, count), in_s...]
    ppermute x4, waiting for transfers between devices: 13.6 us -> 14.6 us  [shifted(): return lax.ppermute(block, axis, route)]
    pallas_call x1, Pallas kernels: 1 us -> 1.94 us  [scan_call(): pl.pallas_call(functools.partial(scan_kernel, rows=rows), out_shape=[shap...]
    pallas_call x2, Pallas kernels: 11.6 us -> 12.5 us  [near_call(): pl.pallas_call(near_kernel, grid=(width // step,), in_specs=[across(signa...]
  transfers between devices with their start and end apart: 6 -> 6, of which waited for: 6 -> 6; matrix products, arithmetic and copies ran while one was open for 0% -> 0% of each run, Pallas kernels for 21% -> 22%
where the time goes in v4:
time: 79.7 us; the launch traced here: 79.1 us
  Pallas kernels  31.7 us (40%)
  starting transfers between devices  25.6 us (32%)
  waiting for transfers between devices  20.9 us (26%)
  between operations  0.81 us (1%)
    ppermute x4, waiting for transfers between devices, shifted(): return lax.ppermute(block, axis, route)  14.6 us
    ppermute x4, starting transfers between devices, shifted(): return lax.ppermute(block, axis, route)  14 us
    pallas_call x2, Pallas kernels, near_call(): pl.pallas_call(near_kernel, grid=(width // step,), in_specs=[across(signa...  12.5 us
    pallas_call x2, Pallas kernels, finish_call(): pl.pallas_call(functools.partial(finish_kernel, rows, first, count), in_s...  8.93 us
    all_to_all x1, starting transfers between devices, local(): lax.all_to_all(packet, 'seq', split_axis=0, concat_axis=0, tiled=True)  7.33 us
    pallas_call x1, Pallas kernels, start_call(): pl.pallas_call(functools.partial(start_kernel, [float(p) for p in node_pl...  6.4 us
    all_to_all x1, starting transfers between devices, local(): lax.all_to_all(entering, 'seq', split_axis=0, concat_axis=0, tiled=True)  4.28 us
    all_to_all x1, waiting for transfers between devices, local(): lax.all_to_all(entering, 'seq', split_axis=0, concat_axis=0, tiled=True)  3.19 us
  transfers between devices with their start and end apart: 6, of which 6 were waited for; matrix products, arithmetic and copies ran while one was open for 0% of the time, Pallas kernels for 22%

profile of v4, /device:TPU:96, one launch (start us, length us, event | category | flops | bytes accessed | tf_op | source)
XLA Modules:
  0.0 79.1 jit_solution(1768247242709030380)
XLA Ops:
  0.6 0.0 copy-start
  0.6 0.0 copy-start.1
  0.7 0.0 copy-start.3
  0.7 0.0 copy-start.6
  0.7 6.4 %start.1 = (bf16[128,4096]{1,0:T(8,128)(2,1)}, bf16[128,4096]{1,0:T(8,128)(2,1)}, bf16[32,40,128]{2,1,0:T(8,128)(2,1)}, f32[128,128]{1,0:T(8,128)}) custom-call(bf16[128,4096]{1,0:T(8,128)(2,1)} %bitcast.18, bf16[128,4096]{1,0:T(8,128)(2,1)} %bitcast.21, f32[1,4096]{1,0:T(1,128)} %gain_ref.5, f32[3,3,1,4096]{3,2,1,0:T(1,128)} %bitcast.14, ...), custom_call_target="tpu_custom_call" | custom-call | flops 6600000000 | bytes 21000000 | tf_op jit(solution)/shard_map/start/pallas_call | solution.py:565
  7.1 7.3 %all-to-all-start = ((bf16[32,40,128]{2,1,0:T(8,128)(2,1)}), bf16[32,40,128]{2,1,0:T(8,128)(2,1)S(1)}, u32[]{:S(2)}, u32[]{:S(2)}) async-start(bf16[32,40,128]{2,1,0:T(8,128)(2,1)} %get-tuple-element.24), calls=%async_computation | async-start | bytes 655360 | tf_op jit(solution)/shard_map/all_to_all | solution.py:691
  14.4 0.0 copy-done
  14.4 0.0 copy-done.1
  14.4 0.0 copy-done.3
  14.5 0.0 copy-start.2
  14.5 0.0 copy-start.4
  14.5 6.2 %near.2 = (f32[128,4096]{1,0:T(8,128)}, f32[8,128]{1,0:T(8,128)S(1)}) custom-call(bf16[128,4096]{1,0:T(8,128)(2,1)} %get-tuple-element.20.signal_ref, f32[16,4096]{1,0:T(8,128)S(1)} %bitcast.8, f32[16,4096]{1,0:T(8,128)S(1)} %bitcast.11, f32[16,128]{1,0:T(8,128)S(1)} %copy-done.6, f32[1,4096]{1,0:T(1,128)S(1)} %copy-done.3, ...), custom_call_target="tpu_custom_call" | custom-call | flops 4400000000 | bytes 14000000 | tf_op jit(solution)/shard_map/near/pallas_call | solution.py:591
  20.7 3.1 %all-to-all-done.packet_ref = bf16[32,40,128]{2,1,0:T(8,128)(2,1)S(1)} async-done(((bf16[32,40,128]{2,1,0:T(8,128)(2,1)}), bf16[32,40,128]{2,1,0:T(8,128)(2,1)S(1)}, u32[]{:S(2)}, u32[]{:S(2)}) %all-to-all-start) | async-done | bytes 327712 | tf_op jit(solution)/shard_map/all_to_all | solution.py:691
  23.8 0.0 copy-done.2
  23.8 1.9 %scan.1 = (bf16[32,40,128]{2,1,0:T(8,128)(2,1)}, f32[8,128]{1,0:T(8,128)S(1)}) custom-call(f32[16,4096]{1,0:T(8,128)S(1)} %bitcast.9, f32[16,4096]{1,0:T(8,128)S(1)} %bitcast.12, f32[1,4096]{1,0:T(1,128)S(1)} %copy-done.3, f32[1,4096]{1,0:T(1,128)S(1)} %copy-done.4, f32[3,3,1,4096]{3,2,1,0:T(1,128)S(1)} %bitcast.15, f32[16,128]{1,0:T(8,128)S(1)} %copy-done.6, ...), custom_call_target="tpu_custom_call" | custom-call | flops 2200000000 | bytes 7000000 | tf_op jit(solution)/shard_map/scan/pallas_call | solution.py:612
  25.8 4.3 %all-to-all-start.1 = ((bf16[32,40,128]{2,1,0:T(8,128)(2,1)}), bf16[32,40,128]{2,1,0:T(8,128)(2,1)S(1)}, u32[]{:S(2)}, u32[]{:S(2)}) async-start(bf16[32,40,128]{2,1,0:T(8,128)(2,1)} %get-tuple-element.28), calls=%async_computation.1 | async-start | bytes 655360 | tf_op jit(solution)/shard_map/all_to_all | solution.py:695
  30.1 0.0 copy-start.5
  30.1 0.0 copy-start.7
  30.1 6.2 %near.3 = (f32[128,4096]{1,0:T(8,128)}, f32[8,128]{1,0:T(8,128)}) custom-call(bf16[128,4096]{1,0:T(8,128)(2,1)} %get-tuple-element.23.signal_ref, f32[16,4096]{1,0:T(8,128)S(1)} %bitcast.10, f32[16,4096]{1,0:T(8,128)S(1)} %bitcast.13, f32[16,128]{1,0:T(8,128)S(1)} %copy-done.6, f32[1,4096]{1,0:T(1,128)S(1)} %copy-done.3, ...), custom_call_target="tpu_custom_call" | custom-call | flops 4400000000 | bytes 14000000 | tf_op jit(solution)/shard_map/near/pallas_call | solution.py:591
  36.3 3.2 %all-to-all-done.1.enter_ref = bf16[32,40,128]{2,1,0:T(8,128)(2,1)S(1)} async-done(((bf16[32,40,128]{2,1,0:T(8,128)(2,1)}), bf16[32,40,128]{2,1,0:T(8,128)(2,1)S(1)}, u32[]{:S(2)}, u32[]{:S(2)}) %all-to-all-start.1) | async-done | bytes 327712 | tf_op jit(solution)/shard_map/all_to_all | solution.py:695
  39.5 5.3 %finish.2 = (bf16[80,4096]{1,0:T(8,128)(2,1)S(1)}, bf16[80,4096]{1,0:T(8,128)(2,1)S(1)}, f32[16,4096]{1,0:T(8,128)S(1)}) custom-call(bf16[128,4096]{1,0:T(8,128)(2,1)} %bitcast.19, bf16[128,4096]{1,0:T(8,128)(2,1)} %bitcast.22, f32[128,4096]{1,0:T(8,128)} %get-tuple-element.22.ahead_hbm, f32[128,4096]{1,0:T(8,128)} %get-tuple-element.27.back_hbm, ...), custom_call_target="tpu_custom_call" | custom-call | flops 6600000000 | bytes 21000000 | tf_op jit(solution)/shard_map/finish/pallas_call | solution.py:641
  44.8 5.0 %collective-permute-start.2 = (bf16[80,4096]{1,0:T(8,128)(2,1)S(1)}, bf16[80,4096]{1,0:T(8,128)(2,1)S(1)}, u32[]{:S(2)}, u32[]{:S(2)}) collective-permute-start(bf16[80,4096]{1,0:T(8,128)(2,1)S(1)} %get-tuple-element.32), channel_id=1, source_target_pairs={{0,32},{32,64},{64,96},{96,128},{128,160},{160,192},{192,224},{224... | collective-permute-start | bytes 1966088 | tf_op jit(solution)/shard_map/ppermute | solution.py:526
  49.8 1.9 %collective-permute-start.3 = (bf16[80,4096]{1,0:T(8,128)(2,1)S(1)}, bf16[80,4096]{1,0:T(8,128)(2,1)S(1)}, u32[]{:S(2)}, u32[]{:S(2)}) collective-permute-start(bf16[80,4096]{1,0:T(8,128)(2,1)S(1)} %get-tuple-element.33), channel_id=1, source_target_pairs={{32,0},{64,32},{96,64},{128,96},{160,128},{192,160},{224,192},{256... | collective-permute-start | bytes 1966088 | tf_op jit(solution)/shard_map/ppermute | solution.py:526
  51.8 3.6 %finish.3 = (bf16[48,4096]{1,0:T(8,128)(2,1)S(1)}, bf16[48,4096]{1,0:T(8,128)(2,1)S(1)}) custom-call(bf16[128,4096]{1,0:T(8,128)(2,1)} %bitcast.20, bf16[128,4096]{1,0:T(8,128)(2,1)} %bitcast.23, f32[128,4096]{1,0:T(8,128)} %get-tuple-element.22.ahead_hbm, f32[128,4096]{1,0:T(8,128)} %get-tuple-element.27.back_hbm, f32[128,128]{1,0:T(8,128)S(1)} %copy-done.7, ...), custom_call_target="tpu_custom_call" | custom-call | flops 6600000000 | bytes 21000000 | tf_op jit(solution)/shard_map/finish/pallas_call | solution.py:641
  55.4 5.1 %collective-permute-start = (bf16[48,4096]{1,0:T(8,128)(2,1)S(1)}, bf16[48,4096]{1,0:T(8,128)(2,1)S(1)}, u32[]{:S(2)}, u32[]{:S(2)}) collective-permute-start(bf16[48,4096]{1,0:T(8,128)(2,1)S(1)} %get-tuple-element.30), channel_id=1, source_target_pairs={{0,32},{32,64},{64,96},{96,128},{128,160},{160,192},{192,224},{224... | collective-permute-start | bytes 1179656 | tf_op jit(solution)/shard_map/ppermute | solution.py:526
  60.6 1.9 %collective-permute-start.1 = (bf16[48,4096]{1,0:T(8,128)(2,1)S(1)}, bf16[48,4096]{1,0:T(8,128)(2,1)S(1)}, u32[]{:S(2)}, u32[]{:S(2)}) collective-permute-start(bf16[48,4096]{1,0:T(8,128)(2,1)S(1)} %get-tuple-element.31), channel_id=1, source_target_pairs={{32,0},{64,32},{96,64},{128,96},{160,128},{192,160},{224,192},{256... | collective-permute-start | bytes 1179656 | tf_op jit(solution)/shard_map/ppermute | solution.py:526
  62.5 2.4 %collective-permute-done.2.layer_ref = bf16[80,4096]{1,0:T(8,128)(2,1)S(1)} collective-permute-done((bf16[80,4096]{1,0:T(8,128)(2,1)S(1)}, bf16[80,4096]{1,0:T(8,128)(2,1)S(1)}, u32[]{:S(2)}, u32[]{:S(2)}) %collective-permute-start.2) | collective-permute-done | bytes 655392 | tf_op jit(solution)/shard_map/ppermute | solution.py:526
  64.8 5.6 %collective-permute-done.3.grad_ref = bf16[80,4096]{1,0:T(8,128)(2,1)S(1)} collective-permute-done((bf16[80,4096]{1,0:T(8,128)(2,1)S(1)}, bf16[80,4096]{1,0:T(8,128)(2,1)S(1)}, u32[]{:S(2)}, u32[]{:S(2)}) %collective-permute-start.3) | collective-permute-done | bytes 655392 | tf_op jit(solution)/shard_map/ppermute | solution.py:526
  70.5 1.1 %join.2 = (bf16[128,4096]{1,0:T(8,128)(2,1)}, bf16[128,4096]{1,0:T(8,128)(2,1)}) custom-call(bf16[80,4096]{1,0:T(8,128)(2,1)S(1)} %collective-permute-done.2.layer_ref, bf16[80,4096]{1,0:T(8,128)(2,1)S(1)} %collective-permute-done.3.grad_ref), custom_call_target="tpu_custom_call" | custom-call | flops 1100000000 | bytes 3500000 | tf_op jit(solution)/shard_map/join/pallas_call | solution.py:668
  71.6 1.3 %collective-permute-done.layer_ref = bf16[48,4096]{1,0:T(8,128)(2,1)S(1)} collective-permute-done((bf16[48,4096]{1,0:T(8,128)(2,1)S(1)}, bf16[48,4096]{1,0:T(8,128)(2,1)S(1)}, u32[]{:S(2)}, u32[]{:S(2)}) %collective-permute-start) | collective-permute-done | bytes 393248 | tf_op jit(solution)/shard_map/ppermute | solution.py:526
  72.9 5.3 %collective-permute-done.1.grad_ref = bf16[48,4096]{1,0:T(8,128)(2,1)S(1)} collective-permute-done((bf16[48,4096]{1,0:T(8,128)(2,1)S(1)}, bf16[48,4096]{1,0:T(8,128)(2,1)S(1)}, u32[]{:S(2)}, u32[]{:S(2)}) %collective-permute-start.1) | collective-permute-done | bytes 393248 | tf_op jit(solution)/shard_map/ppermute | solution.py:526
  78.2 0.9 %join.3 = (bf16[128,4096]{1,0:T(8,128)(2,1)}, bf16[128,4096]{1,0:T(8,128)(2,1)}) custom-call(bf16[48,4096]{1,0:T(8,128)(2,1)S(1)} %collective-permute-done.layer_ref, bf16[48,4096]{1,0:T(8,128)(2,1)S(1)} %collective-permute-done.1.grad_ref, bf16[128,4096]{1,0:T(8,128)(2,1)} %get-tuple-element.34.refs_0_, ...), custom_call_target="tpu_custom_call", output_to_operand_aliasing={{0}: (2, {}), {1}: (3, {})} | custom-call | flops 1100000000 | bytes 3500000 | tf_op jit(solution)/shard_map/join/pallas_call | solution.py:668
  (4 shorter events, 0.0 us)
Async XLA Ops:
  0.6 13.8 %copy-start = (f32[1,16,4096]{2,1,0:T(8,128)S(1)}, f32[1,16,4096]{2,1,0:T(8,128)}, u32[]{:S(2)}) copy-start(f32[1,16,4096]{2,1,0:T(8,128)} %param.15) | copy-start | bytes 786436
  0.6 13.8 %copy-start.1 = (f32[1,16,4096]{2,1,0:T(8,128)S(1)}, f32[1,16,4096]{2,1,0:T(8,128)}, u32[]{:S(2)}) copy-start(f32[1,16,4096]{2,1,0:T(8,128)} %param.16) | copy-start | bytes 786436
  0.7 13.8 %copy-start.3 = (f32[1,4096]{1,0:T(1,128)S(1)}, f32[1,4096]{1,0:T(1,128)}, u32[]{:S(2)}) copy-start(f32[1,4096]{1,0:T(1,128)} %skip_ref.5) | copy-start | bytes 49156
  0.7 13.8 %copy-start.6 = (f32[16,128]{1,0:T(8,128)S(1)}, f32[16,128]{1,0:T(8,128)}, u32[]{:S(2)}) copy-start(f32[16,128]{1,0:T(8,128)} %constant.11.clone.places_ref) | copy-start | bytes 24580
  7.1 16.8 %all-to-all-start = ((bf16[32,40,128]{2,1,0:T(8,128)(2,1)}), bf16[32,40,128]{2,1,0:T(8,128)(2,1)S(1)}, u32[]{:S(2)}, u32[]{:S(2)}) async-start(bf16[32,40,128]{2,1,0:T(8,128)(2,1)} %get-tuple-element.24), calls=%async_computation | async-start | bytes 655360 | tf_op jit(solution)/shard_map/all_to_all | solution.py:691
  14.5 9.4 %copy-start.2 = (f32[1,3,3,4096]{3,0,2,1:T(1,128)S(1)}, f32[1,3,3,4096]{3,0,2,1:T(1,128)}, u32[]{:S(2)}) copy-start(f32[1,3,3,4096]{3,0,2,1:T(1,128)} %param.14) | copy-start | bytes 442372
  14.5 9.4 %copy-start.4 = (f32[1,4096]{1,0:T(1,128)S(1)}, f32[1,4096]{1,0:T(1,128)}, u32[]{:S(2)}) copy-start(f32[1,4096]{1,0:T(1,128)} %gain_ref.5) | copy-start | bytes 49156
  25.8 13.7 %all-to-all-start.1 = ((bf16[32,40,128]{2,1,0:T(8,128)(2,1)}), bf16[32,40,128]{2,1,0:T(8,128)(2,1)S(1)}, u32[]{:S(2)}, u32[]{:S(2)}) async-start(bf16[32,40,128]{2,1,0:T(8,128)(2,1)} %get-tuple-element.28), calls=%async_computation.1 | async-start | bytes 655360 | tf_op jit(solution)/shard_map/all_to_all | solution.py:695
  30.1 9.4 %copy-start.5 = (bf16[256,32]{1,0:T(8,128)(2,1)S(1)}, bf16[256,32]{1,0:T(8,128)(2,1)}, u32[]{:S(2)}) copy-start(bf16[256,32]{1,0:T(8,128)(2,1)} %constant.9.clone.spread_ref) | copy-start | bytes 49156
  30.1 9.4 %copy-start.7 = (f32[128,128]{1,0:T(8,128)S(1)}, f32[128,128]{1,0:T(8,128)}, u32[]{:S(2)}) copy-start(f32[128,128]{1,0:T(8,128)} %get-tuple-element.21.mark_ref.inverse_ref) | copy-start | bytes 196612
  44.8 20.1 %collective-permute-start.2 = (bf16[80,4096]{1,0:T(8,128)(2,1)S(1)}, bf16[80,4096]{1,0:T(8,128)(2,1)S(1)}, u32[]{:S(2)}, u32[]{:S(2)}) collective-permute-start(bf16[80,4096]{1,0:T(8,128)(2,1)S(1)} %get-tuple-element.32), channel_id=1, source_target_pairs={{0,32},{32,64},{64,96},{96,128},{128,160},{160,192},{192,224},{224... | collective-permute-start | bytes 1966088 | tf_op jit(solution)/shard_map/ppermute | solution.py:526
  49.8 20.7 %collective-permute-start.3 = (bf16[80,4096]{1,0:T(8,128)(2,1)S(1)}, bf16[80,4096]{1,0:T(8,128)(2,1)S(1)}, u32[]{:S(2)}, u32[]{:S(2)}) collective-permute-start(bf16[80,4096]{1,0:T(8,128)(2,1)S(1)} %get-tuple-element.33), channel_id=1, source_target_pairs={{32,0},{64,32},{96,64},{128,96},{160,128},{192,160},{224,192},{256... | collective-permute-start | bytes 1966088 | tf_op jit(solution)/shard_map/ppermute | solution.py:526
  55.4 17.5 %collective-permute-start = (bf16[48,4096]{1,0:T(8,128)(2,1)S(1)}, bf16[48,4096]{1,0:T(8,128)(2,1)S(1)}, u32[]{:S(2)}, u32[]{:S(2)}) collective-permute-start(bf16[48,4096]{1,0:T(8,128)(2,1)S(1)} %get-tuple-element.30), channel_id=1, source_target_pairs={{0,32},{32,64},{64,96},{96,128},{128,160},{160,192},{192,224},{224... | collective-permute-start | bytes 1179656 | tf_op jit(solution)/shard_map/ppermute | solution.py:526
  60.6 17.6 %collective-permute-start.1 = (bf16[48,4096]{1,0:T(8,128)(2,1)S(1)}, bf16[48,4096]{1,0:T(8,128)(2,1)S(1)}, u32[]{:S(2)}, u32[]{:S(2)}) collective-permute-start(bf16[48,4096]{1,0:T(8,128)(2,1)S(1)} %get-tuple-element.31), channel_id=1, source_target_pairs={{32,0},{64,32},{96,64},{128,96},{160,128},{192,160},{224,192},{256... | collective-permute-start | bytes 1179656 | tf_op jit(solution)/shard_map/ppermute | solution.py:526

commit v5 on v4

--- a/solution.py
+++ b/solution.py
@@ -17,9 +17,9 @@
 LANES = 128
 START_GROUP = 128
 START_TOGETHER = 8
-PROJECT_UNROLL = 4
+PROJECT_UNROLL = 8
 PIECES = 4
-SPLIT = 80
+SPLIT = 64
 NEAR_STEP = 1024
 NEAR_GROUP = 1024
 FINISH_GROUP = 128
@@ -390,9 +390,9 @@
 ):
     low = first == 0
     if low:
-        layer_ref, grad_ref, edge_ref, *refs = refs
+        grad_ref, layer_ref, edge_ref, *refs = refs
     else:
-        edge_ref, layer_ref, grad_ref, *refs = refs
+        edge_ref, grad_ref, layer_ref, *refs = refs
     (
         x_ref, cot_ref, ahead_ref, back_ref, base_ref, normed_refs, one_refs, two_refs, total_ref, load_sems,
     ) = refs
@@ -503,12 +503,12 @@
     lax.fori_loop(0, width // LANES, emit, 0, unroll=4)
 
 
-def join_kernel(first, layer_ref, grad_ref, *refs):
-    layer_hbm, grad_hbm, sems = refs[-3:]
+def join_kernel(first, grad_ref, layer_ref, *refs):
+    grad_hbm, layer_hbm, sems = refs[-3:]
     count = layer_ref.shape[0]
     half = layer_ref.shape[1] // 2
     copies = []
-    for n, (source, target) in enumerate(((layer_ref, layer_hbm), (grad_ref, grad_hbm))):
+    for n, (source, target) in enumerate(((grad_ref, grad_hbm), (layer_ref, layer_hbm))):
         for h in range(2):
             lanes = pl.ds(h * half, half)
             copies.append(
@@ -661,7 +661,7 @@
     )(*[stay(array) for array in arrays[:4]], *arrays[4:])
 
 
-def join_call(rows, first, layer, grad, *wholes):
+def join_call(rows, first, grad, layer, *wholes):
     far = pl.BlockSpec(memory_space=pltpu.HBM)
     near = pl.BlockSpec(memory_space=pltpu.VMEM)
     out = shape((rows, layer.shape[1]), BF16)
@@ -675,7 +675,7 @@
         compiler_params=params(4),
         cost_estimate=takes(1),
         name="join",
-    )(layer, grad, *wholes)
+    )(grad, layer, *wholes)
 
 
 def local(section_input, cotangent, norm_gain, short_filter, decay_rate, residue, skip_gain):
@@ -696,14 +696,14 @@
     back, mark = near_call(1, gate, *near, mark)
 
     common = (x, cot, ahead, back, inverse, norm_gain, taps, fixed["spread"], enter)
-    layer, grad, edge = finish_call(rows, 0, SPLIT, *common)
+    grad, layer, edge = finish_call(rows, 0, SPLIT, *common)
+    back_low = shifted(grad, "section", -1)
     on_low = shifted(layer, "section", 1)
-    back_low = shifted(grad, "section", -1)
-    layer, grad = finish_call(rows, SPLIT, rows - SPLIT, *common, edge)
+    grad, layer = finish_call(rows, SPLIT, rows - SPLIT, *common, edge)
+    back_high = shifted(grad, "section", -1)
     on_high = shifted(layer, "section", 1)
-    back_high = shifted(grad, "section", -1)
-    joined = join_call(rows, 0, on_low, back_low)
-    passed_on, passed_back = join_call(rows, SPLIT, on_high, back_high, *joined)
+    joined = join_call(rows, 0, back_low, on_low)
+    passed_back, passed_on = join_call(rows, SPLIT, back_high, on_high, *joined)
     return passed_on[None], passed_back[None]
 
 

time: 79.7 us -> 77.8 us (0.976)
  the two profiles are of different devices: /device:TPU:96 before, /device:TPU:384 now
where the time goes in v5:
time: 77.8 us; the launch traced here: 77.2 us
  Pallas kernels  31.1 us (40%)
  starting transfers between devices  24.9 us (32%)
  waiting for transfers between devices  20.2 us (26%)
  between operations  0.98 us (1%)
    ppermute x4, waiting for transfers between devices, shifted(): return lax.ppermute(block, axis, route)  13.9 us
    ppermute x4, starting transfers between devices, shifted(): return lax.ppermute(block, axis, route)  13.3 us
    pallas_call x2, Pallas kernels, near_call(): pl.pallas_call(near_kernel, grid=(width // step,), in_specs=[across(signa...  12.5 us
    pallas_call x2, Pallas kernels, finish_call(): pl.pallas_call(functools.partial(finish_kernel, rows, first, count), in_s...  8.94 us
    all_to_all x1, starting transfers between devices, local(): lax.all_to_all(packet, 'seq', split_axis=0, concat_axis=0, tiled=True)  7.33 us
    pallas_call x1, Pallas kernels, start_call(): pl.pallas_call(functools.partial(start_kernel, [float(p) for p in node_pl...  5.82 us
    all_to_all x1, starting transfers between devices, local(): lax.all_to_all(entering, 'seq', split_axis=0, concat_axis=0, tiled=True)  4.29 us
    all_to_all x1, waiting for transfers between devices, local(): lax.all_to_all(entering, 'seq', split_axis=0, concat_axis=0, tiled=True)  3.19 us
  transfers between devices with their start and end apart: 6, of which 5 were waited for; matrix products, arithmetic and copies ran while one was open for 0% of the time, Pallas kernels for 23%

profile of v5, /device:TPU:384, one launch (start us, length us, event | category | flops | bytes accessed | tf_op | source)
XLA Modules:
  0.0 77.2 jit_solution(5050851632792377547)
XLA Ops:
  0.6 0.0 copy-start
  0.6 0.0 copy-start.1
  0.7 0.0 copy-start.3
  0.7 0.0 copy-start.6
  0.7 5.8 %start.1 = (bf16[128,4096]{1,0:T(8,128)(2,1)}, bf16[128,4096]{1,0:T(8,128)(2,1)}, bf16[32,40,128]{2,1,0:T(8,128)(2,1)}, f32[128,128]{1,0:T(8,128)}) custom-call(bf16[128,4096]{1,0:T(8,128)(2,1)} %bitcast.18, bf16[128,4096]{1,0:T(8,128)(2,1)} %bitcast.21, f32[1,4096]{1,0:T(1,128)} %gain_ref.5, f32[3,3,1,4096]{3,2,1,0:T(1,128)} %bitcast.14, ...), custom_call_target="tpu_custom_call" | custom-call | flops 6600000000 | bytes 21000000 | tf_op jit(solution)/shard_map/start/pallas_call | solution.py:565
  6.5 7.3 %all-to-all-start = ((bf16[32,40,128]{2,1,0:T(8,128)(2,1)}), bf16[32,40,128]{2,1,0:T(8,128)(2,1)S(1)}, u32[]{:S(2)}, u32[]{:S(2)}) async-start(bf16[32,40,128]{2,1,0:T(8,128)(2,1)} %get-tuple-element.24), calls=%async_computation | async-start | bytes 655360 | tf_op jit(solution)/shard_map/all_to_all | solution.py:691
  13.8 0.0 copy-done
  13.8 0.0 copy-done.1
  13.9 0.0 copy-done.3
  13.9 0.0 copy-done.6
  13.9 0.0 copy-start.2
  13.9 0.0 copy-start.4
  13.9 6.3 %near.2 = (f32[128,4096]{1,0:T(8,128)}, f32[8,128]{1,0:T(8,128)S(1)}) custom-call(bf16[128,4096]{1,0:T(8,128)(2,1)} %get-tuple-element.20.signal_ref, f32[16,4096]{1,0:T(8,128)S(1)} %bitcast.8, f32[16,4096]{1,0:T(8,128)S(1)} %bitcast.11, f32[16,128]{1,0:T(8,128)S(1)} %copy-done.6, f32[1,4096]{1,0:T(1,128)S(1)} %copy-done.3, ...), custom_call_target="tpu_custom_call" | custom-call | flops 4400000000 | bytes 14000000 | tf_op jit(solution)/shard_map/near/pallas_call | solution.py:591
  20.2 3.1 %all-to-all-done.packet_ref = bf16[32,40,128]{2,1,0:T(8,128)(2,1)S(1)} async-done(((bf16[32,40,128]{2,1,0:T(8,128)(2,1)}), bf16[32,40,128]{2,1,0:T(8,128)(2,1)S(1)}, u32[]{:S(2)}, u32[]{:S(2)}) %all-to-all-start) | async-done | bytes 327712 | tf_op jit(solution)/shard_map/all_to_all | solution.py:691
  23.3 1.9 %scan.1 = (bf16[32,40,128]{2,1,0:T(8,128)(2,1)}, f32[8,128]{1,0:T(8,128)S(1)}) custom-call(f32[16,4096]{1,0:T(8,128)S(1)} %bitcast.9, f32[16,4096]{1,0:T(8,128)S(1)} %bitcast.12, f32[1,4096]{1,0:T(1,128)S(1)} %copy-done.3, f32[1,4096]{1,0:T(1,128)S(1)} %copy-done.4, f32[3,3,1,4096]{3,2,1,0:T(1,128)S(1)} %bitcast.15, f32[16,128]{1,0:T(8,128)S(1)} %copy-done.6, ...), custom_call_target="tpu_custom_call" | custom-call | flops 2200000000 | bytes 7000000 | tf_op jit(solution)/shard_map/scan/pallas_call | solution.py:612
  25.2 4.3 %all-to-all-start.1 = ((bf16[32,40,128]{2,1,0:T(8,128)(2,1)}), bf16[32,40,128]{2,1,0:T(8,128)(2,1)S(1)}, u32[]{:S(2)}, u32[]{:S(2)}) async-start(bf16[32,40,128]{2,1,0:T(8,128)(2,1)} %get-tuple-element.28), calls=%async_computation.1 | async-start | bytes 655360 | tf_op jit(solution)/shard_map/all_to_all | solution.py:695
  29.5 0.0 copy-start.5
  29.5 0.0 copy-start.7
  29.5 6.2 %near.3 = (f32[128,4096]{1,0:T(8,128)}, f32[8,128]{1,0:T(8,128)}) custom-call(bf16[128,4096]{1,0:T(8,128)(2,1)} %get-tuple-element.23.signal_ref, f32[16,4096]{1,0:T(8,128)S(1)} %bitcast.10, f32[16,4096]{1,0:T(8,128)S(1)} %bitcast.13, f32[16,128]{1,0:T(8,128)S(1)} %copy-done.6, f32[1,4096]{1,0:T(1,128)S(1)} %copy-done.3, ...), custom_call_target="tpu_custom_call" | custom-call | flops 4400000000 | bytes 14000000 | tf_op jit(solution)/shard_map/near/pallas_call | solution.py:591
  35.7 3.2 %all-to-all-done.1.enter_ref = bf16[32,40,128]{2,1,0:T(8,128)(2,1)S(1)} async-done(((bf16[32,40,128]{2,1,0:T(8,128)(2,1)}), bf16[32,40,128]{2,1,0:T(8,128)(2,1)S(1)}, u32[]{:S(2)}, u32[]{:S(2)}) %all-to-all-start.1) | async-done | bytes 327712 | tf_op jit(solution)/shard_map/all_to_all | solution.py:695
  38.9 4.6 %finish.2 = (bf16[64,4096]{1,0:T(8,128)(2,1)S(1)}, bf16[64,4096]{1,0:T(8,128)(2,1)S(1)}, f32[16,4096]{1,0:T(8,128)S(1)}) custom-call(bf16[128,4096]{1,0:T(8,128)(2,1)} %bitcast.19, bf16[128,4096]{1,0:T(8,128)(2,1)} %bitcast.22, f32[128,4096]{1,0:T(8,128)} %get-tuple-element.22.ahead_hbm, f32[128,4096]{1,0:T(8,128)} %get-tuple-element.27.back_hbm, ...), custom_call_target="tpu_custom_call" | custom-call | flops 6600000000 | bytes 21000000 | tf_op jit(solution)/shard_map/finish/pallas_call | solution.py:641
  43.5 4.1 %collective-permute-start.2 = (bf16[64,4096]{1,0:T(8,128)(2,1)S(1)}, bf16[64,4096]{1,0:T(8,128)(2,1)S(1)}, u32[]{:S(2)}, u32[]{:S(2)}) collective-permute-start(bf16[64,4096]{1,0:T(8,128)(2,1)S(1)} %get-tuple-element.32), channel_id=1, source_target_pairs={{32,0},{64,32},{96,64},{128,96},{160,128},{192,160},{224,192},{256... | collective-permute-start | bytes 1572872 | tf_op jit(solution)/shard_map/ppermute | solution.py:526
  47.7 2.1 %collective-permute-start.3 = (bf16[64,4096]{1,0:T(8,128)(2,1)S(1)}, bf16[64,4096]{1,0:T(8,128)(2,1)S(1)}, u32[]{:S(2)}, u32[]{:S(2)}) collective-permute-start(bf16[64,4096]{1,0:T(8,128)(2,1)S(1)} %get-tuple-element.33), channel_id=1, source_target_pairs={{0,32},{32,64},{64,96},{96,128},{128,160},{160,192},{192,224},{224... | collective-permute-start | bytes 1572872 | tf_op jit(solution)/shard_map/ppermute | solution.py:526
  49.8 4.3 %finish.3 = (bf16[64,4096]{1,0:T(8,128)(2,1)S(1)}, bf16[64,4096]{1,0:T(8,128)(2,1)S(1)}) custom-call(bf16[128,4096]{1,0:T(8,128)(2,1)} %bitcast.20, bf16[128,4096]{1,0:T(8,128)(2,1)} %bitcast.23, f32[128,4096]{1,0:T(8,128)} %get-tuple-element.22.ahead_hbm, f32[128,4096]{1,0:T(8,128)} %get-tuple-element.27.back_hbm, f32[128,128]{1,0:T(8,128)S(1)} %copy-done.7, ...), custom_call_target="tpu_custom_call" | custom-call | flops 6600000000 | bytes 21000000 | tf_op jit(solution)/shard_map/finish/pallas_call | solution.py:641
  54.1 5.1 %collective-permute-start = (bf16[64,4096]{1,0:T(8,128)(2,1)S(1)}, bf16[64,4096]{1,0:T(8,128)(2,1)S(1)}, u32[]{:S(2)}, u32[]{:S(2)}) collective-permute-start(bf16[64,4096]{1,0:T(8,128)(2,1)S(1)} %get-tuple-element.30), channel_id=1, source_target_pairs={{32,0},{64,32},{96,64},{128,96},{160,128},{192,160},{224,192},{256... | collective-permute-start | bytes 1572872 | tf_op jit(solution)/shard_map/ppermute | solution.py:526
  59.3 1.9 %collective-permute-start.1 = (bf16[64,4096]{1,0:T(8,128)(2,1)S(1)}, bf16[64,4096]{1,0:T(8,128)(2,1)S(1)}, u32[]{:S(2)}, u32[]{:S(2)}) collective-permute-start(bf16[64,4096]{1,0:T(8,128)(2,1)S(1)} %get-tuple-element.31), channel_id=1, source_target_pairs={{0,32},{32,64},{64,96},{96,128},{128,160},{160,192},{192,224},{224... | collective-permute-start | bytes 1572872 | tf_op jit(solution)/shard_map/ppermute | solution.py:526
  61.2 0.0 collective-permute-done.2.grad_ref
  61.2 3.8 %collective-permute-done.3.layer_ref = bf16[64,4096]{1,0:T(8,128)(2,1)S(1)} collective-permute-done((bf16[64,4096]{1,0:T(8,128)(2,1)S(1)}, bf16[64,4096]{1,0:T(8,128)(2,1)S(1)}, u32[]{:S(2)}, u32[]{:S(2)}) %collective-permute-start.3) | collective-permute-done | bytes 524320 | tf_op jit(solution)/shard_map/ppermute | solution.py:526
  65.0 1.0 %join.2 = (bf16[128,4096]{1,0:T(8,128)(2,1)}, bf16[128,4096]{1,0:T(8,128)(2,1)}) custom-call(bf16[64,4096]{1,0:T(8,128)(2,1)S(1)} %collective-permute-done.2.grad_ref, bf16[64,4096]{1,0:T(8,128)(2,1)S(1)} %collective-permute-done.3.layer_ref), custom_call_target="tpu_custom_call" | custom-call | flops 1100000000 | bytes 3500000 | tf_op jit(solution)/shard_map/join/pallas_call | solution.py:668
  66.0 5.0 %collective-permute-done.grad_ref = bf16[64,4096]{1,0:T(8,128)(2,1)S(1)} collective-permute-done((bf16[64,4096]{1,0:T(8,128)(2,1)S(1)}, bf16[64,4096]{1,0:T(8,128)(2,1)S(1)}, u32[]{:S(2)}, u32[]{:S(2)}) %collective-permute-start) | collective-permute-done | bytes 524320 | tf_op jit(solution)/shard_map/ppermute | solution.py:526
  71.0 5.1 %collective-permute-done.1.layer_ref = bf16[64,4096]{1,0:T(8,128)(2,1)S(1)} collective-permute-done((bf16[64,4096]{1,0:T(8,128)(2,1)S(1)}, bf16[64,4096]{1,0:T(8,128)(2,1)S(1)}, u32[]{:S(2)}, u32[]{:S(2)}) %collective-permute-start.1) | collective-permute-done | bytes 524320 | tf_op jit(solution)/shard_map/ppermute | solution.py:526
  76.1 1.0 %join.3 = (bf16[128,4096]{1,0:T(8,128)(2,1)}, bf16[128,4096]{1,0:T(8,128)(2,1)}) custom-call(bf16[64,4096]{1,0:T(8,128)(2,1)S(1)} %collective-permute-done.grad_ref, bf16[64,4096]{1,0:T(8,128)(2,1)S(1)} %collective-permute-done.1.layer_ref, bf16[128,4096]{1,0:T(8,128)(2,1)} %get-tuple-element.34.refs_0_, ...), custom_call_target="tpu_custom_call", output_to_operand_aliasing={{0}: (2, {}), {1}: (3, {})} | custom-call | flops 1100000000 | bytes 3500000 | tf_op jit(solution)/shard_map/join/pallas_call | solution.py:668
  (4 shorter events, 0.0 us)
Async XLA Ops:
  0.6 13.2 %copy-start = (f32[1,16,4096]{2,1,0:T(8,128)S(1)}, f32[1,16,4096]{2,1,0:T(8,128)}, u32[]{:S(2)}) copy-start(f32[1,16,4096]{2,1,0:T(8,128)} %param.15) | copy-start | bytes 786436
  0.6 13.2 %copy-start.1 = (f32[1,16,4096]{2,1,0:T(8,128)S(1)}, f32[1,16,4096]{2,1,0:T(8,128)}, u32[]{:S(2)}) copy-start(f32[1,16,4096]{2,1,0:T(8,128)} %param.16) | copy-start | bytes 786436
  0.7 13.2 %copy-start.3 = (f32[1,4096]{1,0:T(1,128)S(1)}, f32[1,4096]{1,0:T(1,128)}, u32[]{:S(2)}) copy-start(f32[1,4096]{1,0:T(1,128)} %skip_ref.5) | copy-start | bytes 49156
  0.7 13.2 %copy-start.6 = (f32[16,128]{1,0:T(8,128)S(1)}, f32[16,128]{1,0:T(8,128)}, u32[]{:S(2)}) copy-start(f32[16,128]{1,0:T(8,128)} %constant.11.clone.places_ref) | copy-start | bytes 24580
  6.5 16.8 %all-to-all-start = ((bf16[32,40,128]{2,1,0:T(8,128)(2,1)}), bf16[32,40,128]{2,1,0:T(8,128)(2,1)S(1)}, u32[]{:S(2)}, u32[]{:S(2)}) async-start(bf16[32,40,128]{2,1,0:T(8,128)(2,1)} %get-tuple-element.24), calls=%async_computation | async-start | bytes 655360 | tf_op jit(solution)/shard_map/all_to_all | solution.py:691
  13.9 9.4 %copy-start.2 = (f32[1,3,3,4096]{3,0,2,1:T(1,128)S(1)}, f32[1,3,3,4096]{3,0,2,1:T(1,128)}, u32[]{:S(2)}) copy-start(f32[1,3,3,4096]{3,0,2,1:T(1,128)} %param.14) | copy-start | bytes 442372
  13.9 9.4 %copy-start.4 = (f32[1,4096]{1,0:T(1,128)S(1)}, f32[1,4096]{1,0:T(1,128)}, u32[]{:S(2)}) copy-start(f32[1,4096]{1,0:T(1,128)} %gain_ref.5) | copy-start | bytes 49156
  25.2 13.7 %all-to-all-start.1 = ((bf16[32,40,128]{2,1,0:T(8,128)(2,1)}), bf16[32,40,128]{2,1,0:T(8,128)(2,1)S(1)}, u32[]{:S(2)}, u32[]{:S(2)}) async-start(bf16[32,40,128]{2,1,0:T(8,128)(2,1)} %get-tuple-element.28), calls=%async_computation.1 | async-start | bytes 655360 | tf_op jit(solution)/shard_map/all_to_all | solution.py:695
  29.5 9.4 %copy-start.5 = (bf16[256,32]{1,0:T(8,128)(2,1)S(1)}, bf16[256,32]{1,0:T(8,128)(2,1)}, u32[]{:S(2)}) copy-start(bf16[256,32]{1,0:T(8,128)(2,1)} %constant.9.clone.spread_ref) | copy-start | bytes 49156
  29.5 9.4 %copy-start.7 = (f32[128,128]{1,0:T(8,128)S(1)}, f32[128,128]{1,0:T(8,128)}, u32[]{:S(2)}) copy-start(f32[128,128]{1,0:T(8,128)} %get-tuple-element.21.mark_ref.inverse_ref) | copy-start | bytes 196612
  43.5 17.7 %collective-permute-start.2 = (bf16[64,4096]{1,0:T(8,128)(2,1)S(1)}, bf16[64,4096]{1,0:T(8,128)(2,1)S(1)}, u32[]{:S(2)}, u32[]{:S(2)}) collective-permute-start(bf16[64,4096]{1,0:T(8,128)(2,1)S(1)} %get-tuple-element.32), channel_id=1, source_target_pairs={{32,0},{64,32},{96,64},{128,96},{160,128},{192,160},{224,192},{256... | collective-permute-start | bytes 1572872 | tf_op jit(solution)/shard_map/ppermute | solution.py:526
  47.7 17.3 %collective-permute-start.3 = (bf16[64,4096]{1,0:T(8,128)(2,1)S(1)}, bf16[64,4096]{1,0:T(8,128)(2,1)S(1)}, u32[]{:S(2)}, u32[]{:S(2)}) collective-permute-start(bf16[64,4096]{1,0:T(8,128)(2,1)S(1)} %get-tuple-element.33), channel_id=1, source_target_pairs={{0,32},{32,64},{64,96},{96,128},{128,160},{160,192},{192,224},{224... | collective-permute-start | bytes 1572872 | tf_op jit(solution)/shard_map/ppermute | solution.py:526
  54.1 16.9 %collective-permute-start = (bf16[64,4096]{1,0:T(8,128)(2,1)S(1)}, bf16[64,4096]{1,0:T(8,128)(2,1)S(1)}, u32[]{:S(2)}, u32[]{:S(2)}) collective-permute-start(bf16[64,4096]{1,0:T(8,128)(2,1)S(1)} %get-tuple-element.30), channel_id=1, source_target_pairs={{32,0},{64,32},{96,64},{128,96},{160,128},{192,160},{224,192},{256... | collective-permute-start | bytes 1572872 | tf_op jit(solution)/shard_map/ppermute | solution.py:526
  59.3 16.8 %collective-permute-start.1 = (bf16[64,4096]{1,0:T(8,128)(2,1)S(1)}, bf16[64,4096]{1,0:T(8,128)(2,1)S(1)}, u32[]{:S(2)}, u32[]{:S(2)}) collective-permute-start(bf16[64,4096]{1,0:T(8,128)(2,1)S(1)} %get-tuple-element.31), channel_id=1, source_target_pairs={{0,32},{32,64},{64,96},{96,128},{128,160},{160,192},{192,224},{224... | collective-permute-start | bytes 1572872 | tf_op jit(solution)/shard_map/ppermute | solution.py:526

commit v6 on v5

--- a/solution.py
+++ b/solution.py
@@ -125,9 +125,9 @@
 
 
 def start_kernel(
-    nodes, x_hbm, cot_hbm, gain_hbm, taps_hbm, rates_hbm, moments_hbm,
+    x_hbm, cot_hbm, gain_hbm, taps_hbm, moments_hbm,
     mixed_hbm, gate_hbm, packet_hbm, inverse_hbm,
-    x_ref, cot_ref, gain_ref, taps_ref, rates_ref, moments_ref, mixed_ref, gate_ref, packet_ref, inverse_ref,
+    x_ref, cot_ref, gain_ref, taps_ref, moments_ref, mixed_ref, gate_ref, packet_ref, inverse_ref,
     normed_refs, moment_ref, x_sems, cot_sems, table_sems, mixed_sems, gate_sems, last_sems,
 ):
     rows, width = x_ref.shape
@@ -145,7 +145,7 @@
     table_copies = [
         pltpu.make_async_copy(source, target, table_sems.at[n])
         for n, (source, target) in enumerate(
-            ((gain_hbm, gain_ref), (taps_hbm, taps_ref), (moments_hbm, moments_ref), (rates_hbm, rates_ref))
+            ((gain_hbm, gain_ref), (taps_hbm, taps_ref), (moments_hbm, moments_ref))
         )
     ]
     for copy in x_copies + table_copies + cot_copies:
@@ -204,19 +204,11 @@
 
     def project(i, carry):
         cols = group_of(i)
-        rates = rates_ref[:, cols]
-        states = [0.0, 0.0]
-        for k in range(NODES):
-            power = jnp.exp(rates * (-nodes[k]))
-            states = [
-                states[side] + power * moment_ref[PADDED * side + k : PADDED * side + k + 1, cols]
-                for side in range(2)
-            ]
         x_head = x_ref[0:16, cols].astype(F32)
         x_tail = x_ref[rows - 16 : rows, cols].astype(F32)
         cot_head = cot_ref[0:16, cols].astype(F32)
         packet_ref[i] = jnp.concatenate(
-            states + [x_head[0:2], x_tail[14:16], cot_head[0:2], scales], axis=0
+            [moment_ref[:, cols], x_head[0:2], x_tail[14:16], cot_head[0:2], scales], axis=0
         ).astype(BF16)
         return carry
 
@@ -274,7 +266,7 @@
 
 def scan_kernel(
     rates_ref, residue_ref, skip_ref, gain_ref, taps_ref, places_ref, packet_ref, mark_ref, enter_ref, done_ref,
-    wide_ref, row_ref, base_ref, column_ref, *, rows,
+    wide_ref, row_ref, base_ref, column_ref, power_ref, *, rows, nodes,
 ):
     done_ref[...] = jnp.zeros_like(done_ref)
     count = packet_ref.shape[0]
@@ -289,6 +281,8 @@
     places = places_ref[...]
     for r in range(MODES):
         column_ref[r] = jnp.exp(-rates[r : r + 1] * places)
+    for k in range(NODES):
+        power_ref[k] = jnp.exp(rates * (-nodes[k]))
     for d in range(count):
         wide_ref[d * PACKET : (d + 1) * PACKET] = packet_ref[d].astype(F32)
     x_0, x_1, x_2, x_3, cot_0, cot_1, high, low = [
@@ -336,6 +330,12 @@
             total = total + column_ref[r] * weight[r : r + 1]
         return total[0:NODES]
 
+    def project(row):
+        total = power_ref[0] * wide_ref[row : row + 1]
+        for k in range(1, NODES):
+            total = total + power_ref[k] * wide_ref[row + k : row + k + 1]
+        return total
+
     ahead = jnp.zeros((MODES, LANES), F32)
     back = jnp.zeros((MODES, LANES), F32)
     for step in range(count):
@@ -344,7 +344,7 @@
         base_ref[0, d : d + 1] = over(reached)
         base_ref[1, d : d + 1] = over(reached * fall)
         nodal = spread(reached + coef * (row_ref[0, d : d + 1] + rise * row_ref[1, d : d + 1]))
-        own = wide_ref[d * PACKET : d * PACKET + MODES]
+        own = project(d * PACKET)
         wide_ref[d * PACKET : d * PACKET + PADDED] = jnp.concatenate(
             [nodal, row_ref[4, d : d + 1], row_ref[5, d : d + 1]], axis=0
         )
@@ -352,7 +352,7 @@
 
         d = count - 1 - step
         nodal = spread(coef * fall * back)
-        back = decay * back + wide_ref[d * PACKET + MODES : d * PACKET + 2 * MODES]
+        back = decay * back + project(d * PACKET + PADDED)
         wide_ref[d * PACKET + PADDED : d * PACKET + 2 * PADDED] = jnp.concatenate(
             [nodal, row_ref[6, d : d + 1], row_ref[7, d : d + 1]], axis=0
         )
@@ -550,7 +550,7 @@
     )
 
 
-def start_call(x, cot, gain, taps, rates, moments):
+def start_call(x, cot, gain, taps, moments):
     rows, width = x.shape
     pieces = PIECES
     far = pl.BlockSpec(memory_space=pltpu.HBM)
@@ -560,10 +560,9 @@
         ((width // LANES, PACKET, LANES), BF16),
         ((rows, LANES), F32),
     ]
-    ins = (x, cot, gain, taps, rates, moments)
-    held = (x, cot, gain, taps, rates, moments)
+    ins = held = (x, cot, gain, taps, moments)
     return pl.pallas_call(
-        functools.partial(start_kernel, [float(p) for p in node_places(rows)]),
+        start_kernel,
         in_specs=[far] * len(ins),
         out_specs=[far] * len(outs),
         out_shape=[pltpu.HBM(*out) for out in outs],
@@ -574,7 +573,7 @@
             pltpu.VMEM((2 * PADDED, width), F32),
             pltpu.SemaphoreType.DMA((pieces,)),
             pltpu.SemaphoreType.DMA((pieces,)),
-            pltpu.SemaphoreType.DMA((4,)),
+            pltpu.SemaphoreType.DMA((3,)),
             pltpu.SemaphoreType.DMA((pieces,)),
             pltpu.SemaphoreType.DMA((pieces,)),
             pltpu.SemaphoreType.DMA((2,)),
@@ -610,13 +609,14 @@
 def scan_call(rates, residue, skip, gain, taps, places, gathered, mark, rows):
     count = gathered.shape[0]
     return pl.pallas_call(
-        functools.partial(scan_kernel, rows=rows),
+        functools.partial(scan_kernel, rows=rows, nodes=[float(p) for p in node_places(rows)]),
         out_shape=[shape(gathered.shape, BF16), shape((8, LANES), F32)],
         scratch_shapes=[
             pltpu.VMEM((count * PACKET, LANES), F32),
             pltpu.VMEM((8, count, LANES), F32),
             pltpu.VMEM((4, count, LANES), F32),
             pltpu.VMEM((MODES, PADDED, LANES), F32),
+            pltpu.VMEM((NODES, MODES, LANES), F32),
         ],
         compiler_params=params(8),
         cost_estimate=takes(2),
@@ -687,7 +687,7 @@
     fixed = {name: jnp.asarray(table) for name, table in constants(rows).items()}
 
     weights = residue[0]
-    mixed, gate, packet, inverse = start_call(x, cot, norm_gain, taps, rates, fixed["moments"])
+    mixed, gate, packet, inverse = start_call(x, cot, norm_gain, taps, fixed["moments"])
     gathered = lax.all_to_all(packet, "seq", split_axis=0, concat_axis=0, tiled=True)
     near = (rates, weights, fixed["places"], skip_gain, fixed["near"])
     ahead, mark = near_call(0, mixed, *near, stay(inverse))

time: 77.8 us -> 77.8 us (level)
  no operation moved by 1% of the time
where the time goes in v6:
time: 77.8 us; the launch traced here: 77.3 us
  Pallas kernels  31.2 us (40%)
  starting transfers between devices  24.9 us (32%)
  waiting for transfers between devices  20.2 us (26%)
  between operations  0.98 us (1%)
    ppermute x4, waiting for transfers between devices, shifted(): return lax.ppermute(block, axis, route)  13.9 us
    ppermute x4, starting transfers between devices, shifted(): return lax.ppermute(block, axis, route)  13.3 us
    pallas_call x2, Pallas kernels, near_call(): pl.pallas_call(near_kernel, grid=(width // step,), in_specs=[across(signa...  12.5 us
    pallas_call x2, Pallas kernels, finish_call(): pl.pallas_call(functools.partial(finish_kernel, rows, first, count), in_s...  8.94 us
    all_to_all x1, starting transfers between devices, local(): lax.all_to_all(packet, 'seq', split_axis=0, concat_axis=0, tiled=True)  7.33 us
    pallas_call x1, Pallas kernels, start_call(): pl.pallas_call(start_kernel, in_specs=[far] * len(ins), out_specs=[far] *...  5.44 us
    all_to_all x1, starting transfers between devices, local(): lax.all_to_all(entering, 'seq', split_axis=0, concat_axis=0, tiled=True)  4.29 us
    all_to_all x1, waiting for transfers between devices, local(): lax.all_to_all(entering, 'seq', split_axis=0, concat_axis=0, tiled=True)  3.18 us
  transfers between devices with their start and end apart: 6, of which 5 were waited for; matrix products, arithmetic and copies ran while one was open for 0% of the time, Pallas kernels for 23%

profile of v6, /device:TPU:384, one launch (start us, length us, event | category | flops | bytes accessed | tf_op | source)
XLA Modules:
  0.0 77.3 jit_solution(15387211453892430983)
XLA Ops:
  0.6 0.0 copy-start
  0.6 0.0 copy-start.1
  0.7 0.0 copy-start.3
  0.7 0.0 copy-start.6
  0.7 5.4 %start.1 = (bf16[128,4096]{1,0:T(8,128)(2,1)}, bf16[128,4096]{1,0:T(8,128)(2,1)}, bf16[32,40,128]{2,1,0:T(8,128)(2,1)}, f32[128,128]{1,0:T(8,128)}) custom-call(bf16[128,4096]{1,0:T(8,128)(2,1)} %bitcast.17, bf16[128,4096]{1,0:T(8,128)(2,1)} %bitcast.20, f32[1,4096]{1,0:T(1,128)} %gain_ref.5, f32[3,3,1,4096]{3,2,1,0:T(1,128)} %bitcast.13, ...), custom_call_target="tpu_custom_call" | custom-call | flops 6600000000 | bytes 21000000 | tf_op jit(solution)/shard_map/start/pallas_call | solution.py:564
  6.1 7.3 %all-to-all-start = ((bf16[32,40,128]{2,1,0:T(8,128)(2,1)}), bf16[32,40,128]{2,1,0:T(8,128)(2,1)S(1)}, u32[]{:S(2)}, u32[]{:S(2)}) async-start(bf16[32,40,128]{2,1,0:T(8,128)(2,1)} %get-tuple-element.24), calls=%async_computation | async-start | bytes 655360 | tf_op jit(solution)/shard_map/all_to_all | solution.py:691
  13.5 0.0 copy-done
  13.5 0.0 copy-done.1
  13.5 0.0 copy-done.3
  13.5 0.0 copy-done.6
  13.5 0.0 copy-start.2
  13.5 0.0 copy-start.4
  13.5 6.2 %near.2 = (f32[128,4096]{1,0:T(8,128)}, f32[8,128]{1,0:T(8,128)S(1)}) custom-call(bf16[128,4096]{1,0:T(8,128)(2,1)} %get-tuple-element.20.signal_ref, f32[16,4096]{1,0:T(8,128)S(1)} %bitcast.7, f32[16,4096]{1,0:T(8,128)S(1)} %bitcast.10, f32[16,128]{1,0:T(8,128)S(1)} %copy-done.6, f32[1,4096]{1,0:T(1,128)S(1)} %copy-done.3, ...), custom_call_target="tpu_custom_call" | custom-call | flops 4400000000 | bytes 14000000 | tf_op jit(solution)/shard_map/near/pallas_call | solution.py:590
  19.8 3.1 %all-to-all-done.packet_ref = bf16[32,40,128]{2,1,0:T(8,128)(2,1)S(1)} async-done(((bf16[32,40,128]{2,1,0:T(8,128)(2,1)}), bf16[32,40,128]{2,1,0:T(8,128)(2,1)S(1)}, u32[]{:S(2)}, u32[]{:S(2)}) %all-to-all-start) | async-done | bytes 327712 | tf_op jit(solution)/shard_map/all_to_all | solution.py:691
  22.9 0.0 copy-done.4
  22.9 2.4 %scan.1 = (bf16[32,40,128]{2,1,0:T(8,128)(2,1)}, f32[8,128]{1,0:T(8,128)S(1)}) custom-call(f32[16,4096]{1,0:T(8,128)S(1)} %bitcast.8, f32[16,4096]{1,0:T(8,128)S(1)} %bitcast.11, f32[1,4096]{1,0:T(1,128)S(1)} %copy-done.3, f32[1,4096]{1,0:T(1,128)S(1)} %copy-done.4, f32[3,3,1,4096]{3,2,1,0:T(1,128)S(1)} %bitcast.14, f32[16,128]{1,0:T(8,128)S(1)} %copy-done.6, ...), custom_call_target="tpu_custom_call" | custom-call | flops 2200000000 | bytes 7000000 | tf_op jit(solution)/shard_map/scan/pallas_call | solution.py:611
  25.3 4.3 %all-to-all-start.1 = ((bf16[32,40,128]{2,1,0:T(8,128)(2,1)}), bf16[32,40,128]{2,1,0:T(8,128)(2,1)S(1)}, u32[]{:S(2)}, u32[]{:S(2)}) async-start(bf16[32,40,128]{2,1,0:T(8,128)(2,1)} %get-tuple-element.28), calls=%async_computation.1 | async-start | bytes 655360 | tf_op jit(solution)/shard_map/all_to_all | solution.py:695
  29.6 0.0 copy-start.5
  29.6 6.2 %near.3 = (f32[128,4096]{1,0:T(8,128)}, f32[8,128]{1,0:T(8,128)}) custom-call(bf16[128,4096]{1,0:T(8,128)(2,1)} %get-tuple-element.23.signal_ref, f32[16,4096]{1,0:T(8,128)S(1)} %bitcast.9, f32[16,4096]{1,0:T(8,128)S(1)} %bitcast.12, f32[16,128]{1,0:T(8,128)S(1)} %copy-done.6, f32[1,4096]{1,0:T(1,128)S(1)} %copy-done.3, ...), custom_call_target="tpu_custom_call" | custom-call | flops 4400000000 | bytes 14000000 | tf_op jit(solution)/shard_map/near/pallas_call | solution.py:590
  35.8 3.2 %all-to-all-done.1.enter_ref = bf16[32,40,128]{2,1,0:T(8,128)(2,1)S(1)} async-done(((bf16[32,40,128]{2,1,0:T(8,128)(2,1)}), bf16[32,40,128]{2,1,0:T(8,128)(2,1)S(1)}, u32[]{:S(2)}, u32[]{:S(2)}) %all-to-all-start.1) | async-done | bytes 327712 | tf_op jit(solution)/shard_map/all_to_all | solution.py:695
  39.0 4.6 %finish.2 = (bf16[64,4096]{1,0:T(8,128)(2,1)S(1)}, bf16[64,4096]{1,0:T(8,128)(2,1)S(1)}, f32[16,4096]{1,0:T(8,128)S(1)}) custom-call(bf16[128,4096]{1,0:T(8,128)(2,1)} %bitcast.18, bf16[128,4096]{1,0:T(8,128)(2,1)} %bitcast.21, f32[128,4096]{1,0:T(8,128)} %get-tuple-element.22.ahead_hbm, f32[128,4096]{1,0:T(8,128)} %get-tuple-element.27.back_hbm, ...), custom_call_target="tpu_custom_call" | custom-call | flops 6600000000 | bytes 21000000 | tf_op jit(solution)/shard_map/finish/pallas_call | solution.py:641
  43.6 4.1 %collective-permute-start.2 = (bf16[64,4096]{1,0:T(8,128)(2,1)S(1)}, bf16[64,4096]{1,0:T(8,128)(2,1)S(1)}, u32[]{:S(2)}, u32[]{:S(2)}) collective-permute-start(bf16[64,4096]{1,0:T(8,128)(2,1)S(1)} %get-tuple-element.32), channel_id=1, source_target_pairs={{32,0},{64,32},{96,64},{128,96},{160,128},{192,160},{224,192},{256... | collective-permute-start | bytes 1572872 | tf_op jit(solution)/shard_map/ppermute | solution.py:526
  47.7 2.1 %collective-permute-start.3 = (bf16[64,4096]{1,0:T(8,128)(2,1)S(1)}, bf16[64,4096]{1,0:T(8,128)(2,1)S(1)}, u32[]{:S(2)}, u32[]{:S(2)}) collective-permute-start(bf16[64,4096]{1,0:T(8,128)(2,1)S(1)} %get-tuple-element.33), channel_id=1, source_target_pairs={{0,32},{32,64},{64,96},{96,128},{128,160},{160,192},{192,224},{224... | collective-permute-start | bytes 1572872 | tf_op jit(solution)/shard_map/ppermute | solution.py:526
  49.9 4.3 %finish.3 = (bf16[64,4096]{1,0:T(8,128)(2,1)S(1)}, bf16[64,4096]{1,0:T(8,128)(2,1)S(1)}) custom-call(bf16[128,4096]{1,0:T(8,128)(2,1)} %bitcast.19, bf16[128,4096]{1,0:T(8,128)(2,1)} %bitcast.22, f32[128,4096]{1,0:T(8,128)} %get-tuple-element.22.ahead_hbm, f32[128,4096]{1,0:T(8,128)} %get-tuple-element.27.back_hbm, f32[128,128]{1,0:T(8,128)S(1)} %copy-done.7, ...), custom_call_target="tpu_custom_call" | custom-call | flops 6600000000 | bytes 21000000 | tf_op jit(solution)/shard_map/finish/pallas_call | solution.py:641
  54.2 5.1 %collective-permute-start = (bf16[64,4096]{1,0:T(8,128)(2,1)S(1)}, bf16[64,4096]{1,0:T(8,128)(2,1)S(1)}, u32[]{:S(2)}, u32[]{:S(2)}) collective-permute-start(bf16[64,4096]{1,0:T(8,128)(2,1)S(1)} %get-tuple-element.30), channel_id=1, source_target_pairs={{32,0},{64,32},{96,64},{128,96},{160,128},{192,160},{224,192},{256... | collective-permute-start | bytes 1572872 | tf_op jit(solution)/shard_map/ppermute | solution.py:526
  59.3 1.9 %collective-permute-start.1 = (bf16[64,4096]{1,0:T(8,128)(2,1)S(1)}, bf16[64,4096]{1,0:T(8,128)(2,1)S(1)}, u32[]{:S(2)}, u32[]{:S(2)}) collective-permute-start(bf16[64,4096]{1,0:T(8,128)(2,1)S(1)} %get-tuple-element.31), channel_id=1, source_target_pairs={{0,32},{32,64},{64,96},{96,128},{128,160},{160,192},{192,224},{224... | collective-permute-start | bytes 1572872 | tf_op jit(solution)/shard_map/ppermute | solution.py:526
  61.3 0.0 collective-permute-done.2.grad_ref
  61.3 3.8 %collective-permute-done.3.layer_ref = bf16[64,4096]{1,0:T(8,128)(2,1)S(1)} collective-permute-done((bf16[64,4096]{1,0:T(8,128)(2,1)S(1)}, bf16[64,4096]{1,0:T(8,128)(2,1)S(1)}, u32[]{:S(2)}, u32[]{:S(2)}) %collective-permute-start.3) | collective-permute-done | bytes 524320 | tf_op jit(solution)/shard_map/ppermute | solution.py:526
  65.0 1.0 %join.2 = (bf16[128,4096]{1,0:T(8,128)(2,1)}, bf16[128,4096]{1,0:T(8,128)(2,1)}) custom-call(bf16[64,4096]{1,0:T(8,128)(2,1)S(1)} %collective-permute-done.2.grad_ref, bf16[64,4096]{1,0:T(8,128)(2,1)S(1)} %collective-permute-done.3.layer_ref), custom_call_target="tpu_custom_call" | custom-call | flops 1100000000 | bytes 3500000 | tf_op jit(solution)/shard_map/join/pallas_call | solution.py:668
  66.0 5.0 %collective-permute-done.grad_ref = bf16[64,4096]{1,0:T(8,128)(2,1)S(1)} collective-permute-done((bf16[64,4096]{1,0:T(8,128)(2,1)S(1)}, bf16[64,4096]{1,0:T(8,128)(2,1)S(1)}, u32[]{:S(2)}, u32[]{:S(2)}) %collective-permute-start) | collective-permute-done | bytes 524320 | tf_op jit(solution)/shard_map/ppermute | solution.py:526
  71.1 5.1 %collective-permute-done.1.layer_ref = bf16[64,4096]{1,0:T(8,128)(2,1)S(1)} collective-permute-done((bf16[64,4096]{1,0:T(8,128)(2,1)S(1)}, bf16[64,4096]{1,0:T(8,128)(2,1)S(1)}, u32[]{:S(2)}, u32[]{:S(2)}) %collective-permute-start.1) | collective-permute-done | bytes 524320 | tf_op jit(solution)/shard_map/ppermute | solution.py:526
  76.1 1.0 %join.3 = (bf16[128,4096]{1,0:T(8,128)(2,1)}, bf16[128,4096]{1,0:T(8,128)(2,1)}) custom-call(bf16[64,4096]{1,0:T(8,128)(2,1)S(1)} %collective-permute-done.grad_ref, bf16[64,4096]{1,0:T(8,128)(2,1)S(1)} %collective-permute-done.1.layer_ref, bf16[128,4096]{1,0:T(8,128)(2,1)} %get-tuple-element.34.refs_0_, ...), custom_call_target="tpu_custom_call", output_to_operand_aliasing={{0}: (2, {}), {1}: (3, {})} | custom-call | flops 1100000000 | bytes 3500000 | tf_op jit(solution)/shard_map/join/pallas_call | solution.py:668
  (4 shorter events, 0.0 us)
Async XLA Ops:
  0.6 12.8 %copy-start = (f32[1,16,4096]{2,1,0:T(8,128)S(1)}, f32[1,16,4096]{2,1,0:T(8,128)}, u32[]{:S(2)}) copy-start(f32[1,16,4096]{2,1,0:T(8,128)} %param.15) | copy-start | bytes 786436
  0.6 12.8 %copy-start.1 = (f32[1,16,4096]{2,1,0:T(8,128)S(1)}, f32[1,16,4096]{2,1,0:T(8,128)}, u32[]{:S(2)}) copy-start(f32[1,16,4096]{2,1,0:T(8,128)} %param.16) | copy-start | bytes 786436
  0.7 12.8 %copy-start.3 = (f32[1,4096]{1,0:T(1,128)S(1)}, f32[1,4096]{1,0:T(1,128)}, u32[]{:S(2)}) copy-start(f32[1,4096]{1,0:T(1,128)} %skip_ref.5) | copy-start | bytes 49156
  0.7 12.8 %copy-start.6 = (f32[16,128]{1,0:T(8,128)S(1)}, f32[16,128]{1,0:T(8,128)}, u32[]{:S(2)}) copy-start(f32[16,128]{1,0:T(8,128)} %constant.11.clone.places_ref) | copy-start | bytes 24580
  6.1 16.8 %all-to-all-start = ((bf16[32,40,128]{2,1,0:T(8,128)(2,1)}), bf16[32,40,128]{2,1,0:T(8,128)(2,1)S(1)}, u32[]{:S(2)}, u32[]{:S(2)}) async-start(bf16[32,40,128]{2,1,0:T(8,128)(2,1)} %get-tuple-element.24), calls=%async_computation | async-start | bytes 655360 | tf_op jit(solution)/shard_map/all_to_all | solution.py:691
  13.5 9.4 %copy-start.2 = (f32[1,3,3,4096]{3,0,2,1:T(1,128)S(1)}, f32[1,3,3,4096]{3,0,2,1:T(1,128)}, u32[]{:S(2)}) copy-start(f32[1,3,3,4096]{3,0,2,1:T(1,128)} %param.14) | copy-start | bytes 442372
  13.5 9.4 %copy-start.4 = (f32[1,4096]{1,0:T(1,128)S(1)}, f32[1,4096]{1,0:T(1,128)}, u32[]{:S(2)}) copy-start(f32[1,4096]{1,0:T(1,128)} %gain_ref.5) | copy-start | bytes 49156
  25.3 13.7 %all-to-all-start.1 = ((bf16[32,40,128]{2,1,0:T(8,128)(2,1)}), bf16[32,40,128]{2,1,0:T(8,128)(2,1)S(1)}, u32[]{:S(2)}, u32[]{:S(2)}) async-start(bf16[32,40,128]{2,1,0:T(8,128)(2,1)} %get-tuple-element.28), calls=%async_computation.1 | async-start | bytes 655360 | tf_op jit(solution)/shard_map/all_to_all | solution.py:695
  29.6 9.4 %copy-start.5 = (bf16[256,32]{1,0:T(8,128)(2,1)S(1)}, bf16[256,32]{1,0:T(8,128)(2,1)}, u32[]{:S(2)}) copy-start(bf16[256,32]{1,0:T(8,128)(2,1)} %constant.9.clone.spread_ref) | copy-start | bytes 49156
  29.6 9.4 %copy-start.7 = (f32[128,128]{1,0:T(8,128)S(1)}, f32[128,128]{1,0:T(8,128)}, u32[]{:S(2)}) copy-start(f32[128,128]{1,0:T(8,128)} %get-tuple-element.21.mark_ref.inverse_ref) | copy-start | bytes 196612
  43.6 17.6 %collective-permute-start.2 = (bf16[64,4096]{1,0:T(8,128)(2,1)S(1)}, bf16[64,4096]{1,0:T(8,128)(2,1)S(1)}, u32[]{:S(2)}, u32[]{:S(2)}) collective-permute-start(bf16[64,4096]{1,0:T(8,128)(2,1)S(1)} %get-tuple-element.32), channel_id=1, source_target_pairs={{32,0},{64,32},{96,64},{128,96},{160,128},{192,160},{224,192},{256... | collective-permute-start | bytes 1572872 | tf_op jit(solution)/shard_map/ppermute | solution.py:526
  47.7 17.3 %collective-permute-start.3 = (bf16[64,4096]{1,0:T(8,128)(2,1)S(1)}, bf16[64,4096]{1,0:T(8,128)(2,1)S(1)}, u32[]{:S(2)}, u32[]{:S(2)}) collective-permute-start(bf16[64,4096]{1,0:T(8,128)(2,1)S(1)} %get-tuple-element.33), channel_id=1, source_target_pairs={{0,32},{32,64},{64,96},{96,128},{128,160},{160,192},{192,224},{224... | collective-permute-start | bytes 1572872 | tf_op jit(solution)/shard_map/ppermute | solution.py:526
  54.2 16.9 %collective-permute-start = (bf16[64,4096]{1,0:T(8,128)(2,1)S(1)}, bf16[64,4096]{1,0:T(8,128)(2,1)S(1)}, u32[]{:S(2)}, u32[]{:S(2)}) collective-permute-start(bf16[64,4096]{1,0:T(8,128)(2,1)S(1)} %get-tuple-element.30), channel_id=1, source_target_pairs={{32,0},{64,32},{96,64},{128,96},{160,128},{192,160},{224,192},{256... | collective-permute-start | bytes 1572872 | tf_op jit(solution)/shard_map/ppermute | solution.py:526
  59.3 16.8 %collective-permute-start.1 = (bf16[64,4096]{1,0:T(8,128)(2,1)S(1)}, bf16[64,4096]{1,0:T(8,128)(2,1)S(1)}, u32[]{:S(2)}, u32[]{:S(2)}) collective-permute-start(bf16[64,4096]{1,0:T(8,128)(2,1)S(1)} %get-tuple-element.31), channel_id=1, source_target_pairs={{0,32},{32,64},{64,96},{96,128},{128,160},{160,192},{192,224},{224... | collective-permute-start | bytes 1572872 | tf_op jit(solution)/shard_map/ppermute | solution.py:526
